TPU v7x, 32 devices: a whole 2x2x4 slice. The times are simulated.
32 devices in a mesh: op: 2 (over core), sec: 16 (over z, y, x).
Axes of the slice: x: 2, y: 2, z: 4, core: 2. Of those that a mesh axis runs over, the one named last changes fastest.
Arguments:
- psi: float32 [32, 512, 512], P('sec'), may hold values from -6 to 6
- left_env: float32 [8, 32, 512, 512], P('op', 'sec'), may hold values from -0.25 to 0.25
- right_env: float32 [8, 32, 512, 512], P('op', 'sec'), may hold values from -0.09375 to 0.09375
- target: int32 [32], replicated, may hold values from 0 to 31, as said below
Outputs:
- sigma: float32 [32, 512, 512], P('sec', 'op')
Inputs may be any that keep to these rules, and one draw needn't show every extreme that they name: target is a permutation of the 32 blocks; block r belongs to index r // 2 of sec; the block j of index d of sec (block d * 2 + j) lands on index (d + j + 1) mod (16) of sec, in a slot drawn from the seed.
All inputs are finite; a program needn't handle non-finite values.
Results may differ from a plain program's by a relative error of at most 0.00007.
Values sent between devices are 32-bit elements; how exact they have to be, the bound alone decides.
No kernel may reach another device: no remote copies, remote signals or barrier semaphores. Data moves between devices by JAX's collectives and lax.ppermute only.
A program may use at most 128 MiB of HBM per device.

v0:
```python
import jax
import jax.numpy as jnp
from jax import lax
from jax.sharding import PartitionSpec as P


def from_behind(value, axis, steps):
    count = lax.axis_size(axis)
    pairs = [(source, (source + steps) % count) for source in range(count)]
    return lax.ppermute(value, axis, pairs)


def block_matmul(first, second):
    return jnp.einsum("...ab,...bc->...ac", first, second, precision=lax.Precision.HIGHEST)


def term_contract(first, second):
    return jnp.einsum("kac,kcd->ad", first, second, precision=lax.Precision.HIGHEST)


def per_device(psi, left_env, right_env, target):
    ndevice = lax.axis_size("sec")
    me_index = lax.axis_index("sec")
    sdev = psi.shape[0]
    width = psi.shape[1]
    partial_sum = jnp.zeros((sdev, width, width), jnp.float32)
    left_part = block_matmul(left_env, psi[None])
    for step in range(sdev):
        piece = from_behind(left_part[:, step], "sec", step + 1)
        source = (me_index - step - 1) % ndevice
        slot = target[source * sdev + step] % sdev
        renv = lax.dynamic_index_in_dim(right_env, slot, 1, keepdims=False)
        partial_sum = partial_sum.at[slot].set(term_contract(piece, renv))
    total = lax.psum(partial_sum, "op")
    rows = width // lax.axis_size("op")
    return lax.dynamic_slice_in_dim(total, lax.axis_index("op") * rows, rows, 1)


def solution(mesh):
    return jax.shard_map(
        per_device,
        mesh=mesh,
        in_specs=(
            P("sec", None, None),
            P("op", "sec", None, None),
            P("op", "sec", None, None),
            P(),
        ),
        out_specs=P("sec", "op", None),
        check_vma=False,
    )
```

profile of v0, /device:TPU:0, one launch (start us, length us, event | category | flops | bytes accessed | tf_op | source)
XLA Modules:
  0.0 344.2 jit_solution(11555228583794598250)
XLA Ops:
  6.5 0.0 copy-start
  6.5 0.0 all-reduce.2.cloned.1.call-start
  6.5 1.6 copy-done
  8.1 29.6 %fusion.8 = f32[4,2,512,512]{2,3,0,1:T(8,128)S(1)} fusion(f32[4,2,512,512]{3,2,1,0:T(8,128)} %param.9, f32[2,512,512]{2,1,0:T(8,128)S(1)} %copy-done), kind=kOutput, calls=%fused_computation.10 | convolution fusion | flops 12884901888 | bytes 18874368 | tf_op jit(solution)/shard_map/...ab,...bc->...ac/dot_general | solution.py:14
  37.7 0.0 copy-start.2
  37.7 0.0 copy-start.3
  37.7 4.3 %slice_bitcast_fusion = (f32[4,512,512]{1,2,0:T(8,128)}, f32[4,512,512]{1,2,0:T(8,128)}) fusion(f32[4,2,512,512]{2,3,0,1:T(8,128)S(1)} %fusion.8), kind=kLoop, calls=%fused_computation.2 | loop fusion | bytes 16777216 | tf_op jit(solution)/shard_map/squeeze | solution.py:29
  42.0 2.9 collective-permute-start
  44.9 1.5 collective-permute-start.1
  46.4 0.0 copy-done.2
  46.4 0.6 fusion.35
  50.9 0.0 copy-done.3
  50.9 0.8 and_reduce_fusion
  51.7 168.3 %collective-permute-done = f32[4,512,512]{1,2,0:T(8,128)} collective-permute-done((f32[4,512,512]{1,2,0:T(8,128)}, f32[4,512,512]{1,2,0:T(8,128)}, u32[]{:S(2)}, u32[]{:S(2)}) %collective-permute-start) | collective-permute-done | bytes 4194336 | tf_op jit(solution)/shard_map/ppermute | solution.py:10
  220.0 1.6 broadcast_in_dim.2
  221.6 0.0 copy-start.1
  221.6 11.3 %fusion.30 = f32[2,512,512]{2,1,0:T(8,128)} fusion(f32[2,512,512]{2,1,0:T(8,128)} %broadcast_in_dim.2, s32[]{:T(128)} %select_n.44, f32[4,512,512]{1,2,0:T(8,128)} %collective-permute-done, f32[4,2,512,512]{3,2,1,0:T(8,128)} %param.10, pred[]{:T(512)} %get-tuple-element.30), kind=kOutput, calls=%fused_computation.18 | convolution fusion | flops 6442713088 | bytes 9438720 | tf_op jit(solution)/shard_map/kac,kcd->ad/dot_general | solution.py:18
  232.9 0.0 collective-permute-done.1
  232.9 0.0 copy-done.1
  232.9 10.5 %fusion.21 = f32[2,512,512]{2,1,0:T(8,128)} fusion(f32[2,512,512]{2,1,0:T(8,128)} %fusion.30, s32[]{:T(128)} %select_n.49, f32[4,512,512]{1,2,0:T(8,128)} %collective-permute-done.1, f32[4,2,512,512]{3,2,1,0:T(8,128)S(1)} %copy-done.1, pred[]{:T(512)} %get-tuple-element.29), kind=kOutput, calls=%fused_computation.15 | convolution fusion | flops 6442713088 | bytes 10487296 | tf_op jit(solution)/shard_map/kac,kcd->ad/dot_general | solution.py:18
  243.4 0.0 all-reduce.2.cloned.1.call-update
  243.4 91.7 %all-reduce.2.cloned.1.call-done = f32[2,512,512]{2,1,0:T(8,128)} async-done(((f32[2,512,512]{2,1,0:T(8,128)}), f32[2,512,512]{2,1,0:T(8,128)}) %all-reduce.2.cloned.1.call-update) | async-done | bytes 2097168 | tf_op jit(solution)/shard_map/psum | solution.py:34
  335.1 2.3 constant_dynamic-slice_fusion
Async XLA Ops:
  6.5 1.6 copy-start
  6.5 328.6 %all-reduce.2.cloned.1.call-start = ((), (), s32[]{:S(2)}) async-start(), calls=%async_computation | async-start | bytes 4194304 | tf_op jit(solution)/shard_map/psum | solution.py:34
  37.7 8.7 %copy-start.2 = (s32[32]{0:T(128)S(1)}, s32[32]{0:T(128)}, u32[]{:S(2)}) copy-start(s32[32]{0:T(128)} %param.11) | copy-start | bytes 388
  37.7 13.2 %copy-start.3 = (s32[3]{0:T(128)S(1)}, s32[3]{0:T(128)}, u32[]{:S(2)}) copy-start(s32[3]{0:T(128)} %constant.97.clone.1) | copy-start | bytes 40
  42.0 178.0 %collective-permute-start = (f32[4,512,512]{1,2,0:T(8,128)}, f32[4,512,512]{1,2,0:T(8,128)}, u32[]{:S(2)}, u32[]{:S(2)}) collective-permute-start(f32[4,512,512]{1,2,0:T(8,128)} %get-tuple-element.32), channel_id=1, source_target_pairs={{0,1},{1,2},{2,3},{3,4},{4,5},{5,6},{6,7},{7,8},{8,9},{9,10},{10,1... | collective-permute-start | bytes 12582920 | tf_op jit(solution)/shard_map/ppermute | solution.py:10
  44.9 188.0 %collective-permute-start.1 = (f32[4,512,512]{1,2,0:T(8,128)}, f32[4,512,512]{1,2,0:T(8,128)}, u32[]{:S(2)}, u32[]{:S(2)}) collective-permute-start(f32[4,512,512]{1,2,0:T(8,128)} %get-tuple-element.31), channel_id=1, source_target_pairs={{0,2},{1,3},{2,4},{3,5},{4,6},{5,7},{6,8},{7,9},{8,10},{9,11},{10,... | collective-permute-start | bytes 12582920 | tf_op jit(solution)/shard_map/ppermute | solution.py:10
  221.6 11.3 %copy-start.1 = (f32[4,2,512,512]{3,2,1,0:T(8,128)S(1)}, f32[4,2,512,512]{3,2,1,0:T(8,128)}, u32[]{:S(2)}) copy-start(f32[4,2,512,512]{3,2,1,0:T(8,128)} %param.10) | copy-start | bytes 25165828
Sparse Core Ops, SparseCore 0:
  243.5 91.5 all-reduce.1
where the time goes:
time: 344 us
  waiting for transfers between devices  260 us (76%)
  matrix products  51.4 us (15%)
  between operations  17.3 us (5%)
  local copies, waits for them, and re-layouts  10.3 us (3%)
  starting transfers between devices  4.46 us (1%)
    ppermute x2, waiting for transfers between devices, from_behind(): return lax.ppermute(value, axis, pairs)  168 us
    psum x1, waiting for transfers between devices, per_device(): total = lax.psum(partial_sum, 'op')  91.7 us
    dot_general x1, matrix products, block_matmul(): jnp.einsum('...ab,...bc->...ac', first, second, precision=lax.Precision.H...  29.6 us
    dot_general x2, matrix products, term_contract(): jnp.einsum('kac,kcd->ad', first, second, precision=lax.Precision.HIGHEST)  21.8 us
  transfers between devices with their start and end apart: 3, of which 2 were waited for; matrix products, arithmetic and copies ran while one was open for 4% of the time, Pallas kernels for 0%

commit v1 on v0

v1 whole, which is shorter than its diff:
```python
import jax
import jax.numpy as jnp
from jax import lax
from jax.sharding import PartitionSpec as P


def product(first, second):
    return jnp.einsum("kab,bc->kac", first, second, precision=lax.Precision.HIGH)


def contract(first, second):
    return jnp.einsum("kac,kcd->ad", first, second, precision=lax.Precision.HIGH)


def per_device(psi, left_env, right_env, target):
    count = lax.axis_size("sec")
    me = lax.axis_index("sec")
    op = lax.axis_index("op")
    half = psi.shape[1] // 2

    def send(value, step, who=lambda d: True):
        pairs = [(d, (d + step(d)) % count) for d in range(count) if who(d)]
        return lax.ppermute(value, "sec", pairs)

    relayed = product(left_env[:, 0, half:], psi[0])
    hop = send(relayed, lambda d: (d ^ 2) - d, lambda d: d % 2 == 1)
    direct = product(left_env[:, 0, :half], psi[0])
    upper = send(direct, lambda d: 1)
    second = product(left_env[:, 1], psi[1])
    hop, upper, second, relayed = lax.optimization_barrier((hop, upper, second, relayed))

    whole = send(second, lambda d: 2)
    onward = jnp.where(me % 2 == 1, hop, relayed)
    lower = send(onward, lambda d: 1 if d % 2 == 0 else (-1 if d % 4 == 3 else 3))

    slots = [target[((me - j - 1) % count) * 2 + j] % 2 for j in range(2)]
    right = [lax.dynamic_index_in_dim(right_env, slot, 1, keepdims=False) for slot in slots]

    def both_terms(value):
        own = lax.dynamic_slice_in_dim(value, op * half, half, 0)
        other = lax.dynamic_slice_in_dim(value, (1 - op) * half, half, 0)
        return own + lax.ppermute(other, "op", [(0, 1), (1, 0)])

    sums = [
        both_terms(jnp.concatenate([contract(upper, right[0]), contract(lower, right[0])])),
        both_terms(contract(whole, right[1])),
    ]
    first = slots[0] == 0
    return jnp.stack([jnp.where(first, sums[0], sums[1]), jnp.where(first, sums[1], sums[0])])


def solution(mesh):
    return jax.shard_map(
        per_device,
        mesh=mesh,
        in_specs=(
            P("sec", None, None),
            P("op", "sec", None, None),
            P("op", "sec", None, None),
            P(),
        ),
        out_specs=P("sec", "op", None),
        check_vma=False,
    )
```

time: 344 us -> 164 us (0.48)
  waiting for transfers between devices: 260 us -> 113 us
  matrix products: 51.4 us -> 27.4 us
  between operations: 17.3 us -> 4.02 us
  local copies, waits for them, and re-layouts: 10.3 us -> 2.71 us
  starting transfers between devices: 4.46 us -> 10.9 us
  other arithmetic: 0.79 us -> 4.48 us
    psum x1 -> x0, waiting for transfers between devices: 91.7 us -> none  [per_device(): total = lax.psum(partial_sum, 'op')]
    ppermute x2 -> x6, waiting for transfers between devices: 168 us -> 113 us  [the longest x4 111 us: send(): return lax.ppermute(value, 'sec', pairs)]
    dot_general x3 -> x6, matrix products: 51.4 us -> 27.4 us  [the longest x3 14.9 us: contract(): jnp.einsum('kac,kcd->ad', first, second, precision=lax.Precision.HIGH)]
    ppermute x2 -> x6, starting transfers between devices: 4.46 us -> 10.9 us  [the longest x4 10.8 us: send(): return lax.ppermute(value, 'sec', pairs)]
    squeeze x1 -> x0, local copies, waits for them, and re-layouts: 4.25 us -> none  [per_device(): piece = from_behind(left_part[:, step], 'sec', step + 1)]
  transfers between devices with their start and end apart: 3 -> 6, of which waited for: 2 -> 4; matrix products, arithmetic and copies ran while one was open for 4% -> 16% of each run, Pallas kernels for 0% -> 0%
where the time goes in v1:
time: 164 us; the launch traced here: 163 us
  waiting for transfers between devices  113 us (69%)
  matrix products  27.4 us (17%)
  starting transfers between devices  10.9 us (7%)
  other arithmetic  4.48 us (3%)
  between operations  4.02 us (2%)
  local copies, waits for them, and re-layouts  2.71 us (2%)
    ppermute x4, waiting for transfers between devices, send(): return lax.ppermute(value, 'sec', pairs)  111 us
    dot_general x3, matrix products, contract(): jnp.einsum('kac,kcd->ad', first, second, precision=lax.Precision.HIGH)  14.9 us
    dot_general x3, matrix products, product(): jnp.einsum('kab,bc->kac', first, second, precision=lax.Precision.HIGH)  12.6 us
    ppermute x4, starting transfers between devices, send(): return lax.ppermute(value, 'sec', pairs)  10.8 us
  transfers between devices with their start and end apart: 6, of which 4 were waited for; matrix products, arithmetic and copies ran while one was open for 16% of the time, Pallas kernels for 0%

profile of v1, /device:TPU:0, one launch (start us, length us, event | category | flops | bytes accessed | tf_op | source)
XLA Modules:
  0.0 163.0 jit_solution(69091711961864607)
XLA Ops:
  0.0 3.8 %fusion.12 = f32[4,256,512]{2,1,0:T(8,128)S(1)} fusion(f32[4,2,512,512]{3,2,1,0:T(8,128)} %param.5, f32[2,512,512]{2,1,0:T(8,128)} %param.4), kind=kOutput, calls=%fused_computation.12 | convolution fusion | flops 1610612736 | bytes 5242880 | tf_op jit(solution)/shard_map/kab,bc->kac/dot_general | solution.py:8
  3.8 3.0 %collective-permute-start.1 = (f32[4,256,512]{2,1,0:T(8,128)S(1)}, f32[4,256,512]{2,1,0:T(8,128)S(1)}, u32[]{:S(2)}, u32[]{:S(2)}) collective-permute-start(f32[4,256,512]{2,1,0:T(8,128)S(1)} %fusion.12), channel_id=1, source_target_pairs={{0,1},{1,2},{2,3},{3,4},{4,5},{5,6},{6,7},{7,8},{8,9},{9,10},{10,1... | collective-permute-start | bytes 6291464 | tf_op jit(solution)/shard_map/ppermute | solution.py:23
  6.8 3.7 %fusion.14 = f32[4,256,512]{2,1,0:T(8,128)S(1)} fusion(f32[4,2,512,512]{3,2,1,0:T(8,128)} %param.5, f32[2,512,512]{2,1,0:T(8,128)} %param.4), kind=kOutput, calls=%fused_computation.14 | convolution fusion | flops 1610612736 | bytes 5242880 | tf_op jit(solution)/shard_map/kab,bc->kac/dot_general | solution.py:8
  10.5 0.8 collective-permute-start
  11.3 0.0 copy-done
  11.3 0.0 copy-done.1
  11.3 5.1 %fusion = f32[4,512,512]{2,1,0:T(8,128)} fusion(f32[4,2,512,512]{3,2,1,0:T(8,128)S(1)} %copy-done, f32[2,512,512]{2,1,0:T(8,128)S(1)} %copy-done.1), kind=kOutput, calls=%fused_computation | convolution fusion | flops 3221225472 | bytes 9437184 | tf_op jit(solution)/shard_map/kab,bc->kac/dot_general | solution.py:8
  16.4 40.1 %collective-permute-done.1 = f32[4,256,512]{2,1,0:T(8,128)S(1)} collective-permute-done((f32[4,256,512]{2,1,0:T(8,128)S(1)}, f32[4,256,512]{2,1,0:T(8,128)S(1)}, u32[]{:S(2)}, u32[]{:S(2)}) %collective-permute-start.1) | collective-permute-done | bytes 2097184 | tf_op jit(solution)/shard_map/ppermute | solution.py:23
  56.5 0.0 collective-permute-done
  56.5 1.4 copy-done.2
  57.8 0.0 collective-permute-start.4
  57.8 0.6 copy-done.3
  58.5 1.8 %broadcast_select_fusion = f32[4,256,512]{2,1,0:T(8,128)} fusion(f32[4,256,512]{2,1,0:T(8,128)} %copy-done.2, f32[4,256,512]{2,1,0:T(8,128)S(1)} %fusion.14, pred[]{:T(512)S(6)} %eq.13), kind=kLoop, calls=%fused_computation.30 | loop fusion | flops 524288 | bytes 6291457 | tf_op jit(solution)/shard_map/jit(_where)/select_n | solution.py:33
  60.3 7.0 %collective-permute-start.2 = (f32[4,256,512]{2,1,0:T(8,128)}, f32[4,256,512]{2,1,0:T(8,128)S(1)}, u32[]{:S(2)}, u32[]{:S(2)}) collective-permute-start(f32[4,256,512]{2,1,0:T(8,128)} %broadcast_select_fusion), channel_id=1, source_target_pairs={{0,1},{1,4},{2,3},{3,2},{4,5},{5,8},{6,7},{7,6},{8,9},{9,12},{10,1... | collective-permute-start | bytes 6291464 | tf_op jit(solution)/shard_map/ppermute | solution.py:23
  67.3 0.0 copy-done.4
  67.3 0.7 fusion.39
  71.8 0.0 slice-start
  71.8 5.0 %fusion.21 = f32[256,512]{1,0:T(8,128)S(1)} fusion(f32[4,256,512]{2,1,0:T(8,128)} %copy-done.3, f32[4,2,512,512]{3,2,1,0:T(8,128)} %param.6, s32[]{:T(128)S(6)} %select_n.68), kind=kOutput, calls=%fused_computation.23 | convolution fusion | flops 1610612736 | bytes 6815748 | tf_op jit(solution)/shard_map/kac,kcd->ad/dot_general | solution.py:12
  76.8 0.0 slice-start.1
  76.8 37.0 %collective-permute-done.2 = f32[4,256,512]{2,1,0:T(8,128)S(1)} collective-permute-done((f32[4,256,512]{2,1,0:T(8,128)}, f32[4,256,512]{2,1,0:T(8,128)S(1)}, u32[]{:S(2)}, u32[]{:S(2)}) %collective-permute-start.2) | collective-permute-done | bytes 2097184 | tf_op jit(solution)/shard_map/ppermute | solution.py:23
  113.8 4.2 %fusion.24 = f32[256,512]{1,0:T(8,128)S(1)} fusion(f32[4,256,512]{2,1,0:T(8,128)S(1)} %collective-permute-done.2, f32[4,2,512,512]{3,2,1,0:T(8,128)} %param.6, s32[]{:T(128)S(6)} %select_n.68), kind=kOutput, calls=%fused_computation.24 | convolution fusion | flops 1610612736 | bytes 6815748 | tf_op jit(solution)/shard_map/kac,kcd->ad/dot_general | solution.py:12
  118.0 0.1 fusion.33
  118.1 0.1 collective-permute-start.3
  118.2 34.4 %collective-permute-done.4 = f32[4,512,512]{2,1,0:T(8,128)} collective-permute-done((f32[4,512,512]{2,1,0:T(8,128)}, f32[4,512,512]{2,1,0:T(8,128)}, u32[]{:S(2)}, u32[]{:S(2)}) %collective-permute-start.4) | collective-permute-done | bytes 4194336 | tf_op jit(solution)/shard_map/ppermute | solution.py:23
  152.6 0.0 slice-done
  152.6 0.0 slice-done.1
  152.6 5.7 %fusion.18 = f32[512,512]{1,0:T(8,128)S(1)} fusion(f32[4,512,512]{2,1,0:T(8,128)} %collective-permute-done.4, f32[4,2,512,512]{3,2,1,0:T(8,128)S(1)} %bitcast.55, s32[]{:T(128)S(6)} %select_n.77), kind=kOutput, calls=%fused_computation.18 | convolution fusion | flops 3221225472 | bytes 9437188 | tf_op jit(solution)/shard_map/kac,kcd->ad/dot_general | solution.py:12
  158.4 0.1 collective-permute-start.5
  158.5 0.0 collective-permute-done.3
  158.5 2.0 %collective-permute-done.5 = f32[256,512]{1,0:T(8,128)} collective-permute-done((f32[256,512]{1,0:T(8,128)S(1)}, f32[256,512]{1,0:T(8,128)}, u32[]{:S(2)}, u32[]{:S(2)}) %collective-permute-start.5) | collective-permute-done | bytes 524320 | tf_op jit(solution)/shard_map/ppermute | solution.py:42
  160.5 1.5 select_bitcast_fusion.1
  162.0 1.0 pad_maximum_fusion
  (7 shorter events, 0.1 us)
Async XLA Ops:
  0.0 11.3 %copy-start = (f32[4,2,512,512]{3,2,1,0:T(8,128)S(1)}, f32[4,2,512,512]{3,2,1,0:T(8,128)}, u32[]{:S(2)}) copy-start(f32[4,2,512,512]{3,2,1,0:T(8,128)} %param.5) | copy-start | bytes 25165828
  0.0 11.3 %copy-start.1 = (f32[2,512,512]{2,1,0:T(8,128)S(1)}, f32[2,512,512]{2,1,0:T(8,128)}, u32[]{:S(2)}) copy-start(f32[2,512,512]{2,1,0:T(8,128)} %param.4) | copy-start | bytes 6291460
  3.8 52.6 %collective-permute-start.1 = (f32[4,256,512]{2,1,0:T(8,128)S(1)}, f32[4,256,512]{2,1,0:T(8,128)S(1)}, u32[]{:S(2)}, u32[]{:S(2)}) collective-permute-start(f32[4,256,512]{2,1,0:T(8,128)S(1)} %fusion.12), channel_id=1, source_target_pairs={{0,1},{1,2},{2,3},{3,4},{4,5},{5,6},{6,7},{7,8},{8,9},{9,10},{10,1... | collective-permute-start | bytes 6291464 | tf_op jit(solution)/shard_map/ppermute | solution.py:23
  10.5 46.0 %collective-permute-start = (f32[4,256,512]{2,1,0:T(8,128)S(1)}, f32[4,256,512]{2,1,0:T(8,128)S(1)}, u32[]{:S(2)}, u32[]{:S(2)}) collective-permute-start(f32[4,256,512]{2,1,0:T(8,128)S(1)} %fusion.14), channel_id=1, source_target_pairs={{1,3},{3,1},{5,7},{7,5},{9,11},{11,9},{13,15},{15,13},{17,19},{19,... | collective-permute-start | bytes 6291464 | tf_op jit(solution)/shard_map/ppermute | solution.py:23
  16.4 50.9 %copy-start.4 = (s32[32]{0:T(128)S(1)}, s32[32]{0:T(128)}, u32[]{:S(2)}) copy-start(s32[32]{0:T(128)} %param.7) | copy-start | bytes 388
  56.5 2.0 %copy-start.3 = (f32[4,256,512]{2,1,0:T(8,128)}, f32[4,256,512]{2,1,0:T(8,128)S(1)}, u32[]{:S(2)}) copy-start(f32[4,256,512]{2,1,0:T(8,128)S(1)} %collective-permute-done.1) | copy-start | bytes 6291460
  56.5 1.4 copy-start.2
  57.8 94.8 %collective-permute-start.4 = (f32[4,512,512]{2,1,0:T(8,128)}, f32[4,512,512]{2,1,0:T(8,128)}, u32[]{:S(2)}, u32[]{:S(2)}) collective-permute-start(f32[4,512,512]{2,1,0:T(8,128)} %fusion), channel_id=1, source_target_pairs={{0,2},{1,3},{2,4},{3,5},{4,6},{5,7},{6,8},{7,9},{8,10},{9,11},{10,... | collective-permute-start | bytes 12582920 | tf_op jit(solution)/shard_map/ppermute | solution.py:23
  60.3 53.5 %collective-permute-start.2 = (f32[4,256,512]{2,1,0:T(8,128)}, f32[4,256,512]{2,1,0:T(8,128)S(1)}, u32[]{:S(2)}, u32[]{:S(2)}) collective-permute-start(f32[4,256,512]{2,1,0:T(8,128)} %broadcast_select_fusion), channel_id=1, source_target_pairs={{0,1},{1,4},{2,3},{3,2},{4,5},{5,8},{6,7},{7,6},{8,9},{9,12},{10,1... | collective-permute-start | bytes 6291464 | tf_op jit(solution)/shard_map/ppermute | solution.py:23
  71.8 80.8 %slice-start = ((s8[8388608]{0:T(1024)(128)(4,1)}), s8[4194304]{0:T(1024)(128)(4,1)S(1)}, s32[]{:S(2)}) async-start(s8[8388608]{0:T(1024)(128)(4,1)} %bitcast.54), calls=%async_computation | async-start | bytes 8388608
  76.8 75.8 %slice-start.1 = ((s8[8388608]{0:T(1024)(128)(4,1)}), s8[4194304]{0:T(1024)(128)(4,1)S(1)}, s32[]{:S(2)}) async-start(s8[8388608]{0:T(1024)(128)(4,1)} %bitcast.54), calls=%async_computation.1 | async-start | bytes 8388608
  118.1 40.3 %collective-permute-start.3 = (f32[256,512]{1,0:T(8,128)S(1)}, f32[256,512]{1,0:T(8,128)}, u32[]{:S(2)}, u32[]{:S(2)}) collective-permute-start(f32[256,512]{1,0:T(8,128)S(1)} %fusion.33), channel_id=1, source_target_pairs={{0,16},{16,0},{1,17},{17,1},{2,18},{18,2},{3,19},{19,3},{4,20},{20... | collective-permute-start | bytes 1572872 | tf_op jit(solution)/shard_map/ppermute | solution.py:42
  158.4 2.1 %collective-permute-start.5 = (f32[256,512]{1,0:T(8,128)S(1)}, f32[256,512]{1,0:T(8,128)}, u32[]{:S(2)}, u32[]{:S(2)}) collective-permute-start(f32[256,512]{1,0:T(8,128)S(1)} %constant_dynamic-slice_fusion), channel_id=1, source_target_pairs={{0,16},{16,0},{1,17},{17,1},{2,18},{18,2},{3,19},{19,3},{4,20},{20... | collective-permute-start | bytes 1572872 | tf_op jit(solution)/shard_map/ppermute | solution.py:42

commit v2 on v1

v2 whole, which is shorter than its diff:
```python
import functools

import jax
import jax.numpy as jnp
from jax import lax
from jax.experimental import pallas as pl
from jax.experimental.pallas import tpu as pltpu
from jax.sharding import PartitionSpec as P


def split(value):
    high = value.astype(jnp.bfloat16)
    return high, (value - high.astype(jnp.float32)).astype(jnp.bfloat16)


def product_kernel(row_ref, left_ref, psi_ref, *refs, parts, pieces):
    outs, stack = refs[:-1], refs[-1]
    term = pl.program_id(0)
    width = psi_ref.shape[-1]

    @pl.when(term == 0)
    def _():
        high, low = split(psi_ref[0])
        stack[:width] = high
        stack[width : 2 * width] = high
        stack[2 * width :] = low

    high, low = split(left_ref[0, 0])
    result = jnp.dot(jnp.concatenate([high, low, high], axis=1), stack[...], preferred_element_type=jnp.float32)
    size = result.shape[0] // pieces
    first = 0
    for index, terms in enumerate(parts):

        @pl.when((term >= first) & (term < first + terms))
        def _():
            for piece in range(pieces):
                outs[index * pieces + piece][0] = result[piece * size : (piece + 1) * size]

        first += terms


def product(left_env, psi, block, row, rows, parts, first=0, pieces=1):
    width = psi.shape[-1]
    terms = sum(parts)
    size = rows // pieces
    starts = [sum(parts[:i]) for i in range(len(parts))]
    shapes, specs = [], []
    for start, count in zip(starts, parts):
        for _ in range(pieces):
            shapes.append(jax.ShapeDtypeStruct((count, size, width), jnp.float32))
            specs.append(
                pl.BlockSpec((1, size, width), lambda k, r, a=start, c=count: (jnp.clip(k - a, 0, c - 1), 0, 0))
            )
    return pl.pallas_call(
        functools.partial(product_kernel, parts=parts, pieces=pieces),
        out_shape=shapes,
        grid_spec=pltpu.PrefetchScalarGridSpec(
            num_scalar_prefetch=1,
            grid=(terms,),
            in_specs=[
                pl.BlockSpec((1, 1, rows, width), lambda k, r: (k + first, block, r[0], 0)),
                pl.BlockSpec((1, width, width), lambda k, r: (block, 0, 0)),
            ],
            out_specs=specs,
            scratch_shapes=[pltpu.VMEM((3 * width, width), jnp.bfloat16)],
        ),
        compiler_params=pltpu.CompilerParams(vmem_limit_bytes=48 * 2**20),
        cost_estimate=pl.CostEstimate(
            flops=6 * terms * rows * width * width, bytes_accessed=8 * terms * rows * width, transcendentals=0
        ),
    )(jnp.reshape(row, (1,)).astype(jnp.int32), left_env, psi)


def left_product(first, second):
    return jnp.einsum("kab,bc->kac", first, second, precision=lax.Precision.HIGH)


def contract(first, second):
    return jnp.einsum("kac,kcd->ad", first, second, precision=lax.Precision.HIGH)


def per_device(psi, left_env, right_env, target):
    count = lax.axis_size("sec")
    me = lax.axis_index("sec")
    op = lax.axis_index("op")
    half = psi.shape[1] // 2

    def send(value, step, who=lambda d: True):
        pairs = [(d, (d + step(d)) % count) for d in range(count) if who(d)]
        return lax.ppermute(value, "sec", pairs)

    terms = left_env.shape[0]
    upper_rows = half - 16
    lower = left_product(left_env[:, 0, upper_rows:], psi[0])
    hop = send(lower, lambda d: (d ^ 2) - d, lambda d: d % 2 == 1)
    upper = left_product(left_env[:, 0, :upper_rows], psi[0])
    direct = send(upper, lambda d: 1)
    onward = send(lower, lambda d: 1, lambda d: d % 2 == 0)

    chunks = product(left_env, psi, 1, 1 - op, half, (terms,))
    chunks += product(left_env, psi, 1, op, half, (terms - 1, 1))
    hop, direct, chunks = lax.optimization_barrier((hop, direct, chunks))
    others = send(chunks[0], lambda d: 2)
    most = send(chunks[1], lambda d: 2)
    relayed = send(hop, lambda d: -1 if d % 4 == 3 else 3, lambda d: d % 2 == 1)
    slots = [target[((me - j - 1) % count) * 2 + j] % 2 for j in range(2)]
    right = [lax.dynamic_index_in_dim(right_env, slot, 1, keepdims=False) for slot in slots]

    def exchange(value):
        return lax.ppermute(value, "op", [(0, 1), (1, 0)])

    others_sum = contract(others, right[1])
    others_sum, relayed = lax.optimization_barrier((others_sum, relayed))
    received = jnp.where(me % 2 == 1, onward, relayed)
    block = jnp.concatenate([contract(direct, right[0]), contract(received, right[0])])
    block, last = lax.optimization_barrier((block, chunks[2]))
    last = send(last, lambda d: 2)
    block_own = lax.dynamic_slice_in_dim(block, op * half, half, 0)
    block_other = lax.dynamic_slice_in_dim(block, (1 - op) * half, half, 0)
    done = block_own + exchange(block_other)
    early = contract(most, right[1][:-1]) + exchange(others_sum)
    done, early = lax.optimization_barrier((jnp.stack([done, done]), early))
    final = early + contract(last, right[1][-1:])
    return lax.dynamic_update_index_in_dim(done, final, slots[1], 0)


def solution(mesh):
    return jax.shard_map(
        per_device,
        mesh=mesh,
        in_specs=(
            P("sec", None, None),
            P("op", "sec", None, None),
            P("op", "sec", None, None),
            P(),
        ),
        out_specs=P("sec", "op", None),
        check_vma=False,
    )
```

time: 164 us -> 158 us (0.963)
  waiting for transfers between devices: 113 us -> 95.4 us
  Pallas kernels: 0 us -> 9.22 us
  starting transfers between devices: 10.9 us -> 15.4 us
  other arithmetic: 4.48 us -> 2.15 us
  local copies, waits for them, and re-layouts: 2.71 us -> 4.44 us
    ppermute x4 -> x7, waiting for transfers between devices: 111 us -> 95.4 us  [send(): return lax.ppermute(value, 'sec', pairs)]
    pallas_call x0 -> x2, Pallas kernels: none -> 9.22 us  [product(): pl.pallas_call(functools.partial(product_kernel, parts=parts, pieces=piec...]
    ppermute x4 -> x7, starting transfers between devices: 10.8 us -> 14.8 us  [send(): return lax.ppermute(value, 'sec', pairs)]
    dot_general x3 -> x2, matrix products: 12.6 us -> 9.91 us  [left_product(): jnp.einsum('kab,bc->kac', first, second, precision=lax.Precision.HIGH)]
    dot_general x3 -> x5, matrix products: 14.9 us -> 17.5 us  [contract(): jnp.einsum('kac,kcd->ad', first, second, precision=lax.Precision.HIGH)]
    ppermute x2, waiting for transfers between devices: 2.01 us -> 0.01 us  [exchange(): return lax.ppermute(value, 'op', [(0, 1), (1, 0)])]
    select_n x1 -> x0, other arithmetic: 1.82 us -> none  [per_device(): onward = jnp.where(me % 2 == 1, hop, relayed)]
    unnamed x14 -> x7, local copies, waits for them, and re-layouts: 2.01 us -> 3.79 us
  transfers between devices with their start and end apart: 6 -> 9, of which waited for: 4 -> 4; matrix products, arithmetic and copies ran while one was open for 16% -> 16% of each run, Pallas kernels for 0% -> 6%
where the time goes in v2:
time: 158 us
  waiting for transfers between devices  95.4 us (60%)
  matrix products  27.4 us (17%)
  starting transfers between devices  15.4 us (10%)
  Pallas kernels  9.22 us (6%)
  local copies, waits for them, and re-layouts  4.44 us (3%)
  between operations  4.04 us (3%)
  other arithmetic  2.15 us (1%)
    ppermute x7, waiting for transfers between devices, send(): return lax.ppermute(value, 'sec', pairs)  95.4 us
    dot_general x5, matrix products, contract(): jnp.einsum('kac,kcd->ad', first, second, precision=lax.Precision.HIGH)  17.5 us
    ppermute x7, starting transfers between devices, send(): return lax.ppermute(value, 'sec', pairs)  14.8 us
    dot_general x2, matrix products, left_product(): jnp.einsum('kab,bc->kac', first, second, precision=lax.Precision.HIGH)  9.91 us
    pallas_call x2, Pallas kernels, product(): pl.pallas_call(functools.partial(product_kernel, parts=parts, pieces=piec...  9.22 us
    unnamed x7, local copies, waits for them, and re-layouts  3.79 us
  transfers between devices with their start and end apart: 9, of which 4 were waited for; matrix products, arithmetic and copies ran while one was open for 16% of the time, Pallas kernels for 6%

profile of v2, /device:TPU:0, one launch (start us, length us, event | category | flops | bytes accessed | tf_op | source)
XLA Modules:
  0.0 158.0 jit_solution(17387065421557026306)
XLA Ops:
  0.0 5.3 %fusion.10 = f32[4,272,512]{2,1,0:T(8,128)} fusion(f32[4,2,512,512]{3,2,1,0:T(8,128)} %left_ref.3, f32[2,512,512]{2,1,0:T(8,128)} %psi_ref.3), kind=kOutput, calls=%fused_computation.12 | convolution fusion | flops 1711276032 | bytes 5505024 | tf_op jit(solution)/shard_map/kab,bc->kac/dot_general | solution.py:75
  5.3 2.0 %collective-permute-start = (f32[4,272,512]{2,1,0:T(8,128)}, f32[4,272,512]{2,1,0:T(8,128)}, u32[]{:S(2)}, u32[]{:S(2)}) collective-permute-start(f32[4,272,512]{2,1,0:T(8,128)} %fusion.10), channel_id=1, source_target_pairs={{1,3},{3,1},{5,7},{7,5},{9,11},{11,9},{13,15},{15,13},{17,19},{19,... | collective-permute-start | bytes 6684680 | tf_op jit(solution)/shard_map/ppermute | solution.py:90
  7.3 4.6 %fusion.14 = f32[4,240,512]{2,1,0:T(8,128)} fusion(f32[4,2,512,512]{3,2,1,0:T(8,128)} %left_ref.3, f32[2,512,512]{2,1,0:T(8,128)S(1)} %copy-done), kind=kOutput, calls=%fused_computation.16 | convolution fusion | flops 1509949440 | bytes 4980736 | tf_op jit(solution)/shard_map/kab,bc->kac/dot_general | solution.py:75
  11.9 4.4 %collective-permute-start.1 = (f32[4,240,512]{2,1,0:T(8,128)}, f32[4,240,512]{2,1,0:T(8,128)}, u32[]{:S(2)}, u32[]{:S(2)}) collective-permute-start(f32[4,240,512]{2,1,0:T(8,128)} %fusion.14), channel_id=1, source_target_pairs={{0,1},{1,2},{2,3},{3,4},{4,5},{5,6},{6,7},{7,8},{8,9},{9,10},{10,1... | collective-permute-start | bytes 5898248 | tf_op jit(solution)/shard_map/ppermute | solution.py:90
  16.3 5.1 %shard_map.46 = f32[4,256,512]{2,1,0:T(8,128)} custom-call(s32[1]{0:T(128)} %bitcast.4.row_ref, f32[4,2,512,512]{3,2,1,0:T(8,128)} %left_ref.3, f32[2,512,512]{2,1,0:T(8,128)S(1)} %copy-done), custom_call_target="tpu_custom_call" | custom-call | flops 1610612736 | bytes 4194304 | tf_op jit(solution)/shard_map/pallas_call | solution.py:54
  21.4 4.1 %shard_map.47 = (f32[3,256,512]{2,1,0:T(8,128)S(1)}, f32[1,256,512]{2,1,0:T(8,128)S(1)}) custom-call(s32[1]{0:T(128)} %bitcast.5.row_ref, f32[4,2,512,512]{3,2,1,0:T(8,128)} %left_ref.3, f32[2,512,512]{2,1,0:T(8,128)S(1)} %copy-done), custom_call_target="tpu_custom_call" | custom-call | flops 1610612736 | bytes 4194304 | tf_op jit(solution)/shard_map/pallas_call | solution.py:54
  25.5 1.1 copy-done.1
  26.7 35.5 %collective-permute-done.1 = f32[4,240,512]{2,1,0:T(8,128)} collective-permute-done((f32[4,240,512]{2,1,0:T(8,128)}, f32[4,240,512]{2,1,0:T(8,128)}, u32[]{:S(2)}, u32[]{:S(2)}) %collective-permute-start.1) | collective-permute-done | bytes 1966112 | tf_op jit(solution)/shard_map/ppermute | solution.py:90
  62.1 0.0 collective-permute-done
  62.1 0.0 collective-permute-start.3
  62.1 1.3 collective-permute-start.4
  63.4 5.7 %collective-permute-start.2 = (f32[4,272,512]{2,1,0:T(8,128)}, f32[4,272,512]{2,1,0:T(8,128)}, u32[]{:S(2)}, u32[]{:S(2)}) collective-permute-start(f32[4,272,512]{2,1,0:T(8,128)} %fusion.10), channel_id=1, source_target_pairs={{0,1},{2,3},{4,5},{6,7},{8,9},{10,11},{12,13},{14,15},{16,17},{18,... | collective-permute-start | bytes 6684680 | tf_op jit(solution)/shard_map/ppermute | solution.py:90
  69.1 0.6 fusion.40
  73.6 1.5 collective-permute-start.6
  75.0 4.7 %fusion.26 = f32[240,512]{1,0:T(8,128)S(1)} fusion(f32[4,240,512]{2,1,0:T(8,128)} %collective-permute-done.1, f32[4,2,512,512]{3,2,1,0:T(8,128)} %param.6, s32[]{:T(128)S(6)} %select_n.55), kind=kOutput, calls=%fused_computation.22 | convolution fusion | flops 1509949440 | bytes 6651908 | tf_op jit(solution)/shard_map/kac,kcd->ad/dot_general | solution.py:79
  79.8 34.0 %collective-permute-done.3 = f32[4,256,512]{2,1,0:T(8,128)} collective-permute-done((f32[4,256,512]{2,1,0:T(8,128)}, f32[4,256,512]{2,1,0:T(8,128)}, u32[]{:S(2)}, u32[]{:S(2)}) %collective-permute-start.3) | collective-permute-done | bytes 2097184 | tf_op jit(solution)/shard_map/ppermute | solution.py:90
  113.7 4.8 %fusion.22 = f32[256,512]{1,0:T(8,128)S(1)} fusion(f32[4,256,512]{2,1,0:T(8,128)} %collective-permute-done.3, f32[4,2,512,512]{3,2,1,0:T(8,128)} %param.6, s32[]{:T(128)S(6)} %select_n.61), kind=kOutput, calls=%fused_computation.20 | convolution fusion | flops 1610612736 | bytes 6815748 | tf_op jit(solution)/shard_map/kac,kcd->ad/dot_general | solution.py:79
  118.6 0.0 collective-permute-done.2
  118.6 4.3 %fusion.17 = f32[272,512]{1,0:T(8,128)S(1)} fusion(f32[4,2,512,512]{3,2,1,0:T(8,128)} %param.6, s32[]{:T(128)S(6)} %select_n.55, f32[4,272,512]{2,1,0:T(8,128)} %collective-permute-done.2, f32[4,272,512]{2,1,0:T(8,128)S(1)} %collective-permute-done.4, pred[]{:T(512)S(6)} %eq.9), kind=kOutput, calls=%fused_computation.19 | convolution fusion | flops 1711833088 | bytes 9207813 | tf_op jit(solution)/shard_map/kac,kcd->ad/dot_general | solution.py:79
  122.9 0.1 pad_maximum_fusion
  123.0 0.1 collective-permute-start.5
  123.1 0.5 collective-permute-start.7
  123.6 2.6 %dynamic-slice_bitcast_fusion = f32[4,1,512,512]{3,2,0,1:T(8,128)S(1)} fusion(f32[4,2,512,512]{3,2,1,0:T(8,128)} %param.6, s32[]{:T(128)S(6)} %select_n.61), kind=kLoop, calls=%fused_computation.7 | loop fusion | bytes 8388612
  126.2 0.1 collective-permute-start.8
  126.3 0.0 collective-permute-done.5
  126.3 0.1 add_bitcast_fusion
  126.4 1.1 pad_maximum_fusion.1
  127.5 19.9 %collective-permute-done.6 = f32[3,256,512]{2,1,0:T(8,128)} collective-permute-done((f32[3,256,512]{2,1,0:T(8,128)}, f32[3,256,512]{2,1,0:T(8,128)}, u32[]{:S(2)}, u32[]{:S(2)}) %collective-permute-start.6) | collective-permute-done | bytes 1572896 | tf_op jit(solution)/shard_map/ppermute | solution.py:90
  147.4 3.0 %fusion.29 = f32[256,512]{1,0:T(8,128)S(1)} fusion(f32[256,512]{1,0:T(8,128)S(1)} %collective-permute-done.7, f32[3,256,512]{2,1,0:T(8,128)} %collective-permute-done.6, f32[4,1,512,512]{3,2,0,1:T(8,128)S(1)} %dynamic-slice_bitcast_fusion), kind=kOutput, calls=%fused_computation.23 | convolution fusion | flops 1208090624 | bytes 5767168 | tf_op jit(solution)/shard_map/kac,kcd->ad/dot_general | solution.py:79
  150.4 6.1 %collective-permute-done.8 = f32[1,256,512]{2,1,0:T(8,128)S(1)} collective-permute-done((f32[1,256,512]{2,1,0:T(8,128)S(1)}, f32[1,256,512]{2,1,0:T(8,128)S(1)}, u32[]{:S(2)}, u32[]{:S(2)}) %collective-permute-start.8) | collective-permute-done | bytes 524320 | tf_op jit(solution)/shard_map/ppermute | solution.py:90
  156.5 0.6 fusion.31
  157.1 0.9 bitcast_dynamic-update-slice_fusion
  (8 shorter events, 0.1 us)
Async XLA Ops:
  0.0 7.3 %copy-start = (f32[2,512,512]{2,1,0:T(8,128)S(1)}, f32[2,512,512]{2,1,0:T(8,128)}, u32[]{:S(2)}) copy-start(f32[2,512,512]{2,1,0:T(8,128)} %psi_ref.3) | copy-start | bytes 6291460
  5.3 56.8 %collective-permute-start = (f32[4,272,512]{2,1,0:T(8,128)}, f32[4,272,512]{2,1,0:T(8,128)}, u32[]{:S(2)}, u32[]{:S(2)}) collective-permute-start(f32[4,272,512]{2,1,0:T(8,128)} %fusion.10), channel_id=1, source_target_pairs={{1,3},{3,1},{5,7},{7,5},{9,11},{11,9},{13,15},{15,13},{17,19},{19,... | collective-permute-start | bytes 6684680 | tf_op jit(solution)/shard_map/ppermute | solution.py:90
  11.9 50.2 %collective-permute-start.1 = (f32[4,240,512]{2,1,0:T(8,128)}, f32[4,240,512]{2,1,0:T(8,128)}, u32[]{:S(2)}, u32[]{:S(2)}) collective-permute-start(f32[4,240,512]{2,1,0:T(8,128)} %fusion.14), channel_id=1, source_target_pairs={{0,1},{1,2},{2,3},{3,4},{4,5},{5,6},{6,7},{7,8},{8,9},{9,10},{10,1... | collective-permute-start | bytes 5898248 | tf_op jit(solution)/shard_map/ppermute | solution.py:90
  21.4 47.7 %copy-start.2 = (s32[32]{0:T(128)S(1)}, s32[32]{0:T(128)}, u32[]{:S(2)}) copy-start(s32[32]{0:T(128)} %param.7) | copy-start | bytes 388
  25.5 1.2 copy-start.1
  62.1 51.6 %collective-permute-start.3 = (f32[4,256,512]{2,1,0:T(8,128)}, f32[4,256,512]{2,1,0:T(8,128)}, u32[]{:S(2)}, u32[]{:S(2)}) collective-permute-start(f32[4,256,512]{2,1,0:T(8,128)} %shard_map.46), channel_id=1, source_target_pairs={{0,2},{1,3},{2,4},{3,5},{4,6},{5,7},{6,8},{7,9},{8,10},{9,11},{10,... | collective-permute-start | bytes 6291464 | tf_op jit(solution)/shard_map/ppermute | solution.py:90
  62.1 56.4 %collective-permute-start.4 = (f32[4,272,512]{2,1,0:T(8,128)}, f32[4,272,512]{2,1,0:T(8,128)S(1)}, u32[]{:S(2)}, u32[]{:S(2)}) collective-permute-start(f32[4,272,512]{2,1,0:T(8,128)} %collective-permute-done), channel_id=1, source_target_pairs={{1,4},{3,2},{5,8},{7,6},{9,12},{11,10},{13,0},{15,14},{17,20},{19,... | collective-permute-start | bytes 6684680 | tf_op jit(solution)/shard_map/ppermute | solution.py:90
  63.4 55.1 %collective-permute-start.2 = (f32[4,272,512]{2,1,0:T(8,128)}, f32[4,272,512]{2,1,0:T(8,128)}, u32[]{:S(2)}, u32[]{:S(2)}) collective-permute-start(f32[4,272,512]{2,1,0:T(8,128)} %fusion.10), channel_id=1, source_target_pairs={{0,1},{2,3},{4,5},{6,7},{8,9},{10,11},{12,13},{14,15},{16,17},{18,... | collective-permute-start | bytes 6684680 | tf_op jit(solution)/shard_map/ppermute | solution.py:90
  73.6 73.8 %collective-permute-start.6 = (f32[3,256,512]{2,1,0:T(8,128)}, f32[3,256,512]{2,1,0:T(8,128)}, u32[]{:S(2)}, u32[]{:S(2)}) collective-permute-start(f32[3,256,512]{2,1,0:T(8,128)} %copy-done.1), channel_id=1, source_target_pairs={{0,2},{1,3},{2,4},{3,5},{4,6},{5,7},{6,8},{7,9},{8,10},{9,11},{10,... | collective-permute-start | bytes 4718600 | tf_op jit(solution)/shard_map/ppermute | solution.py:90
  123.0 3.3 %collective-permute-start.5 = (f32[256,512]{1,0:T(8,128)S(1)}, f32[256,512]{1,0:T(8,128)S(1)}, u32[]{:S(2)}, u32[]{:S(2)}) collective-permute-start(f32[256,512]{1,0:T(8,128)S(1)} %constant_dynamic-slice_fusion), channel_id=1, source_target_pairs={{0,16},{16,0},{1,17},{17,1},{2,18},{18,2},{3,19},{19,3},{4,20},{20... | collective-permute-start | bytes 1572872 | tf_op jit(solution)/shard_map/ppermute | solution.py:110
  123.1 24.3 %collective-permute-start.7 = (f32[256,512]{1,0:T(8,128)S(1)}, f32[256,512]{1,0:T(8,128)S(1)}, u32[]{:S(2)}, u32[]{:S(2)}) collective-permute-start(f32[256,512]{1,0:T(8,128)S(1)} %fusion.22), channel_id=1, source_target_pairs={{0,16},{16,0},{1,17},{17,1},{2,18},{18,2},{3,19},{19,3},{4,20},{20... | collective-permute-start | bytes 1572872 | tf_op jit(solution)/shard_map/ppermute | solution.py:110
  126.2 30.3 %collective-permute-start.8 = (f32[1,256,512]{2,1,0:T(8,128)S(1)}, f32[1,256,512]{2,1,0:T(8,128)S(1)}, u32[]{:S(2)}, u32[]{:S(2)}) collective-permute-start(f32[1,256,512]{2,1,0:T(8,128)S(1)} %get-tuple-element.30), channel_id=1, source_target_pairs={{0,2},{1,3},{2,4},{3,5},{4,6},{5,7},{6,8},{7,9},{8,10},{9,11},{10,... | collective-permute-start | bytes 1572872 | tf_op jit(solution)/shard_map/ppermute | solution.py:90

commit v3 on v1

v3 whole, which is shorter than its diff:
```python
import functools

import jax
import jax.numpy as jnp
from jax import lax
from jax.experimental import pallas as pl
from jax.experimental.pallas import tpu as pltpu
from jax.sharding import PartitionSpec as P


def split(value):
    high = value.astype(jnp.bfloat16)
    return high, (value - high.astype(jnp.float32)).astype(jnp.bfloat16)


def product_kernel(place_ref, left_ref, psi_ref, *refs, parts, groups):
    outs = refs[: len(parts)]
    left, psi, stack, result, read, write = refs[len(parts) :]
    terms, rows, width = left.shape
    block = place_ref[0]
    start = pl.multiple_of(place_ref[1] * rows, rows)
    size = terms // groups
    psi_copy = pltpu.make_async_copy(psi_ref.at[block], psi, read.at[0])
    psi_copy.start()
    reads = []
    for group in range(groups):
        span = pl.ds(group * size, size)
        copy = pltpu.make_async_copy(left_ref.at[span, block, pl.ds(start, rows)], left.at[span], read.at[1 + group])
        copy.start()
        reads.append(copy)
    psi_copy.wait()
    high, low = split(psi[...])
    stack[:width] = high
    stack[width : 2 * width] = high
    stack[2 * width :] = low
    places = [(part, i) for part, count in enumerate(parts) for i in range(count)]
    writes = []
    for group in range(groups):
        reads[group].wait()
        span = slice(group * size, (group + 1) * size)
        high, low = split(left[span].reshape(size * rows, width))
        value = jnp.dot(jnp.concatenate([high, low, high], axis=1), stack[...], preferred_element_type=jnp.float32)
        result[span] = value.reshape(size, rows, width)
        for term in range(group * size, (group + 1) * size):
            part, i = places[term]
            copy = pltpu.make_async_copy(result.at[term], outs[part].at[i], write.at[term])
            copy.start()
            writes.append(copy)
    for copy in writes:
        copy.wait()


def product(left_env, psi, block, row, rows, parts):
    terms, _, _, width = left_env.shape
    groups = 2 if terms % 2 == 0 else 1
    place = jnp.stack([jnp.asarray(block, jnp.int32), jnp.asarray(row, jnp.int32)])
    return pl.pallas_call(
        functools.partial(product_kernel, parts=parts, groups=groups),
        out_shape=[jax.ShapeDtypeStruct((count, rows, width), jnp.float32) for count in parts],
        in_specs=[
            pl.BlockSpec(memory_space=pltpu.SMEM),
            pl.BlockSpec(memory_space=pltpu.HBM),
            pl.BlockSpec(memory_space=pltpu.HBM),
        ],
        out_specs=[pl.BlockSpec(memory_space=pl.ANY)] * len(parts),
        scratch_shapes=[
            pltpu.VMEM((terms, rows, width), jnp.float32),
            pltpu.VMEM((width, width), jnp.float32),
            pltpu.VMEM((3 * width, width), jnp.bfloat16),
            pltpu.VMEM((terms, rows, width), jnp.float32),
            pltpu.SemaphoreType.DMA((1 + groups,)),
            pltpu.SemaphoreType.DMA((terms,)),
        ],
        compiler_params=pltpu.CompilerParams(vmem_limit_bytes=32 * 2**20),
        cost_estimate=pl.CostEstimate(
            flops=6 * terms * rows * width * width, bytes_accessed=8 * terms * rows * width, transcendentals=0
        ),
    )(place, left_env, psi)


def contract(first, second):
    return jnp.einsum("kac,kcd->ad", first, second, precision=lax.Precision.HIGH)


def per_device(psi, left_env, right_env, target):
    count = lax.axis_size("sec")
    me = lax.axis_index("sec")
    own = lax.axis_index("op")
    other = 1 - own
    odd = me % 2
    half = psi.shape[1] // 2
    terms = left_env.shape[0]

    def send(value, step, who=lambda d: True):
        pairs = [(d, (d + step(d)) % count) for d in range(count) if who(d)]
        return lax.ppermute(value, "sec", pairs)

    def exchange(value):
        return lax.ppermute(value, "op", [(0, 1), (1, 0)])

    def after(*values):
        return lax.optimization_barrier(values)

    def right_of(slot):
        return lax.dynamic_index_in_dim(right_env, slot, 1, keepdims=False)

    slots = [target[((me - j - 1) % count) * 2 + j] % 2 for j in range(2)]
    right = [right_of(slot) for slot in slots]
    left_env, psi = (pltpu.with_memory_space_constraint(a, pltpu.HBM) for a in (left_env, psi))
    rows_of = functools.partial(product, left_env, psi, rows=half)

    (value,) = rows_of(1 - odd, other, parts=(terms,))
    first = send(value, lambda d: (d ^ 2) - d if d % 2 else 2)
    (value,) = rows_of(0, own, parts=(terms,))
    beside = send(value, lambda d: (d ^ 1) - d)
    (value,) = rows_of(1, jnp.where(odd == 1, other, own), parts=(terms,))
    (kept,) = rows_of(odd, jnp.where(odd == 1, own, other), parts=(terms,))

    first, value, kept = after(first, value, kept)
    second = send(value, lambda d: 2)
    relayed = send(
        jnp.where(odd == 1, first, kept), lambda d: 1 if d % 2 == 0 else (-1 if d % 4 == 3 else 3)
    )
    most = send(jnp.where(odd == 1, kept[:-1], beside[:-1]), lambda d: 2)
    others_1 = contract(jnp.where(odd == 1, second, first), right[1])
    others_1, relayed = after(others_1, relayed)
    others_0 = contract(relayed, right[0])
    others_0, last = after(others_0, jnp.where(odd == 1, kept[-1:], beside[-1:]))
    last = send(last, lambda d: 2)

    early = contract(jnp.where(odd == 1, beside, second), right_of(jnp.where(odd == 1, *slots)))
    late_slot = jnp.where(odd == 1, slots[1], slots[0])
    late_right = right_of(late_slot)
    swapped = [exchange(others_0), exchange(others_1)]
    early = early + jnp.where(odd == 1, *swapped)
    late = contract(most, late_right[:-1]) + jnp.where(odd == 1, swapped[1], swapped[0])
    out, late = after(jnp.stack([early, early]), late)
    final = late + contract(last, late_right[-1:])
    return lax.dynamic_update_index_in_dim(out, final, late_slot, 0)


def solution(mesh):
    return jax.shard_map(
        per_device,
        mesh=mesh,
        in_specs=(
            P("sec", None, None),
            P("op", "sec", None, None),
            P("op", "sec", None, None),
            P(),
        ),
        out_specs=P("sec", "op", None),
        check_vma=False,
    )
```

time: 164 us -> 155 us (0.945)
  waiting for transfers between devices: 113 us -> 89.8 us
  Pallas kernels: 0 us -> 19.5 us
  matrix products: 27.4 us -> 19.3 us
  other arithmetic: 4.48 us -> 8.16 us
  local copies, waits for them, and re-layouts: 2.71 us -> 0.68 us
  starting transfers between devices: 10.9 us -> 12.9 us
    ppermute x4 -> x6, waiting for transfers between devices: 111 us -> 89.8 us  [send(): return lax.ppermute(value, 'sec', pairs)]
    pallas_call x0 -> x4, Pallas kernels: none -> 19.5 us  [product(): pl.pallas_call(functools.partial(product_kernel, parts=parts, groups=grou...]
    dot_general x3 -> x0, matrix products: 12.6 us -> none  [product(): jnp.einsum('kab,bc->kac', first, second, precision=lax.Precision.HIGH)]
    dot_general x3 -> x5, matrix products: 14.9 us -> 19.3 us  [contract(): jnp.einsum('kac,kcd->ad', first, second, precision=lax.Precision.HIGH)]
    select_n x1 -> x3, other arithmetic: 1.82 us -> 6.03 us  [the longest x1 3.11 us: per_device(): most = send(jnp.where(odd == 1, kept[:-1], beside[:-1]), lambda d: 2)]
    ppermute x2, waiting for transfers between devices: 2.01 us -> 0.01 us  [exchange(): return lax.ppermute(value, 'op', [(0, 1), (1, 0)])]
    unnamed x14 -> x6, local copies, waits for them, and re-layouts: 2.01 us -> 0.02 us
    ppermute x4 -> x6, starting transfers between devices: 10.8 us -> 12.3 us  [send(): return lax.ppermute(value, 'sec', pairs)]
  transfers between devices with their start and end apart: 6 -> 8, of which waited for: 4 -> 4; matrix products, arithmetic and copies ran while one was open for 16% -> 16% of each run, Pallas kernels for 0% -> 9%
where the time goes in v3:
time: 155 us
  waiting for transfers between devices  89.8 us (58%)
  Pallas kernels  19.5 us (13%)
  matrix products  19.3 us (12%)
  starting transfers between devices  12.9 us (8%)
  other arithmetic  8.16 us (5%)
  between operations  4.19 us (3%)
    ppermute x6, waiting for transfers between devices, send(): return lax.ppermute(value, 'sec', pairs)  89.8 us
    pallas_call x4, Pallas kernels, product(): pl.pallas_call(functools.partial(product_kernel, parts=parts, groups=grou...  19.5 us
    dot_general x5, matrix products, contract(): jnp.einsum('kac,kcd->ad', first, second, precision=lax.Precision.HIGH)  19.3 us
    ppermute x6, starting transfers between devices, send(): return lax.ppermute(value, 'sec', pairs)  12.3 us
    select_n x1, other arithmetic, per_device(): most = send(jnp.where(odd == 1, kept[:-1], beside[:-1]), lambda d: 2)  3.11 us
  transfers between devices with their start and end apart: 8, of which 4 were waited for; matrix products, arithmetic and copies ran while one was open for 16% of the time, Pallas kernels for 9%

profile of v3, /device:TPU:0, one launch (start us, length us, event | category | flops | bytes accessed | tf_op | source)
XLA Modules:
  0.0 154.6 jit_solution(5957722936224475669)
XLA Ops:
  0.0 0.1 pad_add_fusion
  0.1 5.1 %shard_map.47 = f32[4,256,512]{2,1,0:T(8,128)} custom-call(s32[2]{0:T(128)S(1)} %get-tuple-element.26.place_ref, f32[4,2,512,512]{3,2,1,0:T(8,128)} %left_ref.7, f32[2,512,512]{2,1,0:T(8,128)} %psi_ref.7), custom_call_target="tpu_custom_call" | custom-call | flops 1610612736 | bytes 4194304 | tf_op jit(solution)/shard_map/pallas_call | solution.py:57
  5.2 3.0 %collective-permute-start.1 = (f32[4,256,512]{2,1,0:T(8,128)}, f32[4,256,512]{2,1,0:T(8,128)}, u32[]{:S(2)}, u32[]{:S(2)}) collective-permute-start(f32[4,256,512]{2,1,0:T(8,128)} %shard_map.47), channel_id=1, source_target_pairs={{0,2},{1,3},{2,4},{3,1},{4,6},{5,7},{6,8},{7,5},{8,10},{9,11},{10,... | collective-permute-start | bytes 6291464 | tf_op jit(solution)/shard_map/ppermute | solution.py:96
  8.2 5.1 %shard_map.46 = f32[4,256,512]{2,1,0:T(8,128)} custom-call(s32[2]{0:T(128)S(1)} %get-tuple-element.25.place_ref, f32[4,2,512,512]{3,2,1,0:T(8,128)} %left_ref.7, f32[2,512,512]{2,1,0:T(8,128)} %psi_ref.7), custom_call_target="tpu_custom_call" | custom-call | flops 1610612736 | bytes 4194304 | tf_op jit(solution)/shard_map/pallas_call | solution.py:57
  13.3 1.6 %collective-permute-start = (f32[4,256,512]{2,1,0:T(8,128)}, f32[4,256,512]{2,1,0:T(8,128)}, u32[]{:S(2)}, u32[]{:S(2)}) collective-permute-start(f32[4,256,512]{2,1,0:T(8,128)} %shard_map.46), channel_id=1, source_target_pairs={{0,1},{1,0},{2,3},{3,2},{4,5},{5,4},{6,7},{7,6},{8,9},{9,8},{10,11... | collective-permute-start | bytes 6291464 | tf_op jit(solution)/shard_map/ppermute | solution.py:96
  14.9 0.1 pad_add_fusion.2
  15.0 5.1 %shard_map.48 = f32[4,256,512]{2,1,0:T(8,128)} custom-call(s32[2]{0:T(128)S(1)} %get-tuple-element.27.place_ref, f32[4,2,512,512]{3,2,1,0:T(8,128)} %left_ref.7, f32[2,512,512]{2,1,0:T(8,128)} %psi_ref.7), custom_call_target="tpu_custom_call" | custom-call | flops 1610612736 | bytes 4194304 | tf_op jit(solution)/shard_map/pallas_call | solution.py:57
  20.1 4.2 %shard_map.49 = f32[4,256,512]{2,1,0:T(8,128)S(1)} custom-call(s32[2]{0:T(128)S(1)} %get-tuple-element.28.place_ref, f32[4,2,512,512]{3,2,1,0:T(8,128)} %left_ref.7, f32[2,512,512]{2,1,0:T(8,128)} %psi_ref.7), custom_call_target="tpu_custom_call" | custom-call | flops 1610612736 | bytes 4194304 | tf_op jit(solution)/shard_map/pallas_call | solution.py:57
  24.3 0.0 copy-start
  24.3 32.9 %collective-permute-done.1 = f32[4,256,512]{2,1,0:T(8,128)} collective-permute-done((f32[4,256,512]{2,1,0:T(8,128)}, f32[4,256,512]{2,1,0:T(8,128)}, u32[]{:S(2)}, u32[]{:S(2)}) %collective-permute-start.1) | collective-permute-done | bytes 2097184 | tf_op jit(solution)/shard_map/ppermute | solution.py:96
  57.2 1.8 %broadcast_select_fusion = f32[4,256,512]{2,1,0:T(8,128)} fusion(f32[4,256,512]{2,1,0:T(8,128)} %collective-permute-done.1, f32[4,256,512]{2,1,0:T(8,128)S(1)} %shard_map.49, pred[]{:T(512)S(6)} %eq.8), kind=kLoop, calls=%fused_computation.24 | loop fusion | flops 524288 | bytes 6291457 | tf_op jit(solution)/shard_map/jit(_where)/select_n | solution.py:122
  59.0 1.8 %collective-permute-start.3 = (f32[4,256,512]{2,1,0:T(8,128)}, f32[4,256,512]{2,1,0:T(8,128)}, u32[]{:S(2)}, u32[]{:S(2)}) collective-permute-start(f32[4,256,512]{2,1,0:T(8,128)} %broadcast_select_fusion), channel_id=1, source_target_pairs={{0,1},{1,4},{2,3},{3,2},{4,5},{5,8},{6,7},{7,6},{8,9},{9,12},{10,1... | collective-permute-start | bytes 6291464 | tf_op jit(solution)/shard_map/ppermute | solution.py:96
  60.8 0.7 fusion.46
  65.5 0.0 slice-start
  65.5 3.1 %slice_select_fusion = f32[3,256,512]{2,1,0:T(8,128)} fusion(f32[4,256,512]{2,1,0:T(8,128)} %collective-permute-done, f32[4,256,512]{2,1,0:T(8,128)S(1)} %shard_map.49, pred[]{:T(512)S(6)} %eq.8), kind=kLoop, calls=%fused_computation.13 | loop fusion | flops 393216 | bytes 4718593 | tf_op jit(solution)/shard_map/jit(_where)/select_n | solution.py:124
  68.6 1.5 collective-permute-start.6
  70.1 1.1 slice_select_fusion.1
  71.3 0.0 slice-start.1
  71.3 37.5 %collective-permute-done.2 = f32[4,256,512]{2,1,0:T(8,128)} collective-permute-done((f32[4,256,512]{2,1,0:T(8,128)}, f32[4,256,512]{2,1,0:T(8,128)}, u32[]{:S(2)}, u32[]{:S(2)}) %collective-permute-start.2) | collective-permute-done | bytes 2097184 | tf_op jit(solution)/shard_map/ppermute | solution.py:96
  108.8 4.8 %fusion.21 = f32[256,512]{1,0:T(8,128)S(1)} fusion(f32[4,2,512,512]{3,2,1,0:T(8,128)} %param.6, s32[]{:T(128)S(6)} %select_n.115, f32[4,256,512]{2,1,0:T(8,128)} %collective-permute-done.2, f32[4,256,512]{2,1,0:T(8,128)} %collective-permute-done.1, pred[]{:T(512)S(6)} %eq.8), kind=kOutput, calls=%fused_computation.17 | convolution fusion | flops 1611137024 | bytes 8912901 | tf_op jit(solution)/shard_map/kac,kcd->ad/dot_general | solution.py:82
  113.6 0.0 collective-permute-done.3
  113.7 3.9 %fusion.12 = f32[256,512]{1,0:T(8,128)S(1)} fusion(f32[4,256,512]{2,1,0:T(8,128)} %collective-permute-done.3, f32[4,2,512,512]{3,2,1,0:T(8,128)S(1)} %bitcast.66, s32[]{:T(128)S(6)} %select_n.117), kind=kOutput, calls=%fused_computation.14 | convolution fusion | flops 1610612736 | bytes 6815748 | tf_op jit(solution)/shard_map/kac,kcd->ad/dot_general | solution.py:82
  117.5 0.1 collective-permute-start.4
  117.6 0.5 collective-permute-start.5
  118.1 4.4 %collective-permute-start.7 = (f32[1,256,512]{2,1,0:T(8,128)S(1)}, f32[1,256,512]{2,1,0:T(8,128)S(1)}, u32[]{:S(2)}, u32[]{:S(2)}) collective-permute-start(f32[1,256,512]{2,1,0:T(8,128)S(1)} %slice_select_fusion.1), channel_id=1, source_target_pairs={{0,2},{1,3},{2,4},{3,5},{4,6},{5,7},{6,8},{7,9},{8,10},{9,11},{10,... | collective-permute-start | bytes 1572872 | tf_op jit(solution)/shard_map/ppermute | solution.py:96
  122.6 4.8 %fusion.31 = f32[1,256,512]{2,1,0:T(8,128)S(1)} fusion(f32[4,2,512,512]{3,2,1,0:T(8,128)} %param.6, s32[]{:T(128)S(6)} %select_n.112, f32[4,256,512]{2,1,0:T(8,128)} %collective-permute-done, f32[4,256,512]{2,1,0:T(8,128)} %collective-permute-done.2, pred[]{:T(512)S(6)} %eq.8, f32[256,512]{1,0:T(8,128)S(1)} %collective-permute-done.4, ...), kind=kOutput, calls=%fused_computation.19 | convolution fusion | flops 1611399168 | bytes 9963008 | tf_op jit(solution)/shard_map/kac,kcd->ad/dot_general | solution.py:82
  127.4 1.1 pad_maximum_fusion
  128.5 14.0 %collective-permute-done.6 = f32[3,256,512]{2,1,0:T(8,128)} collective-permute-done((f32[3,256,512]{2,1,0:T(8,128)}, f32[3,256,512]{2,1,0:T(8,128)}, u32[]{:S(2)}, u32[]{:S(2)}) %collective-permute-start.6) | collective-permute-done | bytes 1572896 | tf_op jit(solution)/shard_map/ppermute | solution.py:96
  142.5 3.9 %fusion.36 = f32[256,512]{1,0:T(8,128)S(1)} fusion(f32[3,256,512]{2,1,0:T(8,128)} %collective-permute-done.6, f32[4,2,512,512]{3,2,1,0:T(8,128)} %param.6, s32[]{:T(128)S(6)} %select_n.124, f32[256,512]{1,0:T(8,128)S(1)} %collective-permute-done.5, f32[256,512]{1,0:T(8,128)S(1)} %collective-permute-done.4, pred[]{:T(512)S(6)} %eq.8), kind=kOutput, calls=%fused_computation.20 | convolution fusion | flops 1208221696 | bytes 6291461 | tf_op jit(solution)/shard_map/kac,kcd->ad/dot_general | solution.py:82
  146.4 5.5 %collective-permute-done.7 = f32[1,256,512]{2,1,0:T(8,128)S(1)} collective-permute-done((f32[1,256,512]{2,1,0:T(8,128)S(1)}, f32[1,256,512]{2,1,0:T(8,128)S(1)}, u32[]{:S(2)}, u32[]{:S(2)}) %collective-permute-start.7) | collective-permute-done | bytes 524320 | tf_op jit(solution)/shard_map/ppermute | solution.py:96
  151.9 1.8 %fusion.37 = f32[256,512]{1,0:T(8,128)S(1)} fusion(f32[4,2,512,512]{3,2,1,0:T(8,128)} %param.6, s32[]{:T(128)S(6)} %add.74, s32[]{:T(128)S(6)} %select_n.124, f32[1,256,512]{2,1,0:T(8,128)S(1)} %collective-permute-done.7), kind=kOutput, calls=%fused_computation.22 | convolution fusion | flops 402653184 | bytes 2097160 | tf_op jit(solution)/shard_map/kac,kcd->ad/dot_general | solution.py:82
  153.7 0.9 bitcast_dynamic-update-slice_fusion
  (8 shorter events, 0.0 us)
Async XLA Ops:
  5.2 52.0 %collective-permute-start.1 = (f32[4,256,512]{2,1,0:T(8,128)}, f32[4,256,512]{2,1,0:T(8,128)}, u32[]{:S(2)}, u32[]{:S(2)}) collective-permute-start(f32[4,256,512]{2,1,0:T(8,128)} %shard_map.47), channel_id=1, source_target_pairs={{0,2},{1,3},{2,4},{3,1},{4,6},{5,7},{6,8},{7,5},{8,10},{9,11},{10,... | collective-permute-start | bytes 6291464 | tf_op jit(solution)/shard_map/ppermute | solution.py:96
  13.3 52.2 %collective-permute-start = (f32[4,256,512]{2,1,0:T(8,128)}, f32[4,256,512]{2,1,0:T(8,128)}, u32[]{:S(2)}, u32[]{:S(2)}) collective-permute-start(f32[4,256,512]{2,1,0:T(8,128)} %shard_map.46), channel_id=1, source_target_pairs={{0,1},{1,0},{2,3},{3,2},{4,5},{5,4},{6,7},{7,6},{8,9},{9,8},{10,11... | collective-permute-start | bytes 6291464 | tf_op jit(solution)/shard_map/ppermute | solution.py:96
  24.3 36.5 %copy-start = (s32[32]{0:T(128)S(1)}, s32[32]{0:T(128)}, u32[]{:S(2)}) copy-start(s32[32]{0:T(128)} %param.7) | copy-start | bytes 388
  57.2 51.6 %collective-permute-start.2 = (f32[4,256,512]{2,1,0:T(8,128)}, f32[4,256,512]{2,1,0:T(8,128)}, u32[]{:S(2)}, u32[]{:S(2)}) collective-permute-start(f32[4,256,512]{2,1,0:T(8,128)} %shard_map.48), channel_id=1, source_target_pairs={{0,2},{1,3},{2,4},{3,5},{4,6},{5,7},{6,8},{7,9},{8,10},{9,11},{10,... | collective-permute-start | bytes 6291464 | tf_op jit(solution)/shard_map/ppermute | solution.py:96
  59.0 54.6 %collective-permute-start.3 = (f32[4,256,512]{2,1,0:T(8,128)}, f32[4,256,512]{2,1,0:T(8,128)}, u32[]{:S(2)}, u32[]{:S(2)}) collective-permute-start(f32[4,256,512]{2,1,0:T(8,128)} %broadcast_select_fusion), channel_id=1, source_target_pairs={{0,1},{1,4},{2,3},{3,2},{4,5},{5,8},{6,7},{7,6},{8,9},{9,12},{10,1... | collective-permute-start | bytes 6291464 | tf_op jit(solution)/shard_map/ppermute | solution.py:96
  65.5 48.1 %slice-start = ((s8[8388608]{0:T(1024)(128)(4,1)}), s8[4194304]{0:T(1024)(128)(4,1)S(1)}, s32[]{:S(2)}) async-start(s8[8388608]{0:T(1024)(128)(4,1)} %bitcast.65), calls=%async_computation | async-start | bytes 8388608
  68.6 73.9 %collective-permute-start.6 = (f32[3,256,512]{2,1,0:T(8,128)}, f32[3,256,512]{2,1,0:T(8,128)}, u32[]{:S(2)}, u32[]{:S(2)}) collective-permute-start(f32[3,256,512]{2,1,0:T(8,128)} %slice_select_fusion), channel_id=1, source_target_pairs={{0,2},{1,3},{2,4},{3,5},{4,6},{5,7},{6,8},{7,9},{8,10},{9,11},{10,... | collective-permute-start | bytes 4718600 | tf_op jit(solution)/shard_map/ppermute | solution.py:96
  71.3 42.4 %slice-start.1 = ((s8[8388608]{0:T(1024)(128)(4,1)}), s8[4194304]{0:T(1024)(128)(4,1)S(1)}, s32[]{:S(2)}) async-start(s8[8388608]{0:T(1024)(128)(4,1)} %bitcast.65), calls=%async_computation.1 | async-start | bytes 8388608
  117.5 5.0 %collective-permute-start.4 = (f32[256,512]{1,0:T(8,128)S(1)}, f32[256,512]{1,0:T(8,128)S(1)}, u32[]{:S(2)}, u32[]{:S(2)}) collective-permute-start(f32[256,512]{1,0:T(8,128)S(1)} %fusion.12), channel_id=1, source_target_pairs={{0,16},{16,0},{1,17},{17,1},{2,18},{18,2},{3,19},{19,3},{4,20},{20... | collective-permute-start | bytes 1572872 | tf_op jit(solution)/shard_map/ppermute | solution.py:99
  117.6 4.9 %collective-permute-start.5 = (f32[256,512]{1,0:T(8,128)S(1)}, f32[256,512]{1,0:T(8,128)S(1)}, u32[]{:S(2)}, u32[]{:S(2)}) collective-permute-start(f32[256,512]{1,0:T(8,128)S(1)} %fusion.21), channel_id=1, source_target_pairs={{0,16},{16,0},{1,17},{17,1},{2,18},{18,2},{3,19},{19,3},{4,20},{20... | collective-permute-start | bytes 1572872 | tf_op jit(solution)/shard_map/ppermute | solution.py:99
  118.1 33.7 %collective-permute-start.7 = (f32[1,256,512]{2,1,0:T(8,128)S(1)}, f32[1,256,512]{2,1,0:T(8,128)S(1)}, u32[]{:S(2)}, u32[]{:S(2)}) collective-permute-start(f32[1,256,512]{2,1,0:T(8,128)S(1)} %slice_select_fusion.1), channel_id=1, source_target_pairs={{0,2},{1,3},{2,4},{3,5},{4,6},{5,7},{6,8},{7,9},{8,10},{9,11},{10,... | collective-permute-start | bytes 1572872 | tf_op jit(solution)/shard_map/ppermute | solution.py:96

commit v4 on v3

--- a/solution.py
+++ b/solution.py
@@ -13,9 +13,7 @@
     return high, (value - high.astype(jnp.float32)).astype(jnp.bfloat16)
 
 
-def product_kernel(place_ref, left_ref, psi_ref, *refs, parts, groups):
-    outs = refs[: len(parts)]
-    left, psi, stack, result, read, write = refs[len(parts) :]
+def product_kernel(place_ref, left_ref, psi_ref, out_ref, left, psi, stack, result, read, write, *, first, groups):
     terms, rows, width = left.shape
     block = place_ref[0]
     start = pl.multiple_of(place_ref[1] * rows, rows)
@@ -25,7 +23,8 @@
     reads = []
     for group in range(groups):
         span = pl.ds(group * size, size)
-        copy = pltpu.make_async_copy(left_ref.at[span, block, pl.ds(start, rows)], left.at[span], read.at[1 + group])
+        source = left_ref.at[pl.ds(first + group * size, size), block, pl.ds(start, rows)]
+        copy = pltpu.make_async_copy(source, left.at[span], read.at[1 + group])
         copy.start()
         reads.append(copy)
     psi_copy.wait()
@@ -33,7 +32,6 @@
     stack[:width] = high
     stack[width : 2 * width] = high
     stack[2 * width :] = low
-    places = [(part, i) for part, count in enumerate(parts) for i in range(count)]
     writes = []
     for group in range(groups):
         reads[group].wait()
@@ -41,39 +39,38 @@
         high, low = split(left[span].reshape(size * rows, width))
         value = jnp.dot(jnp.concatenate([high, low, high], axis=1), stack[...], preferred_element_type=jnp.float32)
         result[span] = value.reshape(size, rows, width)
-        for term in range(group * size, (group + 1) * size):
-            part, i = places[term]
-            copy = pltpu.make_async_copy(result.at[term], outs[part].at[i], write.at[term])
-            copy.start()
-            writes.append(copy)
+        copy = pltpu.make_async_copy(result.at[pl.ds(group * size, size)], out_ref.at[pl.ds(group * size, size)], write.at[group])
+        copy.start()
+        writes.append(copy)
     for copy in writes:
         copy.wait()
 
 
-def product(left_env, psi, block, row, rows, parts):
-    terms, _, _, width = left_env.shape
-    groups = 2 if terms % 2 == 0 else 1
+def product(left_env, psi, block, row, rows, first=0, terms=None, cost=1):
+    width = psi.shape[-1]
+    terms = terms or left_env.shape[0] - first
+    groups = 2 if terms % 2 == 0 else terms
     place = jnp.stack([jnp.asarray(block, jnp.int32), jnp.asarray(row, jnp.int32)])
     return pl.pallas_call(
-        functools.partial(product_kernel, parts=parts, groups=groups),
-        out_shape=[jax.ShapeDtypeStruct((count, rows, width), jnp.float32) for count in parts],
+        functools.partial(product_kernel, first=first, groups=groups),
+        out_shape=jax.ShapeDtypeStruct((terms, rows, width), jnp.float32),
         in_specs=[
             pl.BlockSpec(memory_space=pltpu.SMEM),
             pl.BlockSpec(memory_space=pltpu.HBM),
             pl.BlockSpec(memory_space=pltpu.HBM),
         ],
-        out_specs=[pl.BlockSpec(memory_space=pl.ANY)] * len(parts),
+        out_specs=pl.BlockSpec(memory_space=pl.ANY),
         scratch_shapes=[
             pltpu.VMEM((terms, rows, width), jnp.float32),
             pltpu.VMEM((width, width), jnp.float32),
             pltpu.VMEM((3 * width, width), jnp.bfloat16),
             pltpu.VMEM((terms, rows, width), jnp.float32),
             pltpu.SemaphoreType.DMA((1 + groups,)),
-            pltpu.SemaphoreType.DMA((terms,)),
+            pltpu.SemaphoreType.DMA((groups,)),
         ],
         compiler_params=pltpu.CompilerParams(vmem_limit_bytes=32 * 2**20),
         cost_estimate=pl.CostEstimate(
-            flops=6 * terms * rows * width * width, bytes_accessed=8 * terms * rows * width, transcendentals=0
+            flops=6 * terms * rows * width * width * cost, bytes_accessed=8 * terms * rows * width, transcendentals=0
         ),
     )(place, left_env, psi)
 
@@ -109,12 +106,12 @@
     left_env, psi = (pltpu.with_memory_space_constraint(a, pltpu.HBM) for a in (left_env, psi))
     rows_of = functools.partial(product, left_env, psi, rows=half)
 
-    (value,) = rows_of(1 - odd, other, parts=(terms,))
+    value = rows_of(1 - odd, other)
     first = send(value, lambda d: (d ^ 2) - d if d % 2 else 2)
-    (value,) = rows_of(0, own, parts=(terms,))
+    value = rows_of(0, own)
     beside = send(value, lambda d: (d ^ 1) - d)
-    (value,) = rows_of(1, jnp.where(odd == 1, other, own), parts=(terms,))
-    (kept,) = rows_of(odd, jnp.where(odd == 1, own, other), parts=(terms,))
+    value = rows_of(1, jnp.where(odd == 1, other, own))
+    kept = rows_of(odd, jnp.where(odd == 1, own, other))
 
     first, value, kept = after(first, value, kept)
     second = send(value, lambda d: 2)
@@ -134,8 +131,8 @@
     swapped = [exchange(others_0), exchange(others_1)]
     early = early + jnp.where(odd == 1, *swapped)
     late = contract(most, late_right[:-1]) + jnp.where(odd == 1, swapped[1], swapped[0])
-    out, late = after(jnp.stack([early, early]), late)
-    final = late + contract(last, late_right[-1:])
+    out, late, late_right = after(jnp.stack([early, early]), late, late_right[-1])
+    final = late + jnp.dot(last[0], late_right, precision=lax.Precision.HIGH)
     return lax.dynamic_update_index_in_dim(out, final, late_slot, 0)
 
 

time: 155 us -> 154 us (level)
    dot_general x5 -> x4, matrix products: 19.3 us -> 17.5 us  [contract(): jnp.einsum('kac,kcd->ad', first, second, precision=lax.Precision.HIGH)]
  transfers between devices with their start and end apart: 8 -> 8, of which waited for: 4 -> 4; matrix products, arithmetic and copies ran while one was open for 16% -> 17% of each run, Pallas kernels for 9% -> 9%
where the time goes in v4:
time: 154 us; the launch traced here: 153 us
  waiting for transfers between devices  88.4 us (57%)
  Pallas kernels  19.5 us (13%)
  matrix products  18.1 us (12%)
  starting transfers between devices  13.1 us (9%)
  other arithmetic  8.16 us (5%)
  between operations  4.2 us (3%)
  local copies, waits for them, and re-layouts  1.98 us (1%)
    ppermute x6, waiting for transfers between devices, send(): return lax.ppermute(value, 'sec', pairs)  88.4 us
    pallas_call x4, Pallas kernels, product(): pl.pallas_call(functools.partial(product_kernel, first=first, groups=grou...  19.5 us
    dot_general x4, matrix products, contract(): jnp.einsum('kac,kcd->ad', first, second, precision=lax.Precision.HIGH)  17.5 us
    ppermute x6, starting transfers between devices, send(): return lax.ppermute(value, 'sec', pairs)  12.5 us
    select_n x1, other arithmetic, per_device(): most = send(jnp.where(odd == 1, kept[:-1], beside[:-1]), lambda d: 2)  3.11 us
  transfers between devices with their start and end apart: 8, of which 4 were waited for; matrix products, arithmetic and copies ran while one was open for 17% of the time, Pallas kernels for 9%

profile of v4, /device:TPU:0, one launch (start us, length us, event | category | flops | bytes accessed | tf_op | source)
XLA Modules:
  0.0 153.4 jit_solution(13263472115934733325)
XLA Ops:
  0.0 0.1 pad_add_fusion
  0.1 5.1 %shard_map.47 = f32[4,256,512]{2,1,0:T(8,128)} custom-call(s32[2]{0:T(128)S(1)} %get-tuple-element.28.place_ref, f32[4,2,512,512]{3,2,1,0:T(8,128)} %left_ref.7, f32[2,512,512]{2,1,0:T(8,128)} %psi_ref.7), custom_call_target="tpu_custom_call" | custom-call | flops 1610612736 | bytes 4194304 | tf_op jit(solution)/shard_map/pallas_call | solution.py:54
  5.2 3.0 %collective-permute-start.1 = (f32[4,256,512]{2,1,0:T(8,128)}, f32[4,256,512]{2,1,0:T(8,128)}, u32[]{:S(2)}, u32[]{:S(2)}) collective-permute-start(f32[4,256,512]{2,1,0:T(8,128)} %shard_map.47), channel_id=1, source_target_pairs={{0,2},{1,3},{2,4},{3,1},{4,6},{5,7},{6,8},{7,5},{8,10},{9,11},{10,... | collective-permute-start | bytes 6291464 | tf_op jit(solution)/shard_map/ppermute | solution.py:93
  8.2 5.1 %shard_map.46 = f32[4,256,512]{2,1,0:T(8,128)} custom-call(s32[2]{0:T(128)S(1)} %get-tuple-element.27.place_ref, f32[4,2,512,512]{3,2,1,0:T(8,128)} %left_ref.7, f32[2,512,512]{2,1,0:T(8,128)} %psi_ref.7), custom_call_target="tpu_custom_call" | custom-call | flops 1610612736 | bytes 4194304 | tf_op jit(solution)/shard_map/pallas_call | solution.py:54
  13.3 1.6 %collective-permute-start = (f32[4,256,512]{2,1,0:T(8,128)}, f32[4,256,512]{2,1,0:T(8,128)}, u32[]{:S(2)}, u32[]{:S(2)}) collective-permute-start(f32[4,256,512]{2,1,0:T(8,128)} %shard_map.46), channel_id=1, source_target_pairs={{0,1},{1,0},{2,3},{3,2},{4,5},{5,4},{6,7},{7,6},{8,9},{9,8},{10,11... | collective-permute-start | bytes 6291464 | tf_op jit(solution)/shard_map/ppermute | solution.py:93
  14.9 0.1 pad_add_fusion.2
  14.9 5.1 %shard_map.48 = f32[4,256,512]{2,1,0:T(8,128)} custom-call(s32[2]{0:T(128)S(1)} %get-tuple-element.29.place_ref, f32[4,2,512,512]{3,2,1,0:T(8,128)} %left_ref.7, f32[2,512,512]{2,1,0:T(8,128)} %psi_ref.7), custom_call_target="tpu_custom_call" | custom-call | flops 1610612736 | bytes 4194304 | tf_op jit(solution)/shard_map/pallas_call | solution.py:54
  20.0 4.2 %shard_map.49 = f32[4,256,512]{2,1,0:T(8,128)S(1)} custom-call(s32[2]{0:T(128)S(1)} %get-tuple-element.30.place_ref, f32[4,2,512,512]{3,2,1,0:T(8,128)} %left_ref.7, f32[2,512,512]{2,1,0:T(8,128)} %psi_ref.7), custom_call_target="tpu_custom_call" | custom-call | flops 1610612736 | bytes 4194304 | tf_op jit(solution)/shard_map/pallas_call | solution.py:54
  24.2 0.0 copy-start
  24.3 32.9 %collective-permute-done.1 = f32[4,256,512]{2,1,0:T(8,128)} collective-permute-done((f32[4,256,512]{2,1,0:T(8,128)}, f32[4,256,512]{2,1,0:T(8,128)}, u32[]{:S(2)}, u32[]{:S(2)}) %collective-permute-start.1) | collective-permute-done | bytes 2097184 | tf_op jit(solution)/shard_map/ppermute | solution.py:93
  57.2 1.8 %broadcast_select_fusion = f32[4,256,512]{2,1,0:T(8,128)} fusion(f32[4,256,512]{2,1,0:T(8,128)} %collective-permute-done.1, f32[4,256,512]{2,1,0:T(8,128)S(1)} %shard_map.49, pred[]{:T(512)S(6)} %eq.8), kind=kLoop, calls=%fused_computation.23 | loop fusion | flops 524288 | bytes 6291457 | tf_op jit(solution)/shard_map/jit(_where)/select_n | solution.py:119
  59.0 1.8 %collective-permute-start.3 = (f32[4,256,512]{2,1,0:T(8,128)}, f32[4,256,512]{2,1,0:T(8,128)}, u32[]{:S(2)}, u32[]{:S(2)}) collective-permute-start(f32[4,256,512]{2,1,0:T(8,128)} %broadcast_select_fusion), channel_id=1, source_target_pairs={{0,1},{1,4},{2,3},{3,2},{4,5},{5,8},{6,7},{7,6},{8,9},{9,12},{10,1... | collective-permute-start | bytes 6291464 | tf_op jit(solution)/shard_map/ppermute | solution.py:93
  60.8 0.7 fusion.45
  65.5 0.0 slice-start
  65.5 3.1 %slice_select_fusion = f32[3,256,512]{2,1,0:T(8,128)} fusion(f32[4,256,512]{2,1,0:T(8,128)} %collective-permute-done, f32[4,256,512]{2,1,0:T(8,128)S(1)} %shard_map.49, pred[]{:T(512)S(6)} %eq.8), kind=kLoop, calls=%fused_computation.13 | loop fusion | flops 393216 | bytes 4718593 | tf_op jit(solution)/shard_map/jit(_where)/select_n | solution.py:121
  68.6 1.5 collective-permute-start.6
  70.1 1.1 slice_select_fusion.1
  71.3 0.0 slice-start.1
  71.3 37.5 %collective-permute-done.2 = f32[4,256,512]{2,1,0:T(8,128)} collective-permute-done((f32[4,256,512]{2,1,0:T(8,128)}, f32[4,256,512]{2,1,0:T(8,128)}, u32[]{:S(2)}, u32[]{:S(2)}) %collective-permute-start.2) | collective-permute-done | bytes 2097184 | tf_op jit(solution)/shard_map/ppermute | solution.py:93
  108.8 4.8 %fusion.21 = f32[256,512]{1,0:T(8,128)S(1)} fusion(f32[4,2,512,512]{3,2,1,0:T(8,128)} %param.6, s32[]{:T(128)S(6)} %select_n.115, f32[4,256,512]{2,1,0:T(8,128)} %collective-permute-done.2, f32[4,256,512]{2,1,0:T(8,128)} %collective-permute-done.1, pred[]{:T(512)S(6)} %eq.8), kind=kOutput, calls=%fused_computation.17 | convolution fusion | flops 1611137024 | bytes 8912901 | tf_op jit(solution)/shard_map/kac,kcd->ad/dot_general | solution.py:79
  113.6 3.9 %fusion.12 = f32[256,512]{1,0:T(8,128)S(1)} fusion(f32[4,256,512]{2,1,0:T(8,128)} %collective-permute-done.3, f32[4,2,512,512]{3,2,1,0:T(8,128)S(1)} %bitcast.66, s32[]{:T(128)S(6)} %select_n.117), kind=kOutput, calls=%fused_computation.14 | convolution fusion | flops 1610612736 | bytes 6815748 | tf_op jit(solution)/shard_map/kac,kcd->ad/dot_general | solution.py:79
  117.5 0.1 collective-permute-start.4
  117.6 0.5 collective-permute-start.5
  118.1 1.3 dynamic-slice_bitcast_fusion.6
  119.4 4.6 %collective-permute-start.7 = (f32[1,256,512]{2,1,0:T(8,128)S(1)}, f32[1,256,512]{2,1,0:T(8,128)S(1)}, u32[]{:S(2)}, u32[]{:S(2)}) collective-permute-start(f32[1,256,512]{2,1,0:T(8,128)S(1)} %slice_select_fusion.1), channel_id=1, source_target_pairs={{0,2},{1,3},{2,4},{3,5},{4,6},{5,7},{6,8},{7,9},{8,10},{9,11},{10,... | collective-permute-start | bytes 1572872 | tf_op jit(solution)/shard_map/ppermute | solution.py:93
  124.1 4.8 %fusion.31 = f32[1,256,512]{2,1,0:T(8,128)S(1)} fusion(f32[4,2,512,512]{3,2,1,0:T(8,128)} %param.6, s32[]{:T(128)S(6)} %select_n.112, f32[4,256,512]{2,1,0:T(8,128)} %collective-permute-done, f32[4,256,512]{2,1,0:T(8,128)} %collective-permute-done.2, pred[]{:T(512)S(6)} %eq.8, f32[256,512]{1,0:T(8,128)S(1)} %collective-permute-done.4, ...), kind=kOutput, calls=%fused_computation.19 | convolution fusion | flops 1611399168 | bytes 9963008 | tf_op jit(solution)/shard_map/kac,kcd->ad/dot_general | solution.py:79
  128.9 1.1 pad_maximum_fusion
  130.0 12.5 %collective-permute-done.6 = f32[3,256,512]{2,1,0:T(8,128)} collective-permute-done((f32[3,256,512]{2,1,0:T(8,128)}, f32[3,256,512]{2,1,0:T(8,128)}, u32[]{:S(2)}, u32[]{:S(2)}) %collective-permute-start.6) | collective-permute-done | bytes 1572896 | tf_op jit(solution)/shard_map/ppermute | solution.py:93
  142.5 3.9 %fusion.36 = f32[256,512]{1,0:T(8,128)S(1)} fusion(f32[3,256,512]{2,1,0:T(8,128)} %collective-permute-done.6, f32[4,2,512,512]{3,2,1,0:T(8,128)} %param.6, s32[]{:T(128)S(6)} %select_n.124, f32[256,512]{1,0:T(8,128)S(1)} %collective-permute-done.5, f32[256,512]{1,0:T(8,128)S(1)} %collective-permute-done.4, pred[]{:T(512)S(6)} %eq.8), kind=kOutput, calls=%fused_computation.20 | convolution fusion | flops 1208221696 | bytes 6291461 | tf_op jit(solution)/shard_map/kac,kcd->ad/dot_general | solution.py:79
  146.4 5.5 %collective-permute-done.7 = f32[1,256,512]{2,1,0:T(8,128)S(1)} collective-permute-done((f32[1,256,512]{2,1,0:T(8,128)S(1)}, f32[1,256,512]{2,1,0:T(8,128)S(1)}, u32[]{:S(2)}, u32[]{:S(2)}) %collective-permute-start.7) | collective-permute-done | bytes 524320 | tf_op jit(solution)/shard_map/ppermute | solution.py:93
  151.9 0.6 fusion.39
  152.5 0.9 bitcast_dynamic-update-slice_fusion
  (9 shorter events, 0.0 us)
Async XLA Ops:
  5.2 52.0 %collective-permute-start.1 = (f32[4,256,512]{2,1,0:T(8,128)}, f32[4,256,512]{2,1,0:T(8,128)}, u32[]{:S(2)}, u32[]{:S(2)}) collective-permute-start(f32[4,256,512]{2,1,0:T(8,128)} %shard_map.47), channel_id=1, source_target_pairs={{0,2},{1,3},{2,4},{3,1},{4,6},{5,7},{6,8},{7,5},{8,10},{9,11},{10,... | collective-permute-start | bytes 6291464 | tf_op jit(solution)/shard_map/ppermute | solution.py:93
  13.3 52.2 %collective-permute-start = (f32[4,256,512]{2,1,0:T(8,128)}, f32[4,256,512]{2,1,0:T(8,128)}, u32[]{:S(2)}, u32[]{:S(2)}) collective-permute-start(f32[4,256,512]{2,1,0:T(8,128)} %shard_map.46), channel_id=1, source_target_pairs={{0,1},{1,0},{2,3},{3,2},{4,5},{5,4},{6,7},{7,6},{8,9},{9,8},{10,11... | collective-permute-start | bytes 6291464 | tf_op jit(solution)/shard_map/ppermute | solution.py:93
  24.2 36.5 %copy-start = (s32[32]{0:T(128)S(1)}, s32[32]{0:T(128)}, u32[]{:S(2)}) copy-start(s32[32]{0:T(128)} %param.7) | copy-start | bytes 388
  57.2 51.6 %collective-permute-start.2 = (f32[4,256,512]{2,1,0:T(8,128)}, f32[4,256,512]{2,1,0:T(8,128)}, u32[]{:S(2)}, u32[]{:S(2)}) collective-permute-start(f32[4,256,512]{2,1,0:T(8,128)} %shard_map.48), channel_id=1, source_target_pairs={{0,2},{1,3},{2,4},{3,5},{4,6},{5,7},{6,8},{7,9},{8,10},{9,11},{10,... | collective-permute-start | bytes 6291464 | tf_op jit(solution)/shard_map/ppermute | solution.py:93
  59.0 54.6 %collective-permute-start.3 = (f32[4,256,512]{2,1,0:T(8,128)}, f32[4,256,512]{2,1,0:T(8,128)}, u32[]{:S(2)}, u32[]{:S(2)}) collective-permute-start(f32[4,256,512]{2,1,0:T(8,128)} %broadcast_select_fusion), channel_id=1, source_target_pairs={{0,1},{1,4},{2,3},{3,2},{4,5},{5,8},{6,7},{7,6},{8,9},{9,12},{10,1... | collective-permute-start | bytes 6291464 | tf_op jit(solution)/shard_map/ppermute | solution.py:93
  65.5 48.1 %slice-start = ((s8[8388608]{0:T(1024)(128)(4,1)}), s8[4194304]{0:T(1024)(128)(4,1)S(1)}, s32[]{:S(2)}) async-start(s8[8388608]{0:T(1024)(128)(4,1)} %bitcast.65), calls=%async_computation | async-start | bytes 8388608
  68.6 73.9 %collective-permute-start.6 = (f32[3,256,512]{2,1,0:T(8,128)}, f32[3,256,512]{2,1,0:T(8,128)}, u32[]{:S(2)}, u32[]{:S(2)}) collective-permute-start(f32[3,256,512]{2,1,0:T(8,128)} %slice_select_fusion), channel_id=1, source_target_pairs={{0,2},{1,3},{2,4},{3,5},{4,6},{5,7},{6,8},{7,9},{8,10},{9,11},{10,... | collective-permute-start | bytes 4718600 | tf_op jit(solution)/shard_map/ppermute | solution.py:93
  71.3 42.4 %slice-start.1 = ((s8[8388608]{0:T(1024)(128)(4,1)}), s8[4194304]{0:T(1024)(128)(4,1)S(1)}, s32[]{:S(2)}) async-start(s8[8388608]{0:T(1024)(128)(4,1)} %bitcast.65), calls=%async_computation.1 | async-start | bytes 8388608
  117.5 6.5 %collective-permute-start.4 = (f32[256,512]{1,0:T(8,128)S(1)}, f32[256,512]{1,0:T(8,128)S(1)}, u32[]{:S(2)}, u32[]{:S(2)}) collective-permute-start(f32[256,512]{1,0:T(8,128)S(1)} %fusion.12), channel_id=1, source_target_pairs={{0,16},{16,0},{1,17},{17,1},{2,18},{18,2},{3,19},{19,3},{4,20},{20... | collective-permute-start | bytes 1572872 | tf_op jit(solution)/shard_map/ppermute | solution.py:96
  117.6 6.4 %collective-permute-start.5 = (f32[256,512]{1,0:T(8,128)S(1)}, f32[256,512]{1,0:T(8,128)S(1)}, u32[]{:S(2)}, u32[]{:S(2)}) collective-permute-start(f32[256,512]{1,0:T(8,128)S(1)} %fusion.21), channel_id=1, source_target_pairs={{0,16},{16,0},{1,17},{17,1},{2,18},{18,2},{3,19},{19,3},{4,20},{20... | collective-permute-start | bytes 1572872 | tf_op jit(solution)/shard_map/ppermute | solution.py:96
  119.4 32.5 %collective-permute-start.7 = (f32[1,256,512]{2,1,0:T(8,128)S(1)}, f32[1,256,512]{2,1,0:T(8,128)S(1)}, u32[]{:S(2)}, u32[]{:S(2)}) collective-permute-start(f32[1,256,512]{2,1,0:T(8,128)S(1)} %slice_select_fusion.1), channel_id=1, source_target_pairs={{0,2},{1,3},{2,4},{3,5},{4,6},{5,7},{6,8},{7,9},{8,10},{9,11},{10,... | collective-permute-start | bytes 1572872 | tf_op jit(solution)/shard_map/ppermute | solution.py:93

commit v5 on v4

--- a/solution.py
+++ b/solution.py
@@ -13,17 +13,17 @@
     return high, (value - high.astype(jnp.float32)).astype(jnp.bfloat16)
 
 
-def product_kernel(place_ref, left_ref, psi_ref, out_ref, left, psi, stack, result, read, write, *, first, groups):
+def product_kernel(left_ref, psi_ref, out_ref, left, psi, stack, result, read, write, *, place, groups):
     terms, rows, width = left.shape
-    block = place_ref[0]
-    start = pl.multiple_of(place_ref[1] * rows, rows)
+    block, row = place(lax.rem(lax.axis_index("sec"), 2), lax.axis_index("op"))
+    start = pl.multiple_of(row * rows, rows)
     size = terms // groups
     psi_copy = pltpu.make_async_copy(psi_ref.at[block], psi, read.at[0])
     psi_copy.start()
     reads = []
     for group in range(groups):
         span = pl.ds(group * size, size)
-        source = left_ref.at[pl.ds(first + group * size, size), block, pl.ds(start, rows)]
+        source = left_ref.at[pl.ds(group * size, size), block, pl.ds(start, rows)]
         copy = pltpu.make_async_copy(source, left.at[span], read.at[1 + group])
         copy.start()
         reads.append(copy)
@@ -46,16 +46,15 @@
         copy.wait()
 
 
-def product(left_env, psi, block, row, rows, first=0, terms=None, cost=1):
+def product(left_env, psi, place):
     width = psi.shape[-1]
-    terms = terms or left_env.shape[0] - first
-    groups = 2 if terms % 2 == 0 else terms
-    place = jnp.stack([jnp.asarray(block, jnp.int32), jnp.asarray(row, jnp.int32)])
+    rows = width // 2
+    terms = left_env.shape[0]
+    groups = 2 if terms % 2 == 0 else 1
     return pl.pallas_call(
-        functools.partial(product_kernel, first=first, groups=groups),
+        functools.partial(product_kernel, place=place, groups=groups),
         out_shape=jax.ShapeDtypeStruct((terms, rows, width), jnp.float32),
         in_specs=[
-            pl.BlockSpec(memory_space=pltpu.SMEM),
             pl.BlockSpec(memory_space=pltpu.HBM),
             pl.BlockSpec(memory_space=pltpu.HBM),
         ],
@@ -70,9 +69,9 @@
         ],
         compiler_params=pltpu.CompilerParams(vmem_limit_bytes=32 * 2**20),
         cost_estimate=pl.CostEstimate(
-            flops=6 * terms * rows * width * width * cost, bytes_accessed=8 * terms * rows * width, transcendentals=0
+            flops=6 * terms * rows * width * width, bytes_accessed=8 * terms * rows * width, transcendentals=0
         ),
-    )(place, left_env, psi)
+    )(left_env, psi)
 
 
 def contract(first, second):
@@ -82,11 +81,7 @@
 def per_device(psi, left_env, right_env, target):
     count = lax.axis_size("sec")
     me = lax.axis_index("sec")
-    own = lax.axis_index("op")
-    other = 1 - own
     odd = me % 2
-    half = psi.shape[1] // 2
-    terms = left_env.shape[0]
 
     def send(value, step, who=lambda d: True):
         pairs = [(d, (d + step(d)) % count) for d in range(count) if who(d)]
@@ -104,14 +99,14 @@
     slots = [target[((me - j - 1) % count) * 2 + j] % 2 for j in range(2)]
     right = [right_of(slot) for slot in slots]
     left_env, psi = (pltpu.with_memory_space_constraint(a, pltpu.HBM) for a in (left_env, psi))
-    rows_of = functools.partial(product, left_env, psi, rows=half)
+    rows_of = functools.partial(product, left_env, psi)
 
-    value = rows_of(1 - odd, other)
+    value = rows_of(lambda odd, own: (1 - odd, 1 - own))
     first = send(value, lambda d: (d ^ 2) - d if d % 2 else 2)
-    value = rows_of(0, own)
+    value = rows_of(lambda odd, own: (0, own))
     beside = send(value, lambda d: (d ^ 1) - d)
-    value = rows_of(1, jnp.where(odd == 1, other, own))
-    kept = rows_of(odd, jnp.where(odd == 1, own, other))
+    value = rows_of(lambda odd, own: (1, jnp.where(odd == 1, 1 - own, own)))
+    kept = rows_of(lambda odd, own: (odd, jnp.where(odd == 1, own, 1 - own)))
 
     first, value, kept = after(first, value, kept)
     second = send(value, lambda d: 2)

time: 154 us -> 153 us (level)
  waiting for transfers between devices: 88.4 us -> 93.8 us
  starting transfers between devices: 13.1 us -> 8.67 us
  Pallas kernels: 19.5 us -> 17.3 us
    ppermute x6, waiting for transfers between devices: 88.4 us -> 93.2 us  [send(): return lax.ppermute(value, 'sec', pairs)]
    ppermute x6, starting transfers between devices: 12.5 us -> 8.1 us  [send(): return lax.ppermute(value, 'sec', pairs)]
    pallas_call x4, Pallas kernels: 19.5 us -> 17.3 us  [product(): pl.pallas_call(functools.partial(product_kernel, place=place, groups=grou...]
  transfers between devices with their start and end apart: 8 -> 8, of which waited for: 4 -> 5; matrix products, arithmetic and copies ran while one was open for 17% -> 18% of each run, Pallas kernels for 9% -> 8%
where the time goes in v5:
time: 153 us
  waiting for transfers between devices  93.8 us (61%)
  matrix products  18 us (12%)
  Pallas kernels  17.3 us (11%)
  other arithmetic  8.93 us (6%)
  starting transfers between devices  8.67 us (6%)
  between operations  4.01 us (3%)
  local copies, waits for them, and re-layouts  1.96 us (1%)
    ppermute x6, waiting for transfers between devices, send(): return lax.ppermute(value, 'sec', pairs)  93.2 us
    dot_general x4, matrix products, contract(): jnp.einsum('kac,kcd->ad', first, second, precision=lax.Precision.HIGH)  17.4 us
    pallas_call x4, Pallas kernels, product(): pl.pallas_call(functools.partial(product_kernel, place=place, groups=grou...  17.3 us
    ppermute x6, starting transfers between devices, send(): return lax.ppermute(value, 'sec', pairs)  8.1 us
    select_n x1, other arithmetic, per_device(): most = send(jnp.where(odd == 1, kept[:-1], beside[:-1]), lambda d: 2)  3.09 us
  transfers between devices with their start and end apart: 8, of which 5 were waited for; matrix products, arithmetic and copies ran while one was open for 18% of the time, Pallas kernels for 8%

profile of v5, /device:TPU:0, one launch (start us, length us, event | category | flops | bytes accessed | tf_op | source)
XLA Modules:
  0.0 152.7 jit_solution(1961296417444973078)
XLA Ops:
  0.0 4.5 %shard_map.47 = f32[4,256,512]{2,1,0:T(8,128)} custom-call(f32[4,2,512,512]{3,2,1,0:T(8,128)} %left_ref.7, f32[2,512,512]{2,1,0:T(8,128)} %psi_ref.7), custom_call_target="tpu_custom_call" | custom-call | flops 1610612736 | bytes 4194304 | tf_op jit(solution)/shard_map/pallas_call | solution.py:54
  4.6 3.0 %collective-permute-start.1 = (f32[4,256,512]{2,1,0:T(8,128)}, f32[4,256,512]{2,1,0:T(8,128)}, u32[]{:S(2)}, u32[]{:S(2)}) collective-permute-start(f32[4,256,512]{2,1,0:T(8,128)} %shard_map.47), channel_id=1, source_target_pairs={{0,2},{1,3},{2,4},{3,1},{4,6},{5,7},{6,8},{7,5},{8,10},{9,11},{10,... | collective-permute-start | bytes 6291464 | tf_op jit(solution)/shard_map/ppermute | solution.py:88
  7.6 4.5 %shard_map.46 = f32[4,256,512]{2,1,0:T(8,128)} custom-call(f32[4,2,512,512]{3,2,1,0:T(8,128)} %left_ref.7, f32[2,512,512]{2,1,0:T(8,128)} %psi_ref.7), custom_call_target="tpu_custom_call" | custom-call | flops 1610612736 | bytes 4194304 | tf_op jit(solution)/shard_map/pallas_call | solution.py:54
  12.1 1.6 %collective-permute-start = (f32[4,256,512]{2,1,0:T(8,128)}, f32[4,256,512]{2,1,0:T(8,128)}, u32[]{:S(2)}, u32[]{:S(2)}) collective-permute-start(f32[4,256,512]{2,1,0:T(8,128)} %shard_map.46), channel_id=1, source_target_pairs={{0,1},{1,0},{2,3},{3,2},{4,5},{5,4},{6,7},{7,6},{8,9},{9,8},{10,11... | collective-permute-start | bytes 6291464 | tf_op jit(solution)/shard_map/ppermute | solution.py:88
  13.7 4.5 %shard_map.48 = f32[4,256,512]{2,1,0:T(8,128)} custom-call(f32[4,2,512,512]{3,2,1,0:T(8,128)} %left_ref.7, f32[2,512,512]{2,1,0:T(8,128)} %psi_ref.7), custom_call_target="tpu_custom_call" | custom-call | flops 1610612736 | bytes 4194304 | tf_op jit(solution)/shard_map/pallas_call | solution.py:54
  18.2 3.7 %shard_map.49 = f32[4,256,512]{2,1,0:T(8,128)S(1)} custom-call(f32[4,2,512,512]{3,2,1,0:T(8,128)} %left_ref.7, f32[2,512,512]{2,1,0:T(8,128)} %psi_ref.7), custom_call_target="tpu_custom_call" | custom-call | flops 1610612736 | bytes 4194304 | tf_op jit(solution)/shard_map/pallas_call | solution.py:54
  21.9 0.0 copy-start
  21.9 34.6 %collective-permute-done.1 = f32[4,256,512]{2,1,0:T(8,128)} collective-permute-done((f32[4,256,512]{2,1,0:T(8,128)}, f32[4,256,512]{2,1,0:T(8,128)}, u32[]{:S(2)}, u32[]{:S(2)}) %collective-permute-start.1) | collective-permute-done | bytes 2097184 | tf_op jit(solution)/shard_map/ppermute | solution.py:88
  56.6 0.0 collective-permute-start.2
  56.6 1.9 %broadcast_select_fusion = f32[4,256,512]{2,1,0:T(8,128)} fusion(f32[4,256,512]{2,1,0:T(8,128)} %collective-permute-done.1, f32[4,256,512]{2,1,0:T(8,128)S(1)} %shard_map.49, pred[]{:T(512)S(6)} %eq.8), kind=kLoop, calls=%fused_computation.23 | loop fusion | flops 524288 | bytes 6291457 | tf_op jit(solution)/shard_map/jit(_where)/select_n | solution.py:114
  58.5 1.8 %collective-permute-start.3 = (f32[4,256,512]{2,1,0:T(8,128)}, f32[4,256,512]{2,1,0:T(8,128)}, u32[]{:S(2)}, u32[]{:S(2)}) collective-permute-start(f32[4,256,512]{2,1,0:T(8,128)} %broadcast_select_fusion), channel_id=1, source_target_pairs={{0,1},{1,4},{2,3},{3,2},{4,5},{5,8},{6,7},{7,6},{8,9},{9,12},{10,1... | collective-permute-start | bytes 6291464 | tf_op jit(solution)/shard_map/ppermute | solution.py:88
  60.2 0.7 fusion.45
  64.7 0.0 collective-permute-done
  64.7 0.0 slice-start
  64.8 3.1 %slice_select_fusion = f32[3,256,512]{2,1,0:T(8,128)} fusion(f32[4,256,512]{2,1,0:T(8,128)} %collective-permute-done, f32[4,256,512]{2,1,0:T(8,128)S(1)} %shard_map.49, pred[]{:T(512)S(6)} %eq.8), kind=kLoop, calls=%fused_computation.13 | loop fusion | flops 393216 | bytes 4718593 | tf_op jit(solution)/shard_map/jit(_where)/select_n | solution.py:116
  67.8 1.5 collective-permute-start.6
  69.4 2.0 %slice_select_fusion.1 = f32[1,256,512]{2,1,0:T(8,128)} fusion(f32[4,256,512]{2,1,0:T(8,128)} %collective-permute-done, f32[4,256,512]{2,1,0:T(8,128)S(1)} %shard_map.49, pred[]{:T(512)S(6)} %eq.8), kind=kLoop, calls=%fused_computation.26 | loop fusion | flops 131072 | bytes 1572865 | tf_op jit(solution)/shard_map/jit(_where)/select_n | solution.py:120
  71.3 36.8 %collective-permute-done.2 = f32[4,256,512]{2,1,0:T(8,128)} collective-permute-done((f32[4,256,512]{2,1,0:T(8,128)}, f32[4,256,512]{2,1,0:T(8,128)}, u32[]{:S(2)}, u32[]{:S(2)}) %collective-permute-start.2) | collective-permute-done | bytes 2097184 | tf_op jit(solution)/shard_map/ppermute | solution.py:88
  108.1 4.8 %fusion.21 = f32[256,512]{1,0:T(8,128)S(1)} fusion(f32[4,2,512,512]{3,2,1,0:T(8,128)} %param.6, s32[]{:T(128)S(6)} %select_n.107, f32[4,256,512]{2,1,0:T(8,128)} %collective-permute-done.2, f32[4,256,512]{2,1,0:T(8,128)} %collective-permute-done.1, pred[]{:T(512)S(6)} %eq.8), kind=kOutput, calls=%fused_computation.17 | convolution fusion | flops 1611137024 | bytes 8912901 | tf_op jit(solution)/shard_map/kac,kcd->ad/dot_general | solution.py:78
  113.0 3.9 %fusion.12 = f32[256,512]{1,0:T(8,128)S(1)} fusion(f32[4,256,512]{2,1,0:T(8,128)} %collective-permute-done.3, f32[4,2,512,512]{3,2,1,0:T(8,128)S(1)} %bitcast.60, s32[]{:T(128)S(6)} %select_n.109), kind=kOutput, calls=%fused_computation.14 | convolution fusion | flops 1610612736 | bytes 6815748 | tf_op jit(solution)/shard_map/kac,kcd->ad/dot_general | solution.py:78
  116.9 0.1 collective-permute-start.4
  117.0 0.5 collective-permute-start.5
  117.5 1.3 dynamic-slice_bitcast_fusion.6
  118.8 0.2 collective-permute-start.7
  119.0 0.6 collective-permute-done.5
  119.6 4.8 %fusion.31 = f32[1,256,512]{2,1,0:T(8,128)S(1)} fusion(f32[4,2,512,512]{3,2,1,0:T(8,128)} %param.6, s32[]{:T(128)S(6)} %select_n.104, f32[4,256,512]{2,1,0:T(8,128)} %collective-permute-done, f32[4,256,512]{2,1,0:T(8,128)} %collective-permute-done.2, pred[]{:T(512)S(6)} %eq.8, f32[256,512]{1,0:T(8,128)S(1)} %collective-permute-done.4, ...), kind=kOutput, calls=%fused_computation.19 | convolution fusion | flops 1611399168 | bytes 9963008 | tf_op jit(solution)/shard_map/kac,kcd->ad/dot_general | solution.py:78
  124.5 1.1 pad_maximum_fusion
  125.6 16.3 %collective-permute-done.6 = f32[3,256,512]{2,1,0:T(8,128)} collective-permute-done((f32[3,256,512]{2,1,0:T(8,128)}, f32[3,256,512]{2,1,0:T(8,128)}, u32[]{:S(2)}, u32[]{:S(2)}) %collective-permute-start.6) | collective-permute-done | bytes 1572896 | tf_op jit(solution)/shard_map/ppermute | solution.py:88
  141.9 3.9 %fusion.36 = f32[256,512]{1,0:T(8,128)S(1)} fusion(f32[3,256,512]{2,1,0:T(8,128)} %collective-permute-done.6, f32[4,2,512,512]{3,2,1,0:T(8,128)} %param.6, s32[]{:T(128)S(6)} %select_n.116, f32[256,512]{1,0:T(8,128)S(1)} %collective-permute-done.5, f32[256,512]{1,0:T(8,128)S(1)} %collective-permute-done.4, pred[]{:T(512)S(6)} %eq.8), kind=kOutput, calls=%fused_computation.20 | convolution fusion | flops 1208221696 | bytes 6291461 | tf_op jit(solution)/shard_map/kac,kcd->ad/dot_general | solution.py:78
  145.8 5.5 %collective-permute-done.7 = f32[1,256,512]{2,1,0:T(8,128)S(1)} collective-permute-done((f32[1,256,512]{2,1,0:T(8,128)}, f32[1,256,512]{2,1,0:T(8,128)S(1)}, u32[]{:S(2)}, u32[]{:S(2)}) %collective-permute-start.7) | collective-permute-done | bytes 524320 | tf_op jit(solution)/shard_map/ppermute | solution.py:88
  151.2 0.6 fusion.39
  151.9 0.9 bitcast_dynamic-update-slice_fusion
  (7 shorter events, 0.0 us)
Async XLA Ops:
  4.6 52.0 %collective-permute-start.1 = (f32[4,256,512]{2,1,0:T(8,128)}, f32[4,256,512]{2,1,0:T(8,128)}, u32[]{:S(2)}, u32[]{:S(2)}) collective-permute-start(f32[4,256,512]{2,1,0:T(8,128)} %shard_map.47), channel_id=1, source_target_pairs={{0,2},{1,3},{2,4},{3,1},{4,6},{5,7},{6,8},{7,5},{8,10},{9,11},{10,... | collective-permute-start | bytes 6291464 | tf_op jit(solution)/shard_map/ppermute | solution.py:88
  12.1 52.6 %collective-permute-start = (f32[4,256,512]{2,1,0:T(8,128)}, f32[4,256,512]{2,1,0:T(8,128)}, u32[]{:S(2)}, u32[]{:S(2)}) collective-permute-start(f32[4,256,512]{2,1,0:T(8,128)} %shard_map.46), channel_id=1, source_target_pairs={{0,1},{1,0},{2,3},{3,2},{4,5},{5,4},{6,7},{7,6},{8,9},{9,8},{10,11... | collective-permute-start | bytes 6291464 | tf_op jit(solution)/shard_map/ppermute | solution.py:88
  21.9 38.3 %copy-start = (s32[32]{0:T(128)S(1)}, s32[32]{0:T(128)}, u32[]{:S(2)}) copy-start(s32[32]{0:T(128)} %param.7) | copy-start | bytes 388
  56.6 51.6 %collective-permute-start.2 = (f32[4,256,512]{2,1,0:T(8,128)}, f32[4,256,512]{2,1,0:T(8,128)}, u32[]{:S(2)}, u32[]{:S(2)}) collective-permute-start(f32[4,256,512]{2,1,0:T(8,128)} %shard_map.48), channel_id=1, source_target_pairs={{0,2},{1,3},{2,4},{3,5},{4,6},{5,7},{6,8},{7,9},{8,10},{9,11},{10,... | collective-permute-start | bytes 6291464 | tf_op jit(solution)/shard_map/ppermute | solution.py:88
  58.5 54.5 %collective-permute-start.3 = (f32[4,256,512]{2,1,0:T(8,128)}, f32[4,256,512]{2,1,0:T(8,128)}, u32[]{:S(2)}, u32[]{:S(2)}) collective-permute-start(f32[4,256,512]{2,1,0:T(8,128)} %broadcast_select_fusion), channel_id=1, source_target_pairs={{0,1},{1,4},{2,3},{3,2},{4,5},{5,8},{6,7},{7,6},{8,9},{9,12},{10,1... | collective-permute-start | bytes 6291464 | tf_op jit(solution)/shard_map/ppermute | solution.py:88
  64.7 48.2 %slice-start = ((s8[8388608]{0:T(1024)(128)(4,1)}), s8[4194304]{0:T(1024)(128)(4,1)S(1)}, s32[]{:S(2)}) async-start(s8[8388608]{0:T(1024)(128)(4,1)} %bitcast.59), calls=%async_computation | async-start | bytes 8388608
  67.8 74.0 %collective-permute-start.6 = (f32[3,256,512]{2,1,0:T(8,128)}, f32[3,256,512]{2,1,0:T(8,128)}, u32[]{:S(2)}, u32[]{:S(2)}) collective-permute-start(f32[3,256,512]{2,1,0:T(8,128)} %slice_select_fusion), channel_id=1, source_target_pairs={{0,2},{1,3},{2,4},{3,5},{4,6},{5,7},{6,8},{7,9},{8,10},{9,11},{10,... | collective-permute-start | bytes 4718600 | tf_op jit(solution)/shard_map/ppermute | solution.py:88
  71.3 41.7 %slice-start.1 = ((s8[8388608]{0:T(1024)(128)(4,1)}), s8[4194304]{0:T(1024)(128)(4,1)S(1)}, s32[]{:S(2)}) async-start(s8[8388608]{0:T(1024)(128)(4,1)} %bitcast.59), calls=%async_computation.1 | async-start | bytes 8388608
  116.9 2.1 %collective-permute-start.4 = (f32[256,512]{1,0:T(8,128)S(1)}, f32[256,512]{1,0:T(8,128)S(1)}, u32[]{:S(2)}, u32[]{:S(2)}) collective-permute-start(f32[256,512]{1,0:T(8,128)S(1)} %fusion.12), channel_id=1, source_target_pairs={{0,16},{16,0},{1,17},{17,1},{2,18},{18,2},{3,19},{19,3},{4,20},{20... | collective-permute-start | bytes 1572872 | tf_op jit(solution)/shard_map/ppermute | solution.py:91
  117.0 2.6 %collective-permute-start.5 = (f32[256,512]{1,0:T(8,128)S(1)}, f32[256,512]{1,0:T(8,128)S(1)}, u32[]{:S(2)}, u32[]{:S(2)}) collective-permute-start(f32[256,512]{1,0:T(8,128)S(1)} %fusion.21), channel_id=1, source_target_pairs={{0,16},{16,0},{1,17},{17,1},{2,18},{18,2},{3,19},{19,3},{4,20},{20... | collective-permute-start | bytes 1572872 | tf_op jit(solution)/shard_map/ppermute | solution.py:91
  118.8 32.5 %collective-permute-start.7 = (f32[1,256,512]{2,1,0:T(8,128)}, f32[1,256,512]{2,1,0:T(8,128)S(1)}, u32[]{:S(2)}, u32[]{:S(2)}) collective-permute-start(f32[1,256,512]{2,1,0:T(8,128)} %slice_select_fusion.1), channel_id=1, source_target_pairs={{0,2},{1,3},{2,4},{3,5},{4,6},{5,7},{6,8},{7,9},{8,10},{9,11},{10,... | collective-permute-start | bytes 1572872 | tf_op jit(solution)/shard_map/ppermute | solution.py:88

commit v6 on v5

v6 whole, which is shorter than its diff:
```python
import functools

import jax
import jax.numpy as jnp
from jax import lax
from jax.experimental import pallas as pl
from jax.experimental.pallas import tpu as pltpu
from jax.sharding import PartitionSpec as P


def split(value):
    high = value.astype(jnp.bfloat16)
    return high, (value - high.astype(jnp.float32)).astype(jnp.bfloat16)


def product_kernel(left_ref, psi_ref, *refs, place, first, groups):
    count = sum(1 for _, _, fresh in groups if fresh)
    outs = refs[:count]
    left, psi, stack, result, read, write = refs[count:]
    _, rows, width = left.shape
    block, row = place(lax.rem(lax.axis_index("sec"), 2), lax.axis_index("op"))
    start = pl.multiple_of(row * rows, rows)
    psi_copy = pltpu.make_async_copy(psi_ref.at[block], psi, read.at[0])
    psi_copy.start()
    reads = []
    for index, (at, size, _) in enumerate(groups):
        source = left_ref.at[pl.ds(first + at, size), block, pl.ds(start, rows)]
        copy = pltpu.make_async_copy(source, left.at[pl.ds(at, size)], read.at[1 + index])
        copy.start()
        reads.append(copy)
    psi_copy.wait()
    high, low = split(psi[...])
    stack[:width] = high
    stack[width : 2 * width] = high
    stack[2 * width :] = low
    writes = []
    out, base = -1, 0
    for index, (at, size, fresh) in enumerate(groups):
        if fresh:
            out, base = out + 1, at
        reads[index].wait()
        high, low = split(left[at : at + size].reshape(size * rows, width))
        value = jnp.dot(jnp.concatenate([high, low, high], axis=1), stack[...], preferred_element_type=jnp.float32)
        result[at : at + size] = value.reshape(size, rows, width)
        target = outs[out].at[pl.ds(at - base, size)]
        copy = pltpu.make_async_copy(result.at[pl.ds(at, size)], target, write.at[index])
        copy.start()
        writes.append(copy)
    for copy in writes:
        copy.wait()


def product(left_env, psi, place, first=0, parts=None, cost=1):
    width = psi.shape[-1]
    rows = width // 2
    parts = parts or (left_env.shape[0] - first,)
    terms = sum(parts)
    groups, at = [], 0
    for part in parts:
        for size, fresh in ((part - part // 2, True), (part // 2, False)):
            if size:
                groups.append((at, size, fresh))
                at += size
    return pl.pallas_call(
        functools.partial(product_kernel, place=place, first=first, groups=groups),
        out_shape=[jax.ShapeDtypeStruct((part, rows, width), jnp.float32) for part in parts],
        in_specs=[pl.BlockSpec(memory_space=pltpu.HBM)] * 2,
        out_specs=[pl.BlockSpec(memory_space=pl.ANY)] * len(parts),
        scratch_shapes=[
            pltpu.VMEM((terms, rows, width), jnp.float32),
            pltpu.VMEM((width, width), jnp.float32),
            pltpu.VMEM((3 * width, width), jnp.bfloat16),
            pltpu.VMEM((terms, rows, width), jnp.float32),
            pltpu.SemaphoreType.DMA((1 + len(groups),)),
            pltpu.SemaphoreType.DMA((len(groups),)),
        ],
        compiler_params=pltpu.CompilerParams(vmem_limit_bytes=32 * 2**20),
        cost_estimate=pl.CostEstimate(
            flops=6 * terms * rows * width * width * cost, bytes_accessed=8 * terms * rows * width, transcendentals=0
        ),
    )(left_env, psi)


def contract(first, second):
    return jnp.einsum("kac,kcd->ad", first, second, precision=lax.Precision.HIGH)


def per_device(psi, left_env, right_env, target):
    count = lax.axis_size("sec")
    me = lax.axis_index("sec")
    odd = me % 2

    def send(value, step, who=lambda d: True):
        pairs = [(d, (d + step(d)) % count) for d in range(count) if who(d)]
        return lax.ppermute(value, "sec", pairs)

    def exchange(value):
        return lax.ppermute(value, "op", [(0, 1), (1, 0)])

    def after(*values):
        return lax.optimization_barrier(values)

    def right_of(slot):
        return lax.dynamic_index_in_dim(right_env, slot, 1, keepdims=False)

    slots = [target[((me - j - 1) % count) * 2 + j] % 2 for j in range(2)]
    right = [right_of(slot) for slot in slots]
    left_env, psi = (pltpu.with_memory_space_constraint(a, pltpu.HBM) for a in (left_env, psi))
    rows_of = functools.partial(product, left_env, psi)

    terms = left_env.shape[0]
    (value,) = rows_of(lambda odd, own: (1 - odd, 1 - own), parts=(1,))
    ahead = send(value, lambda d: (d ^ 2) - d if d % 2 else 2)
    near, near_last = rows_of(lambda odd, own: (0, own), parts=(terms - 1, 1))
    beside = send(near, lambda d: (d ^ 1) - d)
    (value,) = rows_of(lambda odd, own: (1 - odd, 1 - own), first=1)
    first = send(value, lambda d: (d ^ 2) - d if d % 2 else 2)
    ahead, psi = after(ahead, psi)
    (value,) = product(left_env, psi, lambda odd, own: (1, jnp.where(odd == 1, 1 - own, own)), cost=100)
    beside, psi = after(beside, psi)
    kept, kept_last = product(
        left_env, psi, lambda odd, own: (odd, jnp.where(odd == 1, own, 1 - own)), parts=(terms - 1, 1), cost=100
    )

    first, value, kept, kept_last, near_last = after(first, value, kept, kept_last, near_last)
    second = send(value, lambda d: 2)
    first = jnp.concatenate([ahead, first])
    beside_last = send(near_last, lambda d: (d ^ 1) - d)
    relayed = send(
        jnp.where(odd == 1, first, jnp.concatenate([kept, kept_last])),
        lambda d: 1 if d % 2 == 0 else (-1 if d % 4 == 3 else 3),
    )
    most = send(jnp.where(odd == 1, kept, beside), lambda d: 2)
    others_1 = contract(jnp.where(odd == 1, second, first), right[1])
    others_1, relayed = after(others_1, relayed)
    others_0 = contract(relayed, right[0])
    others_0, last = after(others_0, jnp.where(odd == 1, kept_last, beside_last))
    last = send(last, lambda d: 2)

    beside = jnp.concatenate([beside, beside_last])
    early = contract(jnp.where(odd == 1, beside, second), right_of(jnp.where(odd == 1, *slots)))
    late_slot = jnp.where(odd == 1, slots[1], slots[0])
    late_right = right_of(late_slot)
    swapped = [exchange(others_0), exchange(others_1)]
    early = early + jnp.where(odd == 1, *swapped)
    late = contract(most, late_right[:-1]) + jnp.where(odd == 1, swapped[1], swapped[0])
    out, late, late_right = after(jnp.stack([early, early]), late, late_right[-1])
    final = late + jnp.dot(last[0], late_right, precision=lax.Precision.HIGH)
    return lax.dynamic_update_index_in_dim(out, final, late_slot, 0)


def solution(mesh):
    return jax.shard_map(
        per_device,
        mesh=mesh,
        in_specs=(
            P("sec", None, None),
            P("op", "sec", None, None),
            P("op", "sec", None, None),
            P(),
        ),
        out_specs=P("sec", "op", None),
        check_vma=False,
    )
```

time: 153 us -> 150 us (0.980)
  waiting for transfers between devices: 93.8 us -> 83.4 us
  local copies, waits for them, and re-layouts: 1.96 us -> 5.32 us
  starting transfers between devices: 8.67 us -> 11.5 us
    ppermute x6 -> x8, waiting for transfers between devices: 93.2 us -> 83.2 us  [send(): return lax.ppermute(value, 'sec', pairs)]
    ppermute x6 -> x8, starting transfers between devices: 8.1 us -> 11 us  [send(): return lax.ppermute(value, 'sec', pairs)]
    unnamed x6 -> x15, local copies, waits for them, and re-layouts: 0.02 us -> 1.91 us
    pallas_call x4 -> x5, Pallas kernels: 17.3 us -> 18.6 us  [product(): pl.pallas_call(functools.partial(product_kernel, place=place, first=first...]
  transfers between devices with their start and end apart: 8 -> 10, of which waited for: 5 -> 6; matrix products, arithmetic and copies ran while one was open for 18% -> 21% of each run, Pallas kernels for 8% -> 11%
where the time goes in v6:
time: 150 us
  waiting for transfers between devices  83.4 us (56%)
  matrix products  18.9 us (13%)
  Pallas kernels  18.6 us (12%)
  starting transfers between devices  11.5 us (8%)
  other arithmetic  8.14 us (5%)
  local copies, waits for them, and re-layouts  5.32 us (4%)
  between operations  4 us (3%)
    ppermute x8, waiting for transfers between devices, send(): return lax.ppermute(value, 'sec', pairs)  83.2 us
    pallas_call x5, Pallas kernels, product(): pl.pallas_call(functools.partial(product_kernel, place=place, first=first...  18.6 us
    dot_general x4, matrix products, contract(): jnp.einsum('kac,kcd->ad', first, second, precision=lax.Precision.HIGH)  18.3 us
    ppermute x8, starting transfers between devices, send(): return lax.ppermute(value, 'sec', pairs)  11 us
    select_n x1, other arithmetic, per_device(): most = send(jnp.where(odd == 1, kept, beside), lambda d: 2)  3.17 us
  transfers between devices with their start and end apart: 10, of which 6 were waited for; matrix products, arithmetic and copies ran while one was open for 21% of the time, Pallas kernels for 11%

profile of v6, /device:TPU:0, one launch (start us, length us, event | category | flops | bytes accessed | tf_op | source)
XLA Modules:
  0.0 150.0 jit_solution(371873499666499447)
XLA Ops:
  0.0 2.0 %shard_map.47 = f32[1,256,512]{2,1,0:T(8,128)S(1)} custom-call(f32[4,2,512,512]{3,2,1,0:T(8,128)} %left_ref.9, f32[2,512,512]{2,1,0:T(8,128)} %psi_ref.7), custom_call_target="tpu_custom_call" | custom-call | flops 402653184 | bytes 1048576 | tf_op jit(solution)/shard_map/pallas_call | solution.py:64
  2.0 3.0 %collective-permute-start.1 = (f32[1,256,512]{2,1,0:T(8,128)S(1)}, f32[1,256,512]{2,1,0:T(8,128)S(1)}, u32[]{:S(2)}, u32[]{:S(2)}) collective-permute-start(f32[1,256,512]{2,1,0:T(8,128)S(1)} %shard_map.47), channel_id=1, source_target_pairs={{0,2},{1,3},{2,4},{3,1},{4,6},{5,7},{6,8},{7,5},{8,10},{9,11},{10,... | collective-permute-start | bytes 1572872 | tf_op jit(solution)/shard_map/ppermute | solution.py:95
  5.0 3.9 %shard_map.48 = f32[3,256,512]{2,1,0:T(8,128)} custom-call(f32[4,2,512,512]{3,2,1,0:T(8,128)} %left_ref.9, f32[2,512,512]{2,1,0:T(8,128)} %psi_ref.7), custom_call_target="tpu_custom_call" | custom-call | flops 1207959552 | bytes 3145728 | tf_op jit(solution)/shard_map/pallas_call | solution.py:64
  9.0 1.6 %collective-permute-start.2 = (f32[3,256,512]{2,1,0:T(8,128)}, f32[3,256,512]{2,1,0:T(8,128)}, u32[]{:S(2)}, u32[]{:S(2)}) collective-permute-start(f32[3,256,512]{2,1,0:T(8,128)} %shard_map.48), channel_id=1, source_target_pairs={{0,2},{1,3},{2,4},{3,1},{4,6},{5,7},{6,8},{7,5},{8,10},{9,11},{10,... | collective-permute-start | bytes 4718600 | tf_op jit(solution)/shard_map/ppermute | solution.py:95
  10.5 4.0 %shard_map.46 = (f32[3,256,512]{2,1,0:T(8,128)}, f32[1,256,512]{2,1,0:T(8,128)S(1)}) custom-call(f32[4,2,512,512]{3,2,1,0:T(8,128)} %left_ref.9, f32[2,512,512]{2,1,0:T(8,128)} %psi_ref.7), custom_call_target="tpu_custom_call" | custom-call | flops 1610612736 | bytes 4194304 | tf_op jit(solution)/shard_map/pallas_call | solution.py:64
  14.5 0.5 collective-permute-start
  15.1 5.8 %collective-permute-done.1 = f32[1,256,512]{2,1,0:T(8,128)S(1)} collective-permute-done((f32[1,256,512]{2,1,0:T(8,128)S(1)}, f32[1,256,512]{2,1,0:T(8,128)S(1)}, u32[]{:S(2)}, u32[]{:S(2)}) %collective-permute-start.1) | collective-permute-done | bytes 524320 | tf_op jit(solution)/shard_map/ppermute | solution.py:95
  20.8 4.7 %shard_map.49 = f32[4,256,512]{2,1,0:T(8,128)} custom-call(f32[4,2,512,512]{3,2,1,0:T(8,128)} %left_ref.9, f32[2,512,512]{2,1,0:T(8,128)} %psi_ref.7), custom_call_target="tpu_custom_call" | custom-call | flops 161061273600 | bytes 4194304 | tf_op jit(solution)/shard_map/pallas_call | solution.py:64
  25.6 1.9 %constant_dynamic-update-slice_fusion.1 = f32[4,256,512]{2,1,0:T(8,128)} fusion(f32[1,256,512]{2,1,0:T(8,128)} %copy-done.3), kind=kLoop, calls=%fused_computation.33 | loop fusion | bytes 1048576
  27.4 23.0 %collective-permute-done = f32[3,256,512]{2,1,0:T(8,128)} collective-permute-done((f32[3,256,512]{2,1,0:T(8,128)}, f32[3,256,512]{2,1,0:T(8,128)}, u32[]{:S(2)}, u32[]{:S(2)}) %collective-permute-start) | collective-permute-done | bytes 1572896 | tf_op jit(solution)/shard_map/ppermute | solution.py:95
  50.5 4.0 %shard_map.50 = (f32[3,256,512]{2,1,0:T(8,128)S(1)}, f32[1,256,512]{2,1,0:T(8,128)S(1)}) custom-call(f32[4,2,512,512]{3,2,1,0:T(8,128)} %left_ref.9, f32[2,512,512]{2,1,0:T(8,128)} %psi_ref.7), custom_call_target="tpu_custom_call" | custom-call | flops 161061273600 | bytes 4194304 | tf_op jit(solution)/shard_map/pallas_call | solution.py:64
  54.5 1.6 %collective-permute-start.4 = (f32[4,256,512]{2,1,0:T(8,128)}, f32[4,256,512]{2,1,0:T(8,128)}, u32[]{:S(2)}, u32[]{:S(2)}) collective-permute-start(f32[4,256,512]{2,1,0:T(8,128)} %shard_map.49), channel_id=1, source_target_pairs={{0,2},{1,3},{2,4},{3,5},{4,6},{5,7},{6,8},{7,9},{8,10},{9,11},{10,... | collective-permute-start | bytes 6291464 | tf_op jit(solution)/shard_map/ppermute | solution.py:95
  56.1 1.5 %constant_dynamic-update-slice_fusion = f32[4,256,512]{2,1,0:T(8,128)S(1)} fusion(f32[4,256,512]{2,1,0:T(8,128)S(1)} %copy-done, f32[3,256,512]{2,1,0:T(8,128)} %collective-permute-done.2), kind=kLoop, calls=%fused_computation.32 | loop fusion | bytes 3145728 | tf_op jit(solution)/shard_map/concatenate | solution.py:127
  57.7 2.1 %maximum_select_fusion.2 = f32[4,256,512]{2,1,0:T(8,128)} fusion(f32[4,256,512]{2,1,0:T(8,128)S(1)} %constant_dynamic-update-slice_fusion, f32[1,256,512]{2,1,0:T(8,128)S(1)} %get-tuple-element.37, f32[3,256,512]{2,1,0:T(8,128)S(1)} %get-tuple-element.36, pred[]{:T(512)S(6)} %eq.8), kind=kLoop, calls=%fused_computation.14 | loop fusion | flops 1048576 | bytes 6291457 | tf_op jit(solution)/shard_map/jit(_where)/select_n | solution.py:130
  60.3 2.6 %collective-permute-start.3 = (f32[1,256,512]{2,1,0:T(8,128)S(1)}, f32[1,256,512]{2,1,0:T(8,128)S(1)}, u32[]{:S(2)}, u32[]{:S(2)}) collective-permute-start(f32[1,256,512]{2,1,0:T(8,128)S(1)} %get-tuple-element.32), channel_id=1, source_target_pairs={{0,1},{1,0},{2,3},{3,2},{4,5},{5,4},{6,7},{7,6},{8,9},{9,8},{10,11... | collective-permute-start | bytes 1572872 | tf_op jit(solution)/shard_map/ppermute | solution.py:95
  62.8 0.6 fusion.41
  67.3 3.2 %broadcast_select_fusion = f32[3,256,512]{2,1,0:T(8,128)} fusion(f32[3,256,512]{2,1,0:T(8,128)S(1)} %get-tuple-element.36, f32[3,256,512]{2,1,0:T(8,128)} %collective-permute-done, pred[]{:T(512)S(6)} %eq.8), kind=kLoop, calls=%fused_computation.27 | loop fusion | flops 393216 | bytes 4718593 | tf_op jit(solution)/shard_map/jit(_where)/select_n | solution.py:133
  70.4 0.5 collective-permute-start.8
  70.9 46.7 %collective-permute-done.3 = f32[1,256,512]{2,1,0:T(8,128)S(1)} collective-permute-done((f32[1,256,512]{2,1,0:T(8,128)S(1)}, f32[1,256,512]{2,1,0:T(8,128)S(1)}, u32[]{:S(2)}, u32[]{:S(2)}) %collective-permute-start.3) | collective-permute-done | bytes 524320 | tf_op jit(solution)/shard_map/ppermute | solution.py:95
  117.6 0.9 broadcast_select_fusion.1
  118.5 4.4 %fusion.20 = f32[256,512]{1,0:T(8,128)S(1)} fusion(f32[4,2,512,512]{3,2,1,0:T(8,128)} %param.6, s32[]{:T(128)S(6)} %select_n.107, f32[4,256,512]{2,1,0:T(8,128)} %collective-permute-done.4, f32[4,256,512]{2,1,0:T(8,128)S(1)} %copy-done.2, pred[]{:T(512)S(6)} %eq.8), kind=kOutput, calls=%fused_computation.19 | convolution fusion | flops 1611137024 | bytes 8912901 | tf_op jit(solution)/shard_map/kac,kcd->ad/dot_general | solution.py:85
  123.0 4.7 %fusion.16 = f32[256,512]{1,0:T(8,128)} fusion(f32[4,256,512]{2,1,0:T(8,128)} %collective-permute-done.5, f32[4,2,512,512]{3,2,1,0:T(8,128)S(1)} %bitcast.60, s32[]{:T(128)S(6)} %select_n.109), kind=kOutput, calls=%fused_computation.17 | convolution fusion | flops 1610612736 | bytes 6815748 | tf_op jit(solution)/shard_map/kac,kcd->ad/dot_general | solution.py:85
  127.7 0.5 collective-permute-start.7
  128.2 1.3 dynamic-slice_bitcast_fusion.6
  129.5 0.7 collective-permute-start.9
  130.5 5.3 %fusion.28 = f32[1,256,512]{2,1,0:T(8,128)S(1)} fusion(f32[4,2,512,512]{3,2,1,0:T(8,128)} %param.6, s32[]{:T(128)S(6)} %select_n.104, f32[4,256,512]{2,1,0:T(8,128)} %collective-permute-done.4, f32[1,256,512]{2,1,0:T(8,128)S(1)} %collective-permute-done.3, f32[3,256,512]{2,1,0:T(8,128)} %collective-permute-done, pred[]{:T(512)S(6)} %eq.8, ...), kind=kOutput, calls=%fused_computation.21 | convolution fusion | flops 1611923456 | bytes 9963008 | tf_op jit(solution)/shard_map/kac,kcd->ad/dot_general | solution.py:85
  135.8 1.1 pad_maximum_fusion
  136.9 2.6 %collective-permute-done.8 = f32[3,256,512]{2,1,0:T(8,128)} collective-permute-done((f32[3,256,512]{2,1,0:T(8,128)}, f32[3,256,512]{2,1,0:T(8,128)}, u32[]{:S(2)}, u32[]{:S(2)}) %collective-permute-start.8) | collective-permute-done | bytes 1572896 | tf_op jit(solution)/shard_map/ppermute | solution.py:95
  139.5 3.9 %fusion.31 = f32[256,512]{1,0:T(8,128)S(1)} fusion(f32[3,256,512]{2,1,0:T(8,128)} %collective-permute-done.8, f32[4,2,512,512]{3,2,1,0:T(8,128)} %param.6, s32[]{:T(128)S(6)} %select_n.116, f32[256,512]{1,0:T(8,128)S(1)} %collective-permute-done.7, f32[256,512]{1,0:T(8,128)S(1)} %collective-permute-done.6, pred[]{:T(512)S(6)} %eq.8), kind=kOutput, calls=%fused_computation.22 | convolution fusion | flops 1208221696 | bytes 6291461 | tf_op jit(solution)/shard_map/kac,kcd->ad/dot_general | solution.py:85
  143.4 5.1 %collective-permute-done.9 = f32[1,256,512]{2,1,0:T(8,128)S(1)} collective-permute-done((f32[1,256,512]{2,1,0:T(8,128)}, f32[1,256,512]{2,1,0:T(8,128)S(1)}, u32[]{:S(2)}, u32[]{:S(2)}) %collective-permute-start.9) | collective-permute-done | bytes 524320 | tf_op jit(solution)/shard_map/ppermute | solution.py:95
  148.5 0.6 fusion.34
  149.1 0.9 bitcast_dynamic-update-slice_fusion
  (22 shorter events, 0.8 us)
Async XLA Ops:
  2.0 18.8 %collective-permute-start.1 = (f32[1,256,512]{2,1,0:T(8,128)S(1)}, f32[1,256,512]{2,1,0:T(8,128)S(1)}, u32[]{:S(2)}, u32[]{:S(2)}) collective-permute-start(f32[1,256,512]{2,1,0:T(8,128)S(1)} %shard_map.47), channel_id=1, source_target_pairs={{0,2},{1,3},{2,4},{3,1},{4,6},{5,7},{6,8},{7,5},{8,10},{9,11},{10,... | collective-permute-start | bytes 1572872 | tf_op jit(solution)/shard_map/ppermute | solution.py:95
  9.0 45.5 %collective-permute-start.2 = (f32[3,256,512]{2,1,0:T(8,128)}, f32[3,256,512]{2,1,0:T(8,128)}, u32[]{:S(2)}, u32[]{:S(2)}) collective-permute-start(f32[3,256,512]{2,1,0:T(8,128)} %shard_map.48), channel_id=1, source_target_pairs={{0,2},{1,3},{2,4},{3,1},{4,6},{5,7},{6,8},{7,5},{8,10},{9,11},{10,... | collective-permute-start | bytes 4718600 | tf_op jit(solution)/shard_map/ppermute | solution.py:95
  14.5 36.0 %collective-permute-start = (f32[3,256,512]{2,1,0:T(8,128)}, f32[3,256,512]{2,1,0:T(8,128)}, u32[]{:S(2)}, u32[]{:S(2)}) collective-permute-start(f32[3,256,512]{2,1,0:T(8,128)} %get-tuple-element.25), channel_id=1, source_target_pairs={{0,1},{1,0},{2,3},{3,2},{4,5},{5,4},{6,7},{7,6},{8,9},{9,8},{10,11... | collective-permute-start | bytes 4718600 | tf_op jit(solution)/shard_map/ppermute | solution.py:95
  20.8 4.7 %copy-start.3 = (f32[1,256,512]{2,1,0:T(8,128)}, f32[1,256,512]{2,1,0:T(8,128)S(1)}, u32[]{:S(2)}) copy-start(f32[1,256,512]{2,1,0:T(8,128)S(1)} %collective-permute-done.1) | copy-start | bytes 1572868
  50.5 5.6 %copy-start = (f32[4,256,512]{2,1,0:T(8,128)S(1)}, f32[4,256,512]{2,1,0:T(8,128)}, u32[]{:S(2)}) copy-start(f32[4,256,512]{2,1,0:T(8,128)} %constant_dynamic-update-slice_fusion.1) | copy-start | bytes 6291460
  54.5 64.0 %collective-permute-start.4 = (f32[4,256,512]{2,1,0:T(8,128)}, f32[4,256,512]{2,1,0:T(8,128)}, u32[]{:S(2)}, u32[]{:S(2)}) collective-permute-start(f32[4,256,512]{2,1,0:T(8,128)} %shard_map.49), channel_id=1, source_target_pairs={{0,2},{1,3},{2,4},{3,5},{4,6},{5,7},{6,8},{7,9},{8,10},{9,11},{10,... | collective-permute-start | bytes 6291464 | tf_op jit(solution)/shard_map/ppermute | solution.py:95
  57.6 2.1 %copy-start.1 = (f32[4,256,512]{2,1,0:T(8,128)}, f32[4,256,512]{2,1,0:T(8,128)S(1)}, u32[]{:S(2)}) copy-start(f32[4,256,512]{2,1,0:T(8,128)S(1)} %constant_dynamic-update-slice_fusion) | copy-start | bytes 6291460
  57.6 5.2 %copy-start.4 = (s32[32]{0:T(128)S(1)}, s32[32]{0:T(128)}, u32[]{:S(2)}) copy-start(s32[32]{0:T(128)} %param.7) | copy-start | bytes 388
  59.8 63.2 %collective-permute-start.5 = (f32[4,256,512]{2,1,0:T(8,128)}, f32[4,256,512]{2,1,0:T(8,128)}, u32[]{:S(2)}, u32[]{:S(2)}) collective-permute-start(f32[4,256,512]{2,1,0:T(8,128)} %maximum_select_fusion.2), channel_id=1, source_target_pairs={{0,1},{1,4},{2,3},{3,2},{4,5},{5,8},{6,7},{7,6},{8,9},{9,12},{10,1... | collective-permute-start | bytes 6291464 | tf_op jit(solution)/shard_map/ppermute | solution.py:95
  60.3 57.4 %collective-permute-start.3 = (f32[1,256,512]{2,1,0:T(8,128)S(1)}, f32[1,256,512]{2,1,0:T(8,128)S(1)}, u32[]{:S(2)}, u32[]{:S(2)}) collective-permute-start(f32[1,256,512]{2,1,0:T(8,128)S(1)} %get-tuple-element.32), channel_id=1, source_target_pairs={{0,1},{1,0},{2,3},{3,2},{4,5},{5,4},{6,7},{7,6},{8,9},{9,8},{10,11... | collective-permute-start | bytes 1572872 | tf_op jit(solution)/shard_map/ppermute | solution.py:95
  67.2 51.3 %copy-start.2 = (f32[4,256,512]{2,1,0:T(8,128)S(1)}, f32[4,256,512]{2,1,0:T(8,128)}, u32[]{:S(2)}) copy-start(f32[4,256,512]{2,1,0:T(8,128)} %copy-done.1) | copy-start | bytes 6291460
  67.2 55.7 %slice-start = ((s8[8388608]{0:T(1024)(128)(4,1)}), s8[4194304]{0:T(1024)(128)(4,1)S(1)}, s32[]{:S(2)}) async-start(s8[8388608]{0:T(1024)(128)(4,1)} %bitcast.59), calls=%async_computation | async-start | bytes 8388608
  70.4 69.1 %collective-permute-start.8 = (f32[3,256,512]{2,1,0:T(8,128)}, f32[3,256,512]{2,1,0:T(8,128)}, u32[]{:S(2)}, u32[]{:S(2)}) collective-permute-start(f32[3,256,512]{2,1,0:T(8,128)} %broadcast_select_fusion), channel_id=1, source_target_pairs={{0,2},{1,3},{2,4},{3,5},{4,6},{5,7},{6,8},{7,9},{8,10},{9,11},{10,... | collective-permute-start | bytes 4718600 | tf_op jit(solution)/shard_map/ppermute | solution.py:95
  118.5 4.4 %slice-start.1 = ((s8[8388608]{0:T(1024)(128)(4,1)}), s8[4194304]{0:T(1024)(128)(4,1)S(1)}, s32[]{:S(2)}) async-start(s8[8388608]{0:T(1024)(128)(4,1)} %bitcast.59), calls=%async_computation.1 | async-start | bytes 8388608
  127.7 2.8 %collective-permute-start.6 = (f32[256,512]{1,0:T(8,128)}, f32[256,512]{1,0:T(8,128)S(1)}, u32[]{:S(2)}, u32[]{:S(2)}) collective-permute-start(f32[256,512]{1,0:T(8,128)} %fusion.16), channel_id=1, source_target_pairs={{0,16},{16,0},{1,17},{17,1},{2,18},{18,2},{3,19},{19,3},{4,20},{20... | collective-permute-start | bytes 1572872 | tf_op jit(solution)/shard_map/ppermute | solution.py:98
  127.7 2.8 %collective-permute-start.7 = (f32[256,512]{1,0:T(8,128)S(1)}, f32[256,512]{1,0:T(8,128)S(1)}, u32[]{:S(2)}, u32[]{:S(2)}) collective-permute-start(f32[256,512]{1,0:T(8,128)S(1)} %fusion.20), channel_id=1, source_target_pairs={{0,16},{16,0},{1,17},{17,1},{2,18},{18,2},{3,19},{19,3},{4,20},{20... | collective-permute-start | bytes 1572872 | tf_op jit(solution)/shard_map/ppermute | solution.py:98
  129.5 19.0 %collective-permute-start.9 = (f32[1,256,512]{2,1,0:T(8,128)}, f32[1,256,512]{2,1,0:T(8,128)S(1)}, u32[]{:S(2)}, u32[]{:S(2)}) collective-permute-start(f32[1,256,512]{2,1,0:T(8,128)} %broadcast_select_fusion.1), channel_id=1, source_target_pairs={{0,2},{1,3},{2,4},{3,5},{4,6},{5,7},{6,8},{7,9},{8,10},{9,11},{10,... | collective-permute-start | bytes 1572872 | tf_op jit(solution)/shard_map/ppermute | solution.py:95

commit v7 on v6

--- a/solution.py
+++ b/solution.py
@@ -111,33 +111,29 @@
     terms = left_env.shape[0]
     (value,) = rows_of(lambda odd, own: (1 - odd, 1 - own), parts=(1,))
     ahead = send(value, lambda d: (d ^ 2) - d if d % 2 else 2)
-    near, near_last = rows_of(lambda odd, own: (0, own), parts=(terms - 1, 1))
-    beside = send(near, lambda d: (d ^ 1) - d)
-    (value,) = rows_of(lambda odd, own: (1 - odd, 1 - own), first=1)
+    (value,) = rows_of(lambda odd, own: (0, own))
+    value, later = after(value, psi)
+    beside = send(value, lambda d: (d ^ 1) - d)
+    (value,) = product(left_env, later, lambda odd, own: (1 - odd, 1 - own), first=1)
     first = send(value, lambda d: (d ^ 2) - d if d % 2 else 2)
     ahead, psi = after(ahead, psi)
     (value,) = product(left_env, psi, lambda odd, own: (1, jnp.where(odd == 1, 1 - own, own)), cost=100)
-    beside, psi = after(beside, psi)
-    kept, kept_last = product(
-        left_env, psi, lambda odd, own: (odd, jnp.where(odd == 1, own, 1 - own)), parts=(terms - 1, 1), cost=100
-    )
+    (kept,) = product(left_env, psi, lambda odd, own: (odd, jnp.where(odd == 1, own, 1 - own)), cost=1)
 
-    first, value, kept, kept_last, near_last = after(first, value, kept, kept_last, near_last)
+    first, value, kept = after(first, value, kept)
     second = send(value, lambda d: 2)
     first = jnp.concatenate([ahead, first])
-    beside_last = send(near_last, lambda d: (d ^ 1) - d)
     relayed = send(
-        jnp.where(odd == 1, first, jnp.concatenate([kept, kept_last])),
+        jnp.where(odd == 1, first, kept),
         lambda d: 1 if d % 2 == 0 else (-1 if d % 4 == 3 else 3),
     )
-    most = send(jnp.where(odd == 1, kept, beside), lambda d: 2)
+    most = send(jnp.where(odd == 1, kept[:-1], beside[:-1]), lambda d: 2)
     others_1 = contract(jnp.where(odd == 1, second, first), right[1])
     others_1, relayed = after(others_1, relayed)
     others_0 = contract(relayed, right[0])
-    others_0, last = after(others_0, jnp.where(odd == 1, kept_last, beside_last))
+    others_0, last = after(others_0, jnp.where(odd == 1, kept[-1:], beside[-1:]))
     last = send(last, lambda d: 2)
 
-    beside = jnp.concatenate([beside, beside_last])
     early = contract(jnp.where(odd == 1, beside, second), right_of(jnp.where(odd == 1, *slots)))
     late_slot = jnp.where(odd == 1, slots[1], slots[0])
     late_right = right_of(late_slot)

time: 150 us -> 150 us (level)
  waiting for transfers between devices: 83.4 us -> 87.4 us
  starting transfers between devices: 11.5 us -> 7.65 us
    ppermute x8 -> x7, starting transfers between devices: 11 us -> 7.08 us  [send(): return lax.ppermute(value, 'sec', pairs)]
    ppermute x8 -> x7, waiting for transfers between devices: 83.2 us -> 86.8 us  [send(): return lax.ppermute(value, 'sec', pairs)]
  transfers between devices with their start and end apart: 10 -> 9, of which waited for: 6 -> 6; matrix products, arithmetic and copies ran while one was open for 21% -> 20% of each run, Pallas kernels for 11% -> 11%
where the time goes in v7:
time: 150 us; the launch traced here: 149 us
  waiting for transfers between devices  87.4 us (58%)
  Pallas kernels  19 us (13%)
  matrix products  17.5 us (12%)
  other arithmetic  9.02 us (6%)
  starting transfers between devices  7.65 us (5%)
  local copies, waits for them, and re-layouts  4.57 us (3%)
  between operations  4.06 us (3%)
    ppermute x7, waiting for transfers between devices, send(): return lax.ppermute(value, 'sec', pairs)  86.8 us
    pallas_call x5, Pallas kernels, product(): pl.pallas_call(functools.partial(product_kernel, place=place, first=first...  19 us
    dot_general x4, matrix products, contract(): jnp.einsum('kac,kcd->ad', first, second, precision=lax.Precision.HIGH)  16.9 us
    ppermute x7, starting transfers between devices, send(): return lax.ppermute(value, 'sec', pairs)  7.08 us
    select_n x1, other arithmetic, per_device(): most = send(jnp.where(odd == 1, kept[:-1], beside[:-1]), lambda d: 2)  3.11 us
  transfers between devices with their start and end apart: 9, of which 6 were waited for; matrix products, arithmetic and copies ran while one was open for 20% of the time, Pallas kernels for 11%

profile of v7, /device:TPU:0, one launch (start us, length us, event | category | flops | bytes accessed | tf_op | source)
XLA Modules:
  0.0 149.1 jit_solution(4667833219399669831)
XLA Ops:
  0.0 2.0 %shard_map.48 = f32[1,256,512]{2,1,0:T(8,128)S(1)} custom-call(f32[4,2,512,512]{3,2,1,0:T(8,128)} %left_ref.9, f32[2,512,512]{2,1,0:T(8,128)} %psi_ref.6), custom_call_target="tpu_custom_call" | custom-call | flops 402653184 | bytes 1048576 | tf_op jit(solution)/shard_map/pallas_call | solution.py:64
  2.0 3.0 %collective-permute-start.2 = (f32[1,256,512]{2,1,0:T(8,128)S(1)}, f32[1,256,512]{2,1,0:T(8,128)S(1)}, u32[]{:S(2)}, u32[]{:S(2)}) collective-permute-start(f32[1,256,512]{2,1,0:T(8,128)S(1)} %shard_map.48), channel_id=1, source_target_pairs={{0,2},{1,3},{2,4},{3,1},{4,6},{5,7},{6,8},{7,5},{8,10},{9,11},{10,... | collective-permute-start | bytes 1572872 | tf_op jit(solution)/shard_map/ppermute | solution.py:95
  5.0 4.6 %shard_map.46 = f32[4,256,512]{2,1,0:T(8,128)} custom-call(f32[4,2,512,512]{3,2,1,0:T(8,128)} %left_ref.9, f32[2,512,512]{2,1,0:T(8,128)} %psi_ref.6), custom_call_target="tpu_custom_call" | custom-call | flops 1610612736 | bytes 4194304 | tf_op jit(solution)/shard_map/pallas_call | solution.py:64
  9.6 1.6 %collective-permute-start = (f32[4,256,512]{2,1,0:T(8,128)}, f32[4,256,512]{2,1,0:T(8,128)}, u32[]{:S(2)}, u32[]{:S(2)}) collective-permute-start(f32[4,256,512]{2,1,0:T(8,128)} %shard_map.46), channel_id=1, source_target_pairs={{0,1},{1,0},{2,3},{3,2},{4,5},{5,4},{6,7},{7,6},{8,9},{9,8},{10,11... | collective-permute-start | bytes 6291464 | tf_op jit(solution)/shard_map/ppermute | solution.py:95
  11.2 3.9 %shard_map.47 = f32[3,256,512]{2,1,0:T(8,128)} custom-call(f32[4,2,512,512]{3,2,1,0:T(8,128)} %left_ref.9, f32[2,512,512]{2,1,0:T(8,128)} %psi_ref.6), custom_call_target="tpu_custom_call" | custom-call | flops 1207959552 | bytes 3145728 | tf_op jit(solution)/shard_map/pallas_call | solution.py:64
  15.1 0.6 collective-permute-start.1
  15.6 4.4 %collective-permute-done.2 = f32[1,256,512]{2,1,0:T(8,128)S(1)} collective-permute-done((f32[1,256,512]{2,1,0:T(8,128)S(1)}, f32[1,256,512]{2,1,0:T(8,128)S(1)}, u32[]{:S(2)}, u32[]{:S(2)}) %collective-permute-start.2) | collective-permute-done | bytes 524320 | tf_op jit(solution)/shard_map/ppermute | solution.py:95
  20.0 4.8 %shard_map.49 = f32[4,256,512]{2,1,0:T(8,128)} custom-call(f32[4,2,512,512]{3,2,1,0:T(8,128)} %left_ref.9, f32[2,512,512]{2,1,0:T(8,128)} %psi_ref.6), custom_call_target="tpu_custom_call" | custom-call | flops 161061273600 | bytes 4194304 | tf_op jit(solution)/shard_map/pallas_call | solution.py:64
  24.8 1.1 constant_dynamic-update-slice_fusion.1
  25.9 3.7 %shard_map.50 = f32[4,256,512]{2,1,0:T(8,128)S(1)} custom-call(f32[4,2,512,512]{3,2,1,0:T(8,128)} %left_ref.9, f32[2,512,512]{2,1,0:T(8,128)} %psi_ref.6), custom_call_target="tpu_custom_call" | custom-call | flops 1610612736 | bytes 4194304 | tf_op jit(solution)/shard_map/pallas_call | solution.py:64
  29.6 24.2 %collective-permute-done.1 = f32[3,256,512]{2,1,0:T(8,128)} collective-permute-done((f32[3,256,512]{2,1,0:T(8,128)}, f32[3,256,512]{2,1,0:T(8,128)}, u32[]{:S(2)}, u32[]{:S(2)}) %collective-permute-start.1) | collective-permute-done | bytes 1572896 | tf_op jit(solution)/shard_map/ppermute | solution.py:95
  53.8 1.5 %constant_dynamic-update-slice_fusion = f32[4,256,512]{2,1,0:T(8,128)S(1)} fusion(f32[4,256,512]{2,1,0:T(8,128)S(1)} %constant_dynamic-update-slice_fusion.1, f32[3,256,512]{2,1,0:T(8,128)} %collective-permute-done.1), kind=kLoop, calls=%fused_computation.30 | loop fusion | bytes 3145728 | tf_op jit(solution)/shard_map/concatenate | solution.py:125
  55.4 2.0 %broadcast_select_fusion = f32[4,256,512]{2,1,0:T(8,128)} fusion(f32[4,256,512]{2,1,0:T(8,128)S(1)} %constant_dynamic-update-slice_fusion, f32[4,256,512]{2,1,0:T(8,128)S(1)} %shard_map.50, pred[]{:T(512)S(6)} %eq.8), kind=kLoop, calls=%fused_computation.23 | loop fusion | flops 524288 | bytes 6291457 | tf_op jit(solution)/shard_map/jit(_where)/select_n | solution.py:127
  57.4 0.2 collective-permute-start.4
  57.5 0.6 fusion.45
  62.1 3.1 %slice_select_fusion = f32[3,256,512]{2,1,0:T(8,128)} fusion(f32[4,256,512]{2,1,0:T(8,128)} %collective-permute-done, f32[4,256,512]{2,1,0:T(8,128)S(1)} %shard_map.50, pred[]{:T(512)S(6)} %eq.8), kind=kLoop, calls=%fused_computation.13 | loop fusion | flops 393216 | bytes 4718593 | tf_op jit(solution)/shard_map/jit(_where)/select_n | solution.py:130
  65.2 1.5 %collective-permute-start.7 = (f32[3,256,512]{2,1,0:T(8,128)}, f32[3,256,512]{2,1,0:T(8,128)}, u32[]{:S(2)}, u32[]{:S(2)}) collective-permute-start(f32[3,256,512]{2,1,0:T(8,128)} %slice_select_fusion), channel_id=1, source_target_pairs={{0,2},{1,3},{2,4},{3,5},{4,6},{5,7},{6,8},{7,9},{8,10},{9,11},{10,... | collective-permute-start | bytes 4718600 | tf_op jit(solution)/shard_map/ppermute | solution.py:95
  66.7 1.9 %slice_select_fusion.1 = f32[1,256,512]{2,1,0:T(8,128)} fusion(f32[4,256,512]{2,1,0:T(8,128)} %collective-permute-done, f32[4,256,512]{2,1,0:T(8,128)S(1)} %shard_map.50, pred[]{:T(512)S(6)} %eq.8), kind=kLoop, calls=%fused_computation.26 | loop fusion | flops 131072 | bytes 1572865 | tf_op jit(solution)/shard_map/jit(_where)/select_n | solution.py:134
  68.6 36.7 %collective-permute-done.3 = f32[4,256,512]{2,1,0:T(8,128)} collective-permute-done((f32[4,256,512]{2,1,0:T(8,128)}, f32[4,256,512]{2,1,0:T(8,128)}, u32[]{:S(2)}, u32[]{:S(2)}) %collective-permute-start.3) | collective-permute-done | bytes 2097184 | tf_op jit(solution)/shard_map/ppermute | solution.py:95
  105.4 4.2 %fusion.21 = f32[256,512]{1,0:T(8,128)S(1)} fusion(f32[4,2,512,512]{3,2,1,0:T(8,128)} %param.6, s32[]{:T(128)S(6)} %select_n.107, f32[4,256,512]{2,1,0:T(8,128)} %collective-permute-done.3, f32[4,256,512]{2,1,0:T(8,128)S(1)} %copy-done.1, pred[]{:T(512)S(6)} %eq.8), kind=kOutput, calls=%fused_computation.17 | convolution fusion | flops 1611137024 | bytes 8912901 | tf_op jit(solution)/shard_map/kac,kcd->ad/dot_general | solution.py:85
  109.7 3.9 %fusion.12 = f32[256,512]{1,0:T(8,128)S(1)} fusion(f32[4,256,512]{2,1,0:T(8,128)} %collective-permute-done.4, f32[4,2,512,512]{3,2,1,0:T(8,128)S(1)} %bitcast.60, s32[]{:T(128)S(6)} %select_n.109), kind=kOutput, calls=%fused_computation.14 | convolution fusion | flops 1610612736 | bytes 6815748 | tf_op jit(solution)/shard_map/kac,kcd->ad/dot_general | solution.py:85
  113.7 0.5 collective-permute-start.6
  114.2 1.3 dynamic-slice_bitcast_fusion.6
  115.4 0.2 collective-permute-start.8
  115.7 0.6 collective-permute-done.6
  116.3 4.8 %fusion.31 = f32[1,256,512]{2,1,0:T(8,128)S(1)} fusion(f32[4,2,512,512]{3,2,1,0:T(8,128)} %param.6, s32[]{:T(128)S(6)} %select_n.104, f32[4,256,512]{2,1,0:T(8,128)} %collective-permute-done, f32[4,256,512]{2,1,0:T(8,128)} %collective-permute-done.3, pred[]{:T(512)S(6)} %eq.8, f32[256,512]{1,0:T(8,128)S(1)} %collective-permute-done.5, ...), kind=kOutput, calls=%fused_computation.19 | convolution fusion | flops 1611399168 | bytes 9963008 | tf_op jit(solution)/shard_map/kac,kcd->ad/dot_general | solution.py:85
  121.1 1.1 pad_maximum_fusion
  122.3 16.8 %collective-permute-done.7 = f32[3,256,512]{2,1,0:T(8,128)} collective-permute-done((f32[3,256,512]{2,1,0:T(8,128)}, f32[3,256,512]{2,1,0:T(8,128)}, u32[]{:S(2)}, u32[]{:S(2)}) %collective-permute-start.7) | collective-permute-done | bytes 1572896 | tf_op jit(solution)/shard_map/ppermute | solution.py:95
  139.1 3.9 %fusion.36 = f32[256,512]{1,0:T(8,128)S(1)} fusion(f32[3,256,512]{2,1,0:T(8,128)} %collective-permute-done.7, f32[4,2,512,512]{3,2,1,0:T(8,128)} %param.6, s32[]{:T(128)S(6)} %select_n.116, f32[256,512]{1,0:T(8,128)S(1)} %collective-permute-done.6, f32[256,512]{1,0:T(8,128)S(1)} %collective-permute-done.5, pred[]{:T(512)S(6)} %eq.8), kind=kOutput, calls=%fused_computation.20 | convolution fusion | flops 1208221696 | bytes 6291461 | tf_op jit(solution)/shard_map/kac,kcd->ad/dot_general | solution.py:85
  143.0 4.6 %collective-permute-done.8 = f32[1,256,512]{2,1,0:T(8,128)S(1)} collective-permute-done((f32[1,256,512]{2,1,0:T(8,128)}, f32[1,256,512]{2,1,0:T(8,128)S(1)}, u32[]{:S(2)}, u32[]{:S(2)}) %collective-permute-start.8) | collective-permute-done | bytes 524320 | tf_op jit(solution)/shard_map/ppermute | solution.py:95
  147.6 0.6 fusion.39
  148.2 0.9 bitcast_dynamic-update-slice_fusion
  (18 shorter events, 0.1 us)
Async XLA Ops:
  2.0 18.0 %collective-permute-start.2 = (f32[1,256,512]{2,1,0:T(8,128)S(1)}, f32[1,256,512]{2,1,0:T(8,128)S(1)}, u32[]{:S(2)}, u32[]{:S(2)}) collective-permute-start(f32[1,256,512]{2,1,0:T(8,128)S(1)} %shard_map.48), channel_id=1, source_target_pairs={{0,2},{1,3},{2,4},{3,1},{4,6},{5,7},{6,8},{7,5},{8,10},{9,11},{10,... | collective-permute-start | bytes 1572872 | tf_op jit(solution)/shard_map/ppermute | solution.py:95
  9.6 52.5 %collective-permute-start = (f32[4,256,512]{2,1,0:T(8,128)}, f32[4,256,512]{2,1,0:T(8,128)}, u32[]{:S(2)}, u32[]{:S(2)}) collective-permute-start(f32[4,256,512]{2,1,0:T(8,128)} %shard_map.46), channel_id=1, source_target_pairs={{0,1},{1,0},{2,3},{3,2},{4,5},{5,4},{6,7},{7,6},{8,9},{9,8},{10,11... | collective-permute-start | bytes 6291464 | tf_op jit(solution)/shard_map/ppermute | solution.py:95
  15.1 38.7 %collective-permute-start.1 = (f32[3,256,512]{2,1,0:T(8,128)}, f32[3,256,512]{2,1,0:T(8,128)}, u32[]{:S(2)}, u32[]{:S(2)}) collective-permute-start(f32[3,256,512]{2,1,0:T(8,128)} %shard_map.47), channel_id=1, source_target_pairs={{0,2},{1,3},{2,4},{3,1},{4,6},{5,7},{6,8},{7,5},{8,10},{9,11},{10,... | collective-permute-start | bytes 4718600 | tf_op jit(solution)/shard_map/ppermute | solution.py:95
  20.0 4.8 %copy-start.2 = (f32[1,256,512]{2,1,0:T(8,128)}, f32[1,256,512]{2,1,0:T(8,128)S(1)}, u32[]{:S(2)}) copy-start(f32[1,256,512]{2,1,0:T(8,128)S(1)} %collective-permute-done.2) | copy-start | bytes 1572868
  53.8 51.6 %collective-permute-start.3 = (f32[4,256,512]{2,1,0:T(8,128)}, f32[4,256,512]{2,1,0:T(8,128)}, u32[]{:S(2)}, u32[]{:S(2)}) collective-permute-start(f32[4,256,512]{2,1,0:T(8,128)} %shard_map.49), channel_id=1, source_target_pairs={{0,2},{1,3},{2,4},{3,5},{4,6},{5,7},{6,8},{7,9},{8,10},{9,11},{10,... | collective-permute-start | bytes 6291464 | tf_op jit(solution)/shard_map/ppermute | solution.py:95
  55.3 2.0 %copy-start = (f32[4,256,512]{2,1,0:T(8,128)}, f32[4,256,512]{2,1,0:T(8,128)S(1)}, u32[]{:S(2)}) copy-start(f32[4,256,512]{2,1,0:T(8,128)S(1)} %constant_dynamic-update-slice_fusion) | copy-start | bytes 6291460
  55.4 2.2 %copy-start.3 = (s32[32]{0:T(128)S(1)}, s32[32]{0:T(128)}, u32[]{:S(2)}) copy-start(s32[32]{0:T(128)} %param.7) | copy-start | bytes 388
  57.4 52.3 %collective-permute-start.4 = (f32[4,256,512]{2,1,0:T(8,128)}, f32[4,256,512]{2,1,0:T(8,128)}, u32[]{:S(2)}, u32[]{:S(2)}) collective-permute-start(f32[4,256,512]{2,1,0:T(8,128)} %broadcast_select_fusion), channel_id=1, source_target_pairs={{0,1},{1,4},{2,3},{3,2},{4,5},{5,8},{6,7},{7,6},{8,9},{9,12},{10,1... | collective-permute-start | bytes 6291464 | tf_op jit(solution)/shard_map/ppermute | solution.py:95
  62.0 43.4 %copy-start.1 = (f32[4,256,512]{2,1,0:T(8,128)S(1)}, f32[4,256,512]{2,1,0:T(8,128)}, u32[]{:S(2)}) copy-start(f32[4,256,512]{2,1,0:T(8,128)} %copy-done) | copy-start | bytes 6291460
  62.1 47.6 %slice-start = ((s8[8388608]{0:T(1024)(128)(4,1)}), s8[4194304]{0:T(1024)(128)(4,1)S(1)}, s32[]{:S(2)}) async-start(s8[8388608]{0:T(1024)(128)(4,1)} %bitcast.59), calls=%async_computation | async-start | bytes 8388608
  65.2 73.9 %collective-permute-start.7 = (f32[3,256,512]{2,1,0:T(8,128)}, f32[3,256,512]{2,1,0:T(8,128)}, u32[]{:S(2)}, u32[]{:S(2)}) collective-permute-start(f32[3,256,512]{2,1,0:T(8,128)} %slice_select_fusion), channel_id=1, source_target_pairs={{0,2},{1,3},{2,4},{3,5},{4,6},{5,7},{6,8},{7,9},{8,10},{9,11},{10,... | collective-permute-start | bytes 4718600 | tf_op jit(solution)/shard_map/ppermute | solution.py:95
  68.6 41.0 %slice-start.1 = ((s8[8388608]{0:T(1024)(128)(4,1)}), s8[4194304]{0:T(1024)(128)(4,1)S(1)}, s32[]{:S(2)}) async-start(s8[8388608]{0:T(1024)(128)(4,1)} %bitcast.59), calls=%async_computation.1 | async-start | bytes 8388608
  113.6 2.1 %collective-permute-start.5 = (f32[256,512]{1,0:T(8,128)S(1)}, f32[256,512]{1,0:T(8,128)S(1)}, u32[]{:S(2)}, u32[]{:S(2)}) collective-permute-start(f32[256,512]{1,0:T(8,128)S(1)} %fusion.12), channel_id=1, source_target_pairs={{0,16},{16,0},{1,17},{17,1},{2,18},{18,2},{3,19},{19,3},{4,20},{20... | collective-permute-start | bytes 1572872 | tf_op jit(solution)/shard_map/ppermute | solution.py:98
  113.7 2.6 %collective-permute-start.6 = (f32[256,512]{1,0:T(8,128)S(1)}, f32[256,512]{1,0:T(8,128)S(1)}, u32[]{:S(2)}, u32[]{:S(2)}) collective-permute-start(f32[256,512]{1,0:T(8,128)S(1)} %fusion.21), channel_id=1, source_target_pairs={{0,16},{16,0},{1,17},{17,1},{2,18},{18,2},{3,19},{19,3},{4,20},{20... | collective-permute-start | bytes 1572872 | tf_op jit(solution)/shard_map/ppermute | solution.py:98
  115.4 32.2 %collective-permute-start.8 = (f32[1,256,512]{2,1,0:T(8,128)}, f32[1,256,512]{2,1,0:T(8,128)S(1)}, u32[]{:S(2)}, u32[]{:S(2)}) collective-permute-start(f32[1,256,512]{2,1,0:T(8,128)} %slice_select_fusion.1), channel_id=1, source_target_pairs={{0,2},{1,3},{2,4},{3,5},{4,6},{5,7},{6,8},{7,9},{8,10},{9,11},{10,... | collective-permute-start | bytes 1572872 | tf_op jit(solution)/shard_map/ppermute | solution.py:95

commit v8 on v7

--- a/solution.py
+++ b/solution.py
@@ -120,14 +120,15 @@
     (value,) = product(left_env, psi, lambda odd, own: (1, jnp.where(odd == 1, 1 - own, own)), cost=100)
     (kept,) = product(left_env, psi, lambda odd, own: (odd, jnp.where(odd == 1, own, 1 - own)), cost=1)
 
-    first, value, kept = after(first, value, kept)
-    second = send(value, lambda d: 2)
+    onward = send(kept, lambda d: 1, lambda d: d % 2 == 0)
+    second_even = send(value, lambda d: 2, lambda d: d % 2 == 0)
+    first, gated = after(first, value)
+    second_odd = send(gated, lambda d: 2, lambda d: d % 2 == 1)
     first = jnp.concatenate([ahead, first])
-    relayed = send(
-        jnp.where(odd == 1, first, kept),
-        lambda d: 1 if d % 2 == 0 else (-1 if d % 4 == 3 else 3),
-    )
+    hop = send(first, lambda d: -1 if d % 4 == 3 else 3, lambda d: d % 2 == 1)
     most = send(jnp.where(odd == 1, kept[:-1], beside[:-1]), lambda d: 2)
+    second = jnp.where(odd == 1, second_odd, second_even)
+    relayed = jnp.where(odd == 1, onward, hop)
     others_1 = contract(jnp.where(odd == 1, second, first), right[1])
     others_1, relayed = after(others_1, relayed)
     others_0 = contract(relayed, right[0])

time: 150 us -> 148 us (0.987); the launches traced: 149 us -> 145 us
  waiting for transfers between devices: 87.4 us -> 75.1 us
  starting transfers between devices: 7.65 us -> 14.9 us
    ppermute x7 -> x9, waiting for transfers between devices: 86.8 us -> 74.1 us  [send(): return lax.ppermute(value, 'sec', pairs)]
    ppermute x7 -> x9, starting transfers between devices: 7.08 us -> 14.4 us  [send(): return lax.ppermute(value, 'sec', pairs)]
  transfers between devices with their start and end apart: 9 -> 11, of which waited for: 6 -> 8; matrix products, arithmetic and copies ran while one was open for 20% -> 21% of each run, Pallas kernels for 11% -> 12%
where the time goes in v8:
time: 148 us; the launch traced here: 145 us
  waiting for transfers between devices  75.1 us (51%)
  Pallas kernels  19 us (13%)
  matrix products  17.8 us (12%)
  starting transfers between devices  14.9 us (10%)
  other arithmetic  9.14 us (6%)
  local copies, waits for them, and re-layouts  5.4 us (4%)
  between operations  3.86 us (3%)
    ppermute x9, waiting for transfers between devices, send(): return lax.ppermute(value, 'sec', pairs)  74.1 us
    pallas_call x5, Pallas kernels, product(): pl.pallas_call(functools.partial(product_kernel, place=place, first=first...  19 us
    dot_general x4, matrix products, contract(): jnp.einsum('kac,kcd->ad', first, second, precision=lax.Precision.HIGH)  17.1 us
    ppermute x9, starting transfers between devices, send(): return lax.ppermute(value, 'sec', pairs)  14.4 us
  transfers between devices with their start and end apart: 11, of which 8 were waited for; matrix products, arithmetic and copies ran while one was open for 21% of the time, Pallas kernels for 12%

profile of v8, /device:TPU:0, one launch (start us, length us, event | category | flops | bytes accessed | tf_op | source)
XLA Modules:
  0.0 145.1 jit_solution(16741085745678739081)
XLA Ops:
  0.0 2.0 %shard_map.48 = f32[1,256,512]{2,1,0:T(8,128)S(1)} custom-call(f32[4,2,512,512]{3,2,1,0:T(8,128)} %left_ref.9, f32[2,512,512]{2,1,0:T(8,128)} %psi_ref.6), custom_call_target="tpu_custom_call" | custom-call | flops 402653184 | bytes 1048576 | tf_op jit(solution)/shard_map/pallas_call | solution.py:64
  2.0 3.0 %collective-permute-start.2 = (f32[1,256,512]{2,1,0:T(8,128)S(1)}, f32[1,256,512]{2,1,0:T(8,128)S(1)}, u32[]{:S(2)}, u32[]{:S(2)}) collective-permute-start(f32[1,256,512]{2,1,0:T(8,128)S(1)} %shard_map.48), channel_id=1, source_target_pairs={{0,2},{1,3},{2,4},{3,1},{4,6},{5,7},{6,8},{7,5},{8,10},{9,11},{10,... | collective-permute-start | bytes 1572872 | tf_op jit(solution)/shard_map/ppermute | solution.py:95
  5.0 4.6 %shard_map.46 = f32[4,256,512]{2,1,0:T(8,128)} custom-call(f32[4,2,512,512]{3,2,1,0:T(8,128)} %left_ref.9, f32[2,512,512]{2,1,0:T(8,128)} %psi_ref.6), custom_call_target="tpu_custom_call" | custom-call | flops 1610612736 | bytes 4194304 | tf_op jit(solution)/shard_map/pallas_call | solution.py:64
  9.6 4.0 %shard_map.47 = f32[3,256,512]{2,1,0:T(8,128)} custom-call(f32[4,2,512,512]{3,2,1,0:T(8,128)} %left_ref.9, f32[2,512,512]{2,1,0:T(8,128)} %psi_ref.6), custom_call_target="tpu_custom_call" | custom-call | flops 1207959552 | bytes 3145728 | tf_op jit(solution)/shard_map/pallas_call | solution.py:64
  13.6 1.6 %collective-permute-start.1 = (f32[3,256,512]{2,1,0:T(8,128)}, f32[3,256,512]{2,1,0:T(8,128)}, u32[]{:S(2)}, u32[]{:S(2)}) collective-permute-start(f32[3,256,512]{2,1,0:T(8,128)} %shard_map.47), channel_id=1, source_target_pairs={{0,2},{1,3},{2,4},{3,1},{4,6},{5,7},{6,8},{7,5},{8,10},{9,11},{10,... | collective-permute-start | bytes 4718600 | tf_op jit(solution)/shard_map/ppermute | solution.py:95
  15.6 5.2 %collective-permute-done.2 = f32[1,256,512]{2,1,0:T(8,128)S(1)} collective-permute-done((f32[1,256,512]{2,1,0:T(8,128)S(1)}, f32[1,256,512]{2,1,0:T(8,128)S(1)}, u32[]{:S(2)}, u32[]{:S(2)}) %collective-permute-start.2) | collective-permute-done | bytes 524320 | tf_op jit(solution)/shard_map/ppermute | solution.py:95
  20.8 4.7 %shard_map.49 = f32[4,256,512]{2,1,0:T(8,128)} custom-call(f32[4,2,512,512]{3,2,1,0:T(8,128)} %left_ref.9, f32[2,512,512]{2,1,0:T(8,128)} %psi_ref.6), custom_call_target="tpu_custom_call" | custom-call | flops 161061273600 | bytes 4194304 | tf_op jit(solution)/shard_map/pallas_call | solution.py:64
  25.6 1.9 %collective-permute-start.4 = (f32[4,256,512]{2,1,0:T(8,128)}, f32[4,256,512]{2,1,0:T(8,128)}, u32[]{:S(2)}, u32[]{:S(2)}) collective-permute-start(f32[4,256,512]{2,1,0:T(8,128)} %shard_map.49), channel_id=1, source_target_pairs={{0,2},{2,4},{4,6},{6,8},{8,10},{10,12},{12,14},{14,0},{16,18},{18,... | collective-permute-start | bytes 6291464 | tf_op jit(solution)/shard_map/ppermute | solution.py:95
  27.5 27.1 %collective-permute-done.1 = f32[3,256,512]{2,1,0:T(8,128)} collective-permute-done((f32[3,256,512]{2,1,0:T(8,128)}, f32[3,256,512]{2,1,0:T(8,128)}, u32[]{:S(2)}, u32[]{:S(2)}) %collective-permute-start.1) | collective-permute-done | bytes 1572896 | tf_op jit(solution)/shard_map/ppermute | solution.py:95
  54.6 2.0 %collective-permute-start.3 = (f32[4,256,512]{2,1,0:T(8,128)}, f32[4,256,512]{2,1,0:T(8,128)}, u32[]{:S(2)}, u32[]{:S(2)}) collective-permute-start(f32[4,256,512]{2,1,0:T(8,128)} %shard_map.49), channel_id=1, source_target_pairs={{1,3},{3,5},{5,7},{7,9},{9,11},{11,13},{13,15},{15,1},{17,19},{19,... | collective-permute-start | bytes 6291464 | tf_op jit(solution)/shard_map/ppermute | solution.py:95
  56.7 3.7 %shard_map.50 = f32[4,256,512]{2,1,0:T(8,128)S(1)} custom-call(f32[4,2,512,512]{3,2,1,0:T(8,128)} %left_ref.9, f32[2,512,512]{2,1,0:T(8,128)} %psi_ref.6), custom_call_target="tpu_custom_call" | custom-call | flops 1610612736 | bytes 4194304 | tf_op jit(solution)/shard_map/pallas_call | solution.py:64
  60.4 2.6 %collective-permute-start.5 = (f32[4,256,512]{2,1,0:T(8,128)S(1)}, f32[4,256,512]{2,1,0:T(8,128)}, u32[]{:S(2)}, u32[]{:S(2)}) collective-permute-start(f32[4,256,512]{2,1,0:T(8,128)S(1)} %shard_map.50), channel_id=1, source_target_pairs={{0,1},{2,3},{4,5},{6,7},{8,9},{10,11},{12,13},{14,15},{16,17},{18,... | collective-permute-start | bytes 6291464 | tf_op jit(solution)/shard_map/ppermute | solution.py:95
  63.0 0.8 constant_dynamic-update-slice_fusion.1
  63.8 2.7 %constant_dynamic-update-slice_fusion = f32[4,256,512]{2,1,0:T(8,128)} fusion(f32[4,256,512]{2,1,0:T(8,128)} %constant_dynamic-update-slice_fusion.1, f32[3,256,512]{2,1,0:T(8,128)} %collective-permute-done.1), kind=kLoop, calls=%fused_computation.31 | loop fusion | bytes 3145728 | tf_op jit(solution)/shard_map/concatenate | solution.py:127
  66.5 1.3 collective-permute-start.6
  72.1 2.9 %slice_select_fusion = f32[3,256,512]{2,1,0:T(8,128)} fusion(f32[4,256,512]{2,1,0:T(8,128)} %collective-permute-done, f32[4,256,512]{2,1,0:T(8,128)S(1)} %shard_map.50, pred[]{:T(512)S(6)} %eq.8), kind=kLoop, calls=%fused_computation.13 | loop fusion | flops 393216 | bytes 4718593 | tf_op jit(solution)/shard_map/jit(_where)/select_n | solution.py:129
  75.0 1.4 collective-permute-start.9
  76.4 2.1 %slice_select_fusion.1 = f32[1,256,512]{2,1,0:T(8,128)} fusion(f32[4,256,512]{2,1,0:T(8,128)} %collective-permute-done, f32[4,256,512]{2,1,0:T(8,128)S(1)} %shard_map.50, pred[]{:T(512)S(6)} %eq.8), kind=kLoop, calls=%fused_computation.27 | loop fusion | flops 131072 | bytes 1572865 | tf_op jit(solution)/shard_map/jit(_where)/select_n | solution.py:135
  78.5 21.1 %collective-permute-done.4 = f32[4,256,512]{2,1,0:T(8,128)} collective-permute-done((f32[4,256,512]{2,1,0:T(8,128)}, f32[4,256,512]{2,1,0:T(8,128)}, u32[]{:S(2)}, u32[]{:S(2)}) %collective-permute-start.4) | collective-permute-done | bytes 2097184 | tf_op jit(solution)/shard_map/ppermute | solution.py:95
  99.6 5.5 %fusion.21 = f32[256,512]{1,0:T(8,128)S(1)} fusion(f32[4,2,512,512]{3,2,1,0:T(8,128)} %param.6, s32[]{:T(128)S(6)} %select_n.112, f32[4,256,512]{2,1,0:T(8,128)} %constant_dynamic-update-slice_fusion, pred[]{:T(512)S(6)} %eq.8, f32[4,256,512]{2,1,0:T(8,128)} %collective-permute-done.3, f32[4,256,512]{2,1,0:T(8,128)} %collective-permute-done.4), kind=kOutput, calls=%fused_computation.17 | convolution fusion | flops 1611661312 | bytes 11010053 | tf_op jit(solution)/shard_map/kac,kcd->ad/dot_general | solution.py:85
  105.4 11.9 %collective-permute-done.6 = f32[4,256,512]{2,1,0:T(8,128)} collective-permute-done((f32[4,256,512]{2,1,0:T(8,128)}, f32[4,256,512]{2,1,0:T(8,128)}, u32[]{:S(2)}, u32[]{:S(2)}) %collective-permute-start.6) | collective-permute-done | bytes 2097184 | tf_op jit(solution)/shard_map/ppermute | solution.py:95
  117.4 2.1 %broadcast_select_fusion = f32[4,256,512]{2,1,0:T(8,128)S(1)} fusion(f32[4,256,512]{2,1,0:T(8,128)} %collective-permute-done.5, f32[4,256,512]{2,1,0:T(8,128)} %collective-permute-done.6, pred[]{:T(512)S(6)} %eq.8), kind=kLoop, calls=%fused_computation.23 | loop fusion | flops 524288 | bytes 6291457 | tf_op jit(solution)/shard_map/jit(_where)/select_n | solution.py:131
  119.5 2.9 %fusion.12 = f32[256,512]{1,0:T(8,128)} fusion(f32[4,256,512]{2,1,0:T(8,128)S(1)} %broadcast_select_fusion, f32[4,2,512,512]{3,2,1,0:T(8,128)S(1)} %bitcast.60, s32[]{:T(128)S(6)} %select_n.114), kind=kOutput, calls=%fused_computation.14 | convolution fusion | flops 1610612736 | bytes 6815748 | tf_op jit(solution)/shard_map/kac,kcd->ad/dot_general | solution.py:85
  123.0 1.3 dynamic-slice_bitcast_fusion.6
  124.4 1.0 collective-permute-done.7
  125.3 4.8 %fusion.31 = f32[1,256,512]{2,1,0:T(8,128)S(1)} fusion(f32[4,2,512,512]{3,2,1,0:T(8,128)} %param.6, s32[]{:T(128)S(6)} %select_n.109, f32[4,256,512]{2,1,0:T(8,128)} %collective-permute-done, pred[]{:T(512)S(6)} %eq.8, f32[4,256,512]{2,1,0:T(8,128)} %collective-permute-done.3, f32[4,256,512]{2,1,0:T(8,128)} %collective-permute-done.4, ...), kind=kOutput, calls=%fused_computation.19 | convolution fusion | flops 1611923456 | bytes 12060160 | tf_op jit(solution)/shard_map/kac,kcd->ad/dot_general | solution.py:85
  130.2 1.1 pad_maximum_fusion
  131.3 2.0 %collective-permute-done.9 = f32[3,256,512]{2,1,0:T(8,128)} collective-permute-done((f32[3,256,512]{2,1,0:T(8,128)}, f32[3,256,512]{2,1,0:T(8,128)}, u32[]{:S(2)}, u32[]{:S(2)}) %collective-permute-start.9) | collective-permute-done | bytes 1572896 | tf_op jit(solution)/shard_map/ppermute | solution.py:95
  133.3 3.9 %fusion.36 = f32[256,512]{1,0:T(8,128)S(1)} fusion(f32[3,256,512]{2,1,0:T(8,128)} %collective-permute-done.9, f32[4,2,512,512]{3,2,1,0:T(8,128)} %param.6, s32[]{:T(128)S(6)} %select_n.121, f32[256,512]{1,0:T(8,128)S(1)} %collective-permute-done.8, f32[256,512]{1,0:T(8,128)S(1)} %collective-permute-done.7, pred[]{:T(512)S(6)} %eq.8), kind=kOutput, calls=%fused_computation.20 | convolution fusion | flops 1208221696 | bytes 6291461 | tf_op jit(solution)/shard_map/kac,kcd->ad/dot_general | solution.py:85
  137.2 6.4 %collective-permute-done.10 = f32[1,256,512]{2,1,0:T(8,128)S(1)} collective-permute-done((f32[1,256,512]{2,1,0:T(8,128)}, f32[1,256,512]{2,1,0:T(8,128)S(1)}, u32[]{:S(2)}, u32[]{:S(2)}) %collective-permute-start.10) | collective-permute-done | bytes 524320 | tf_op jit(solution)/shard_map/ppermute | solution.py:95
  143.6 0.6 fusion.39
  144.2 0.9 bitcast_dynamic-update-slice_fusion
  (20 shorter events, 2.1 us)
Async XLA Ops:
  2.0 18.8 %collective-permute-start.2 = (f32[1,256,512]{2,1,0:T(8,128)S(1)}, f32[1,256,512]{2,1,0:T(8,128)S(1)}, u32[]{:S(2)}, u32[]{:S(2)}) collective-permute-start(f32[1,256,512]{2,1,0:T(8,128)S(1)} %shard_map.48), channel_id=1, source_target_pairs={{0,2},{1,3},{2,4},{3,1},{4,6},{5,7},{6,8},{7,5},{8,10},{9,11},{10,... | collective-permute-start | bytes 1572872 | tf_op jit(solution)/shard_map/ppermute | solution.py:95
  13.6 41.0 %collective-permute-start.1 = (f32[3,256,512]{2,1,0:T(8,128)}, f32[3,256,512]{2,1,0:T(8,128)}, u32[]{:S(2)}, u32[]{:S(2)}) collective-permute-start(f32[3,256,512]{2,1,0:T(8,128)} %shard_map.47), channel_id=1, source_target_pairs={{0,2},{1,3},{2,4},{3,1},{4,6},{5,7},{6,8},{7,5},{8,10},{9,11},{10,... | collective-permute-start | bytes 4718600 | tf_op jit(solution)/shard_map/ppermute | solution.py:95
  15.2 56.9 %collective-permute-start = (f32[4,256,512]{2,1,0:T(8,128)}, f32[4,256,512]{2,1,0:T(8,128)}, u32[]{:S(2)}, u32[]{:S(2)}) collective-permute-start(f32[4,256,512]{2,1,0:T(8,128)} %shard_map.46), channel_id=1, source_target_pairs={{0,1},{1,0},{2,3},{3,2},{4,5},{5,4},{6,7},{7,6},{8,9},{9,8},{10,11... | collective-permute-start | bytes 6291464 | tf_op jit(solution)/shard_map/ppermute | solution.py:95
  20.8 4.7 %copy-start = (f32[1,256,512]{2,1,0:T(8,128)}, f32[1,256,512]{2,1,0:T(8,128)S(1)}, u32[]{:S(2)}) copy-start(f32[1,256,512]{2,1,0:T(8,128)S(1)} %collective-permute-done.2) | copy-start | bytes 1572868
  25.6 74.0 %collective-permute-start.4 = (f32[4,256,512]{2,1,0:T(8,128)}, f32[4,256,512]{2,1,0:T(8,128)}, u32[]{:S(2)}, u32[]{:S(2)}) collective-permute-start(f32[4,256,512]{2,1,0:T(8,128)} %shard_map.49), channel_id=1, source_target_pairs={{0,2},{2,4},{4,6},{6,8},{8,10},{10,12},{12,14},{14,0},{16,18},{18,... | collective-permute-start | bytes 6291464 | tf_op jit(solution)/shard_map/ppermute | solution.py:95
  27.5 35.5 %copy-start.1 = (f32[1,256,512]{2,1,0:T(8,128)S(1)}, f32[1,256,512]{2,1,0:T(8,128)}, u32[]{:S(2)}) copy-start(f32[1,256,512]{2,1,0:T(8,128)} %copy-done) | copy-start | bytes 1572868
  54.6 44.9 %collective-permute-start.3 = (f32[4,256,512]{2,1,0:T(8,128)}, f32[4,256,512]{2,1,0:T(8,128)}, u32[]{:S(2)}, u32[]{:S(2)}) collective-permute-start(f32[4,256,512]{2,1,0:T(8,128)} %shard_map.49), channel_id=1, source_target_pairs={{1,3},{3,5},{5,7},{7,9},{9,11},{11,13},{13,15},{15,1},{17,19},{19,... | collective-permute-start | bytes 6291464 | tf_op jit(solution)/shard_map/ppermute | solution.py:95
  60.4 7.5 %copy-start.2 = (s32[32]{0:T(128)S(1)}, s32[32]{0:T(128)}, u32[]{:S(2)}) copy-start(s32[32]{0:T(128)} %param.7) | copy-start | bytes 388
  60.4 45.1 %collective-permute-start.5 = (f32[4,256,512]{2,1,0:T(8,128)S(1)}, f32[4,256,512]{2,1,0:T(8,128)}, u32[]{:S(2)}, u32[]{:S(2)}) collective-permute-start(f32[4,256,512]{2,1,0:T(8,128)S(1)} %shard_map.50), channel_id=1, source_target_pairs={{0,1},{2,3},{4,5},{6,7},{8,9},{10,11},{12,13},{14,15},{16,17},{18,... | collective-permute-start | bytes 6291464 | tf_op jit(solution)/shard_map/ppermute | solution.py:95
  66.5 50.9 %collective-permute-start.6 = (f32[4,256,512]{2,1,0:T(8,128)}, f32[4,256,512]{2,1,0:T(8,128)}, u32[]{:S(2)}, u32[]{:S(2)}) collective-permute-start(f32[4,256,512]{2,1,0:T(8,128)} %constant_dynamic-update-slice_fusion), channel_id=1, source_target_pairs={{1,4},{3,2},{5,8},{7,6},{9,12},{11,10},{13,0},{15,14},{17,20},{19,... | collective-permute-start | bytes 6291464 | tf_op jit(solution)/shard_map/ppermute | solution.py:95
  75.0 58.3 %collective-permute-start.9 = (f32[3,256,512]{2,1,0:T(8,128)}, f32[3,256,512]{2,1,0:T(8,128)}, u32[]{:S(2)}, u32[]{:S(2)}) collective-permute-start(f32[3,256,512]{2,1,0:T(8,128)} %slice_select_fusion), channel_id=1, source_target_pairs={{0,2},{1,3},{2,4},{3,5},{4,6},{5,7},{6,8},{7,9},{8,10},{9,11},{10,... | collective-permute-start | bytes 4718600 | tf_op jit(solution)/shard_map/ppermute | solution.py:95
  76.4 43.1 %slice-start = ((s8[8388608]{0:T(1024)(128)(4,1)}), s8[4194304]{0:T(1024)(128)(4,1)S(1)}, s32[]{:S(2)}) async-start(s8[8388608]{0:T(1024)(128)(4,1)} %bitcast.59), calls=%async_computation | async-start | bytes 8388608
  78.5 41.0 %slice-start.1 = ((s8[8388608]{0:T(1024)(128)(4,1)}), s8[4194304]{0:T(1024)(128)(4,1)S(1)}, s32[]{:S(2)}) async-start(s8[8388608]{0:T(1024)(128)(4,1)} %bitcast.59), calls=%async_computation.1 | async-start | bytes 8388608
  122.5 2.8 %collective-permute-start.7 = (f32[256,512]{1,0:T(8,128)}, f32[256,512]{1,0:T(8,128)S(1)}, u32[]{:S(2)}, u32[]{:S(2)}) collective-permute-start(f32[256,512]{1,0:T(8,128)} %fusion.12), channel_id=1, source_target_pairs={{0,16},{16,0},{1,17},{17,1},{2,18},{18,2},{3,19},{19,3},{4,20},{20... | collective-permute-start | bytes 1572872 | tf_op jit(solution)/shard_map/ppermute | solution.py:98
  122.5 2.8 %collective-permute-start.8 = (f32[256,512]{1,0:T(8,128)S(1)}, f32[256,512]{1,0:T(8,128)S(1)}, u32[]{:S(2)}, u32[]{:S(2)}) collective-permute-start(f32[256,512]{1,0:T(8,128)S(1)} %fusion.21), channel_id=1, source_target_pairs={{0,16},{16,0},{1,17},{17,1},{2,18},{18,2},{3,19},{19,3},{4,20},{20... | collective-permute-start | bytes 1572872 | tf_op jit(solution)/shard_map/ppermute | solution.py:98
  124.3 19.3 %collective-permute-start.10 = (f32[1,256,512]{2,1,0:T(8,128)}, f32[1,256,512]{2,1,0:T(8,128)S(1)}, u32[]{:S(2)}, u32[]{:S(2)}) collective-permute-start(f32[1,256,512]{2,1,0:T(8,128)} %slice_select_fusion.1), channel_id=1, source_target_pairs={{0,2},{1,3},{2,4},{3,5},{4,6},{5,7},{6,8},{7,9},{8,10},{9,11},{10,... | collective-permute-start | bytes 1572872 | tf_op jit(solution)/shard_map/ppermute | solution.py:95
